TPU v7x, 128 devices: a whole 4x4x4 slice. The times are simulated.
128 devices in a mesh: inline: 16 (over x, z), xline: 8 (over y, core).
Axes of the slice: x: 4, y: 4, z: 4, core: 2. Of those that a mesh axis runs over, the one named last changes fastest.
Arguments:
- traces: bfloat16 [32768, 2048], P(('inline', 'xline')), may hold values from -6 to 6
- trace_dest: int32 [32768, 1], P(('inline', 'xline')), may hold values from 0 to 127; in each aligned block of 256 rows (0 to 255, 256 to 511, ...) at most 4 rows name the same one
- trace_bin: int32 [32768], P(('inline', 'xline')), may hold values from 0 to 3
- trace_class: int32 [32768], P(('inline', 'xline')), may hold values from 0 to 7
- band_weights: bfloat16 [8, 16, 2, 128, 128], replicated, may hold values from -0.375 to 0.375
- conv_first: bfloat16 [32, 8, 3, 3, 3], replicated, may hold values from -0.4375 to 0.4375
- conv_second: bfloat16 [32, 32, 3, 3, 3], replicated, may hold values from -0.21875 to 0.21875
Outputs:
- regular: bfloat16 [32, 32, 16, 2048], P(None, 'inline', 'xline')
Inputs may be any that keep to these rules, and one draw needn't show every extreme that they name: `trace_dest`: among the 256 traces of one device no tile is named more than 4 times, a bound that some block reaches.
All inputs are finite; a program needn't handle non-finite values.
Results may differ from a plain program's by a relative error of at most 0.0065.
Values may be sent and summed in bfloat16 or wider, within the bound.
No kernel may reach another device: no remote copies, remote signals or barrier semaphores. Data moves between devices by JAX's collectives and lax.ppermute only.
A program may use at most 256 MiB of HBM per device.

v0:
```python
import jax
import jax.numpy as jnp
from jax import lax
from jax.sharding import PartitionSpec as P

CLASSES = 8
BI = 2
BX = 2


def padded_2(block, sides, width):
    for axis, dim in sides:
        count = lax.axis_size(axis)
        forward = [(i, i + 1) for i in range(count - 1)]
        backward = [(target, source) for source, target in forward]
        low = lax.ppermute(
            lax.slice_in_dim(block, block.shape[dim] - width, None, axis=dim), axis, forward
        )
        high = lax.ppermute(lax.slice_in_dim(block, 0, width, axis=dim), axis, backward)
        block = jnp.concatenate([low, block, high], axis=dim)
    return block


def convolve(padded, kernel):
    inner_i = padded.shape[1] - 2
    inner_x = padded.shape[2] - 2
    samples = padded.shape[3]
    timed = jnp.pad(padded, ((0, 0), (0, 0), (0, 0), (1, 1)))
    total = jnp.zeros((kernel.shape[0], inner_i, inner_x, samples), jnp.float32)
    for first in range(3):
        for second in range(3):
            for third in range(3):
                window = timed[
                    :, first : first + inner_i, second : second + inner_x, third : third + samples
                ]
                total = total + jnp.einsum(
                    "oc,cijs->oijs",
                    kernel[:, :, first, second, third],
                    window,
                    preferred_element_type=jnp.float32,
                )
    return total


def per_device(traces, trace_dest, trace_bin, trace_class, band_weights, conv_first, conv_second):
    inline_size = lax.axis_size("inline")
    xline_size = lax.axis_size("xline")
    devices_all = inline_size * xline_size
    trace_total, samples = traces.shape
    capacity = max(2, 2 * trace_total // devices_all)
    band_width = band_weights.shape[-1]
    target = trace_dest[:, 0]
    order = jnp.arange(trace_total, dtype=jnp.int32)
    earlier = (target[:, None] == target[None, :]) & (order[None, :] < order[:, None])
    slot_index = jnp.sum(earlier.astype(jnp.int32), axis=1)
    position = target * capacity + slot_index
    tile_bins = BI * BX
    bin_code = trace_class * tile_bins + trace_bin
    outgoing = jnp.zeros((devices_all * capacity, samples), jnp.bfloat16).at[position].set(traces)
    out_codes = jnp.full((devices_all * capacity,), -1, jnp.int32).at[position].set(bin_code)
    arrived, arrived_codes = (
        lax.all_to_all(
            outgoing.reshape(devices_all, capacity, samples),
            ("inline", "xline"),
            split_axis=0,
            concat_axis=0,
            tiled=True,
        ),
        lax.all_to_all(
            out_codes.reshape(devices_all, capacity),
            ("inline", "xline"),
            split_axis=0,
            concat_axis=0,
            tiled=True,
        ),
    )
    arrived = arrived.reshape(devices_all * capacity, samples)
    arrived_codes = arrived_codes.reshape(devices_all * capacity)
    cells = jnp.arange(CLASSES * tile_bins, dtype=jnp.int32)
    selector = (cells[:, None] == arrived_codes[None, :]).astype(jnp.bfloat16)
    stacked = jnp.dot(selector, arrived, preferred_element_type=jnp.float32)
    fold_count = jnp.sum(selector.astype(jnp.float32), axis=1)
    averaged = (stacked / jnp.maximum(fold_count, 1.0)[:, None]).astype(jnp.bfloat16)
    blocks = averaged.reshape(CLASSES, tile_bins, samples // band_width, band_width)
    following = jnp.concatenate([blocks[:, :, 1:], jnp.zeros_like(blocks[:, :, :1])], axis=2)
    shifted = jnp.einsum(
        "cbkt,cktu->cbku", blocks, band_weights[:, :, 0], preferred_element_type=jnp.float32
    )
    shifted = shifted + jnp.einsum(
        "cbkt,cktu->cbku", following, band_weights[:, :, 1], preferred_element_type=jnp.float32
    )
    volume = shifted.astype(jnp.bfloat16).reshape(CLASSES, BI, BX, samples)
    padded = padded_2(volume, (("inline", 1), ("xline", 2)), 1)
    hidden = jax.nn.gelu(convolve(padded, conv_first)).astype(jnp.bfloat16)
    hidden_padded = padded_2(hidden, (("inline", 1), ("xline", 2)), 1)
    return convolve(hidden_padded, conv_second).astype(jnp.bfloat16)


def solution(mesh):
    return jax.shard_map(
        per_device,
        mesh=mesh,
        in_specs=(
            P(("inline", "xline"), None),
            P(("inline", "xline"), None),
            P(("inline", "xline")),
            P(("inline", "xline")),
            P(),
            P(),
            P(),
        ),
        out_specs=P(None, "inline", "xline", None),
        check_vma=False,
    )
```

profile of v0, /device:TPU:3, one launch (start us, length us, event | category | flops | bytes accessed | tf_op | source)
XLA Modules:
  0.0 139.4 jit_solution(15244979938267228307)
XLA Ops:
  0.0 0.9 convert_reduce_fusion
  1.6 0.7 multiply_add_fusion
  2.3 1.4 scatter_custom_fusion
  3.7 0.7 all_to_all.9
  4.5 10.8 %all-to-all-start = ((s32[128,1,4]{2,1,0:T(1,128)}), s32[128,1,4]{2,1,0:T(1,128)S(1)}, u32[]{:S(2)}, u32[]{:S(2)}) async-start(s32[128,1,4]{2,1,0:T(1,128)} %bitcast.3), calls=%async_computation | async-start | bytes 131072 | tf_op jit(solution)/shard_map/all_to_all | solution.py:69
  15.3 3.5 %scatter_custom_fusion.1 = bf16[512,2048]{1,0:T(8,128)(2,1)S(1)} fusion(s32[256]{0:T(256)S(1)} %bitcast.506, bf16[256,2048]{1,0:T(8,128)(2,1)} %param.7, bf16[]{:T(256)} %constant.2.clone.1), kind=kCustom, calls=%fused_computation.114 | custom fusion | bytes 2097664 | tf_op jit(solution)/shard_map/scatter | solution.py:59
  18.8 2.2 %reshape.23 = bf16[128,4,2048]{2,1,0:T(4,128)(2,1)} reshape(bf16[512,2048]{1,0:T(8,128)(2,1)S(1)} %scatter_custom_fusion.1) | data formatting | bytes 4194304 | tf_op jit(solution)/shard_map/reshape | solution.py:63
  21.1 2.6 %all-to-all-done = s32[128,1,4]{2,1,0:T(1,128)S(1)} async-done(((s32[128,1,4]{2,1,0:T(1,128)}), s32[128,1,4]{2,1,0:T(1,128)S(1)}, u32[]{:S(2)}, u32[]{:S(2)}) %all-to-all-start) | async-done | bytes 2080 | tf_op jit(solution)/shard_map/all_to_all | solution.py:69
  23.6 7.2 %all-to-all-start.1 = ((bf16[128,4,2048]{2,1,0:T(4,128)(2,1)}), bf16[128,4,2048]{2,1,0:T(4,128)(2,1)S(1)}, u32[]{:S(2)}, u32[]{:S(2)}) async-start(bf16[128,4,2048]{2,1,0:T(4,128)(2,1)} %reshape.23), calls=%async_computation.1 | async-start | bytes 4194304 | tf_op jit(solution)/shard_map/all_to_all | solution.py:62
  31.3 0.8 reduce.3
  32.4 27.7 %all-to-all-done.1 = bf16[128,4,2048]{2,1,0:T(4,128)(2,1)S(1)} async-done(((bf16[128,4,2048]{2,1,0:T(4,128)(2,1)}), bf16[128,4,2048]{2,1,0:T(4,128)(2,1)S(1)}, u32[]{:S(2)}, u32[]{:S(2)}) %all-to-all-start.1) | async-done | bytes 2097184 | tf_op jit(solution)/shard_map/all_to_all | solution.py:62
  60.1 2.1 %reshape.24 = bf16[512,2048]{1,0:T(8,128)(2,1)} reshape(bf16[128,4,2048]{2,1,0:T(4,128)(2,1)S(1)} %all-to-all-done.1) | data formatting | bytes 4194304 | tf_op jit(solution)/shard_map/reshape | solution.py:77
  62.1 2.0 %fusion.57 = bf16[4,8,16,128]{3,1,2,0:T(8,128)(2,1)S(1)} fusion(bf16[512,2048]{1,0:T(8,128)(2,1)} %reshape.24, f32[32]{0:T(128)S(1)} %broadcast_maximum_fusion, s32[512]{0:T(512)S(1)} %eq.35), kind=kOutput, calls=%fused_computation.103 | convolution fusion | flops 67256320 | bytes 2230400 | tf_op jit(solution)/shard_map/dot_general | solution.py:81
  64.3 3.4 %fusion.1 = f32[8,16,4,128]{3,2,1,0:T(4,128)S(1)} fusion(bf16[8,16,2,128,128]{4,3,2,1,0:T(8,128)(2,1)} %param.11, bf16[8,4,16,128]{3,1,2,0:T(4,128)(2,1)S(1)} %copy.28), kind=kOutput, calls=%fused_computation.5 | convolution fusion | flops 15728640 | bytes 4579328 | tf_op jit(solution)/shard_map/cbkt,cktu->cbku/dot_general | solution.py:89
  67.7 3.4 %fusion.54 = bf16[8,4,16,128]{3,1,2,0:T(4,128)(2,1)S(1)} fusion(f32[8,16,4,128]{3,2,1,0:T(4,128)S(1)} %fusion.1, bf16[8,16,2,128,128]{4,3,2,1,0:T(8,128)(2,1)} %param.11, bf16[8,4,16,128]{3,2,1,0:T(8,128)(2,1)S(1)} %bitcast.502), kind=kOutput, calls=%fused_computation.102 | convolution fusion | flops 16908288 | bytes 4718592 | tf_op jit(solution)/shard_map/cbkt,cktu->cbku/dot_general | solution.py:86
  71.2 2.5 %collective-permute-start = (bf16[8,1,2,2048]{3,0,2,1:T(8,128)(2,1)S(1)}, bf16[8,1,2,2048]{3,0,2,1:T(8,128)(2,1)S(1)}, u32[]{:S(2)}, u32[]{:S(2)}) collective-permute-start(bf16[8,1,2,2048]{3,0,2,1:T(8,128)(2,1)S(1)} %get-tuple-element.14), channel_id=1, source_target_pairs={{0,8},{8,16},{16,24},{24,32},{32,40},{40,48},{48,56},{56,64},{64,7... | collective-permute-start | bytes 196616 | tf_op jit(solution)/shard_map/ppermute | solution.py:16
  73.7 4.9 %collective-permute-start.1 = (bf16[8,1,2,2048]{3,0,2,1:T(8,128)(2,1)S(1)}, bf16[8,1,2,2048]{3,0,2,1:T(8,128)(2,1)S(1)}, u32[]{:S(2)}, u32[]{:S(2)}) collective-permute-start(bf16[8,1,2,2048]{3,0,2,1:T(8,128)(2,1)S(1)} %get-tuple-element.13), channel_id=1, source_target_pairs={{8,0},{16,8},{24,16},{32,24},{40,32},{48,40},{56,48},{64,56},{72,6... | collective-permute-start | bytes 196616 | tf_op jit(solution)/shard_map/ppermute | solution.py:19
  78.7 1.3 collective-permute-done.1
  79.9 3.3 %collective-permute-start.2 = (bf16[8,4,1,2048]{3,0,2,1:T(8,128)(2,1)S(1)}, bf16[8,4,1,2048]{3,0,2,1:T(8,128)(2,1)S(1)}, u32[]{:S(2)}, u32[]{:S(2)}) collective-permute-start(bf16[8,4,1,2048]{3,0,2,1:T(8,128)(2,1)S(1)} %get-tuple-element.11), channel_id=1, source_target_pairs={{0,1},{1,2},{2,3},{3,4},{4,5},{5,6},{6,7},{8,9},{9,10},{10,11},{11... | collective-permute-start | bytes 393224 | tf_op jit(solution)/shard_map/ppermute | solution.py:16
  83.2 2.4 %collective-permute-start.3 = (bf16[8,4,1,2048]{3,0,2,1:T(8,128)(2,1)S(1)}, bf16[8,4,1,2048]{3,0,2,1:T(8,128)(2,1)S(1)}, u32[]{:S(2)}, u32[]{:S(2)}) collective-permute-start(bf16[8,4,1,2048]{3,0,2,1:T(8,128)(2,1)S(1)} %get-tuple-element.12), channel_id=1, source_target_pairs={{1,0},{2,1},{3,2},{4,3},{5,4},{6,5},{7,6},{9,8},{10,9},{11,10},{12... | collective-permute-start | bytes 393224 | tf_op jit(solution)/shard_map/ppermute | solution.py:19
  86.0 3.5 %collective-permute-done.3 = bf16[8,4,1,2048]{3,0,2,1:T(8,128)(2,1)S(1)} collective-permute-done((bf16[8,4,1,2048]{3,0,2,1:T(8,128)(2,1)S(1)}, bf16[8,4,1,2048]{3,0,2,1:T(8,128)(2,1)S(1)}, u32[]{:S(2)}, u32[]{:S(2)}) %collective-permute-start.3) | collective-permute-done | bytes 131104 | tf_op jit(solution)/shard_map/ppermute | solution.py:19
  97.3 0.9 fusion.22
  100.1 1.9 %collective-permute-start.4 = (bf16[32,1,2,2048]{3,0,2,1:T(8,128)(2,1)S(1)}, bf16[32,1,2,2048]{3,0,2,1:T(8,128)(2,1)S(1)}, u32[]{:S(2)}, u32[]{:S(2)}) collective-permute-start(bf16[32,1,2,2048]{3,0,2,1:T(8,128)(2,1)S(1)} %get-tuple-element.9), channel_id=1, source_target_pairs={{0,8},{8,16},{16,24},{24,32},{32,40},{40,48},{48,56},{56,64},{64,7... | collective-permute-start | bytes 786440 | tf_op jit(solution)/shard_map/ppermute | solution.py:16
  102.1 6.1 %collective-permute-start.5 = (bf16[32,1,2,2048]{3,0,2,1:T(8,128)(2,1)S(1)}, bf16[32,1,2,2048]{3,0,2,1:T(8,128)(2,1)S(1)}, u32[]{:S(2)}, u32[]{:S(2)}) collective-permute-start(bf16[32,1,2,2048]{3,0,2,1:T(8,128)(2,1)S(1)} %get-tuple-element.10), channel_id=1, source_target_pairs={{8,0},{16,8},{24,16},{32,24},{40,32},{48,40},{56,48},{64,56},{72,6... | collective-permute-start | bytes 786440 | tf_op jit(solution)/shard_map/ppermute | solution.py:19
  108.2 2.1 %collective-permute-done.4 = bf16[32,1,2,2048]{3,0,2,1:T(8,128)(2,1)S(1)} collective-permute-done((bf16[32,1,2,2048]{3,0,2,1:T(8,128)(2,1)S(1)}, bf16[32,1,2,2048]{3,0,2,1:T(8,128)(2,1)S(1)}, u32[]{:S(2)}, u32[]{:S(2)}) %collective-permute-start.4) | collective-permute-done | bytes 262176 | tf_op jit(solution)/shard_map/ppermute | solution.py:16
  110.2 1.8 %collective-permute-done.5 = bf16[32,1,2,2048]{3,0,2,1:T(8,128)(2,1)S(1)} collective-permute-done((bf16[32,1,2,2048]{3,0,2,1:T(8,128)(2,1)S(1)}, bf16[32,1,2,2048]{3,0,2,1:T(8,128)(2,1)S(1)}, u32[]{:S(2)}, u32[]{:S(2)}) %collective-permute-start.5) | collective-permute-done | bytes 262176 | tf_op jit(solution)/shard_map/ppermute | solution.py:19
  112.2 4.6 %collective-permute-start.6 = (bf16[32,4,1,2048]{3,0,2,1:T(8,128)(2,1)S(1)}, bf16[32,4,1,2048]{3,0,2,1:T(8,128)(2,1)S(1)}, u32[]{:S(2)}, u32[]{:S(2)}) collective-permute-start(bf16[32,4,1,2048]{3,0,2,1:T(8,128)(2,1)S(1)} %get-tuple-element.7), channel_id=1, source_target_pairs={{0,1},{1,2},{2,3},{3,4},{4,5},{5,6},{6,7},{8,9},{9,10},{10,11},{11... | collective-permute-start | bytes 1572872 | tf_op jit(solution)/shard_map/ppermute | solution.py:16
  116.9 2.1 %collective-permute-start.7 = (bf16[32,4,1,2048]{3,0,2,1:T(8,128)(2,1)S(1)}, bf16[32,4,1,2048]{3,0,2,1:T(8,128)(2,1)S(1)}, u32[]{:S(2)}, u32[]{:S(2)}) collective-permute-start(bf16[32,4,1,2048]{3,0,2,1:T(8,128)(2,1)S(1)} %get-tuple-element.8), channel_id=1, source_target_pairs={{1,0},{2,1},{3,2},{4,3},{5,4},{6,5},{7,6},{9,8},{10,9},{11,10},{12... | collective-permute-start | bytes 1572872 | tf_op jit(solution)/shard_map/ppermute | solution.py:19
  119.0 4.0 %collective-permute-done.6 = bf16[32,4,1,2048]{3,0,2,1:T(8,128)(2,1)S(1)} collective-permute-done((bf16[32,4,1,2048]{3,0,2,1:T(8,128)(2,1)S(1)}, bf16[32,4,1,2048]{3,0,2,1:T(8,128)(2,1)S(1)}, u32[]{:S(2)}, u32[]{:S(2)}) %collective-permute-start.6) | collective-permute-done | bytes 524320 | tf_op jit(solution)/shard_map/ppermute | solution.py:16
  123.0 4.4 %collective-permute-done.7 = bf16[32,4,1,2048]{3,0,2,1:T(8,128)(2,1)S(1)} collective-permute-done((bf16[32,4,1,2048]{3,0,2,1:T(8,128)(2,1)S(1)}, bf16[32,4,1,2048]{3,0,2,1:T(8,128)(2,1)S(1)}, u32[]{:S(2)}, u32[]{:S(2)}) %collective-permute-start.7) | collective-permute-done | bytes 524320 | tf_op jit(solution)/shard_map/ppermute | solution.py:19
  127.4 1.8 %select_maximum_fusion = bf16[32,4,4,2050]{3,0,2,1:T(8,128)(2,1)S(1)} fusion(bf16[32,4,1,2048]{3,0,2,1:T(8,128)(2,1)S(1)} %collective-permute-done.7, bf16[32,4,1,2048]{3,0,2,1:T(8,128)(2,1)S(1)} %collective-permute-done.6, bf16[32,1,2,2048]{3,0,2,1:T(8,128)(2,1)S(1)} %collective-permute-done.5, bf16[32,2,2,2048]{3,0,2,1:T(8,128)(2,1)S(1)} %fusion.66, ...), kind=kLoop, calls=%fused_computation.88 | loop fusion | flops 18892800 | bytes 4196352 | tf_op jit(solution)/shard_map/concatenate | solution.py:20
  138.1 1.3 copy.32
  (78 shorter events, 20.4 us)
Async XLA Ops:
  4.5 19.2 %all-to-all-start = ((s32[128,1,4]{2,1,0:T(1,128)}), s32[128,1,4]{2,1,0:T(1,128)S(1)}, u32[]{:S(2)}, u32[]{:S(2)}) async-start(s32[128,1,4]{2,1,0:T(1,128)} %bitcast.3), calls=%async_computation | async-start | bytes 131072 | tf_op jit(solution)/shard_map/all_to_all | solution.py:69
  23.6 36.4 %all-to-all-start.1 = ((bf16[128,4,2048]{2,1,0:T(4,128)(2,1)}), bf16[128,4,2048]{2,1,0:T(4,128)(2,1)S(1)}, u32[]{:S(2)}, u32[]{:S(2)}) async-start(bf16[128,4,2048]{2,1,0:T(4,128)(2,1)} %reshape.23), calls=%async_computation.1 | async-start | bytes 4194304 | tf_op jit(solution)/shard_map/all_to_all | solution.py:62
  67.7 18.0 %copy-start.1 = (bf16[32,8,3,3,3]{0,1,4,3,2:T(8,128)(2,1)S(1)}, bf16[32,8,3,3,3]{0,1,4,3,2:T(8,128)(2,1)}, u32[]{:S(2)}) copy-start(bf16[32,8,3,3,3]{0,1,4,3,2:T(8,128)(2,1)} %param.12) | copy-start | bytes 41476
  71.2 7.4 %collective-permute-start = (bf16[8,1,2,2048]{3,0,2,1:T(8,128)(2,1)S(1)}, bf16[8,1,2,2048]{3,0,2,1:T(8,128)(2,1)S(1)}, u32[]{:S(2)}, u32[]{:S(2)}) collective-permute-start(bf16[8,1,2,2048]{3,0,2,1:T(8,128)(2,1)S(1)} %get-tuple-element.14), channel_id=1, source_target_pairs={{0,8},{8,16},{16,24},{24,32},{32,40},{40,48},{48,56},{56,64},{64,7... | collective-permute-start | bytes 196616 | tf_op jit(solution)/shard_map/ppermute | solution.py:16
  73.7 6.2 %collective-permute-start.1 = (bf16[8,1,2,2048]{3,0,2,1:T(8,128)(2,1)S(1)}, bf16[8,1,2,2048]{3,0,2,1:T(8,128)(2,1)S(1)}, u32[]{:S(2)}, u32[]{:S(2)}) collective-permute-start(bf16[8,1,2,2048]{3,0,2,1:T(8,128)(2,1)S(1)} %get-tuple-element.13), channel_id=1, source_target_pairs={{8,0},{16,8},{24,16},{32,24},{40,32},{48,40},{56,48},{64,56},{72,6... | collective-permute-start | bytes 196616 | tf_op jit(solution)/shard_map/ppermute | solution.py:19
  79.9 6.1 %collective-permute-start.2 = (bf16[8,4,1,2048]{3,0,2,1:T(8,128)(2,1)S(1)}, bf16[8,4,1,2048]{3,0,2,1:T(8,128)(2,1)S(1)}, u32[]{:S(2)}, u32[]{:S(2)}) collective-permute-start(bf16[8,4,1,2048]{3,0,2,1:T(8,128)(2,1)S(1)} %get-tuple-element.11), channel_id=1, source_target_pairs={{0,1},{1,2},{2,3},{3,4},{4,5},{5,6},{6,7},{8,9},{9,10},{10,11},{11... | collective-permute-start | bytes 393224 | tf_op jit(solution)/shard_map/ppermute | solution.py:16
  83.2 6.3 %collective-permute-start.3 = (bf16[8,4,1,2048]{3,0,2,1:T(8,128)(2,1)S(1)}, bf16[8,4,1,2048]{3,0,2,1:T(8,128)(2,1)S(1)}, u32[]{:S(2)}, u32[]{:S(2)}) collective-permute-start(bf16[8,4,1,2048]{3,0,2,1:T(8,128)(2,1)S(1)} %get-tuple-element.12), channel_id=1, source_target_pairs={{1,0},{2,1},{3,2},{4,3},{5,4},{6,5},{7,6},{9,8},{10,9},{11,10},{12... | collective-permute-start | bytes 393224 | tf_op jit(solution)/shard_map/ppermute | solution.py:19
  100.1 10.1 %collective-permute-start.4 = (bf16[32,1,2,2048]{3,0,2,1:T(8,128)(2,1)S(1)}, bf16[32,1,2,2048]{3,0,2,1:T(8,128)(2,1)S(1)}, u32[]{:S(2)}, u32[]{:S(2)}) collective-permute-start(bf16[32,1,2,2048]{3,0,2,1:T(8,128)(2,1)S(1)} %get-tuple-element.9), channel_id=1, source_target_pairs={{0,8},{8,16},{16,24},{24,32},{32,40},{40,48},{48,56},{56,64},{64,7... | collective-permute-start | bytes 786440 | tf_op jit(solution)/shard_map/ppermute | solution.py:16
  102.1 9.9 %collective-permute-start.5 = (bf16[32,1,2,2048]{3,0,2,1:T(8,128)(2,1)S(1)}, bf16[32,1,2,2048]{3,0,2,1:T(8,128)(2,1)S(1)}, u32[]{:S(2)}, u32[]{:S(2)}) collective-permute-start(bf16[32,1,2,2048]{3,0,2,1:T(8,128)(2,1)S(1)} %get-tuple-element.10), channel_id=1, source_target_pairs={{8,0},{16,8},{24,16},{32,24},{40,32},{48,40},{56,48},{64,56},{72,6... | collective-permute-start | bytes 786440 | tf_op jit(solution)/shard_map/ppermute | solution.py:19
  112.2 16.9 %copy-start = (bf16[32,32,3,3,3]{1,0,4,3,2:T(8,128)(2,1)S(1)}, bf16[32,32,3,3,3]{1,0,4,3,2:T(8,128)(2,1)}, u32[]{:S(2)}) copy-start(bf16[32,32,3,3,3]{1,0,4,3,2:T(8,128)(2,1)} %param.13) | copy-start | bytes 165892
  112.2 10.8 %collective-permute-start.6 = (bf16[32,4,1,2048]{3,0,2,1:T(8,128)(2,1)S(1)}, bf16[32,4,1,2048]{3,0,2,1:T(8,128)(2,1)S(1)}, u32[]{:S(2)}, u32[]{:S(2)}) collective-permute-start(bf16[32,4,1,2048]{3,0,2,1:T(8,128)(2,1)S(1)} %get-tuple-element.7), channel_id=1, source_target_pairs={{0,1},{1,2},{2,3},{3,4},{4,5},{5,6},{6,7},{8,9},{9,10},{10,11},{11... | collective-permute-start | bytes 1572872 | tf_op jit(solution)/shard_map/ppermute | solution.py:16
  116.9 10.5 %collective-permute-start.7 = (bf16[32,4,1,2048]{3,0,2,1:T(8,128)(2,1)S(1)}, bf16[32,4,1,2048]{3,0,2,1:T(8,128)(2,1)S(1)}, u32[]{:S(2)}, u32[]{:S(2)}) collective-permute-start(bf16[32,4,1,2048]{3,0,2,1:T(8,128)(2,1)S(1)} %get-tuple-element.8), channel_id=1, source_target_pairs={{1,0},{2,1},{3,2},{4,3},{5,4},{6,5},{7,6},{9,8},{10,9},{11,10},{12... | collective-permute-start | bytes 1572872 | tf_op jit(solution)/shard_map/ppermute | solution.py:19
where the time goes:
time: 141 us; the launch traced here: 139 us
  waiting for transfers between devices  47.2 us (33%)
  starting transfers between devices  45.9 us (33%)
  matrix products  27.6 us (20%)
  local copies, waits for them, and re-layouts  12.2 us (9%)
  other arithmetic  5.77 us (4%)
    all_to_all x1, waiting for transfers between devices, per_device(): lax.all_to_all(outgoing.reshape(devices_all, capacity, samples), ('inline...  27.7 us
    dot_general x54, matrix products, convolve(): jnp.einsum('oc,cijs->oijs', kernel[:, :, first, second, third], window, p...  18.8 us
    ppermute x4, starting transfers between devices, padded_2(): lax.ppermute(lax.slice_in_dim(block, 0, width, axis=dim), axis, backward)  15.6 us
    ppermute x4, starting transfers between devices, padded_2(): lax.ppermute(lax.slice_in_dim(block, block.shape[dim] - width, None, axis...  12.3 us
    ppermute x4, waiting for transfers between devices, padded_2(): lax.ppermute(lax.slice_in_dim(block, 0, width, axis=dim), axis, backward)  10.9 us
    all_to_all x1, starting transfers between devices, per_device(): lax.all_to_all(out_codes.reshape(devices_all, capacity), ('inline', 'xlin...  10.8 us
    all_to_all x1, starting transfers between devices, per_device(): lax.all_to_all(outgoing.reshape(devices_all, capacity, samples), ('inline...  7.18 us
    ppermute x4, waiting for transfers between devices, padded_2(): lax.ppermute(lax.slice_in_dim(block, block.shape[dim] - width, None, axis...  6.05 us
  transfers between devices with their start and end apart: 10, of which 8 were waited for; matrix products, arithmetic and copies ran while one was open for 5% of the time, Pallas kernels for 0%

commit v1 on v0

v1 whole, which is shorter than its diff:
```python
import jax
import jax.numpy as jnp
import numpy as np
from jax import lax
from jax.experimental import pallas as pl
from jax.experimental.pallas import tpu as pltpu
from jax.sharding import PartitionSpec as P

CLASSES = 8
BI = 2
BX = 2
CH = 32
CAP = 4
ALL = ("inline", "xline")
BF = jnp.bfloat16
F32 = jnp.float32
CELLS = CLASSES * BI * BX


def iota(shape, dim):
    return lax.broadcasted_iota(jnp.int32, shape, dim)


def nt(a, b):
    return lax.dot_general(a, b, (((1,), (1,)), ((), ())), preferred_element_type=F32)


def tn(a, b):
    return lax.dot_general(a, b, (((0,), (0,)), ((), ())), preferred_element_type=F32)


def nn(a, b):
    return jnp.dot(a, b, preferred_element_type=F32)


def before(count):
    return (iota((count, count), 0) < iota((count, count), 1)).astype(BF)


def pack_kernel(dest_ref, bin_ref, class_ref, traces_ref, out_ref, tags, loaded, packed, tag_sem, load_sem, store_sem):
    rows, width = packed.shape
    count, half = loaded.shape[0] // 2, loaded.shape[1]
    devices = rows // (2 * CAP)
    strips = load_sem.shape[0]
    tile = half // strips
    small = []
    for number, ref in enumerate((dest_ref, bin_ref, class_ref)):
        small.append(pltpu.make_async_copy(ref, tags.at[number], tag_sem.at[number]))
        small[-1].start()
    loads = []
    for strip in range(strips):
        for side in range(2):
            loads.append(
                pltpu.make_async_copy(
                    traces_ref.at[:, pl.ds(side * half + strip * tile, tile)],
                    loaded.at[pl.ds(side * count, count), pl.ds(strip * tile, tile)],
                    load_sem.at[strip, side],
                )
            )
            loads[-1].start()
    for copy in small:
        copy.wait()
    dest = tags[0]
    named = iota((devices, count), 0) == dest
    rank = nn(named.astype(BF), before(count))
    slot = jnp.sum(jnp.where(named, rank, 0.0), axis=0, keepdims=True)
    position = dest * (2 * CAP) + slot.astype(jnp.int32)
    row = iota((rows, count), 0)
    place = jnp.concatenate(
        [(row == position).astype(BF), (row == position + CAP).astype(BF)], axis=1
    )
    cell = tags[1] * CLASSES + tags[2]
    lane = iota((128, count), 0)
    tagged = jnp.concatenate(
        [((lane == cell) | (lane == 127)).astype(BF), (lane == cell + CELLS).astype(BF)], axis=1
    )
    stores = []

    def store(at, size, number):
        copy = pltpu.make_async_copy(
            packed.at[:, pl.ds(at, size)], out_ref.at[:, pl.ds(at, size)], store_sem.at[number]
        )
        copy.start()
        stores.append(copy)

    packed[:, half:] = nt(place, tagged).astype(BF)
    store(half, 128, strips)
    for strip in range(strips):
        loads[2 * strip].wait()
        loads[2 * strip + 1].wait()
        at = strip * tile
        packed[:, at : at + tile] = nn(place, loaded[:, at : at + tile]).astype(BF)
        store(at, tile, strip)
    for copy in stores:
        copy.wait()


def pack(traces, dest, bins, classes, devices):
    count, samples = traces.shape
    rows, width = devices * 2 * CAP, samples // 2 + 128
    strips = 4
    kept = pl.BlockSpec(memory_space=pltpu.HBM)
    pin = lambda array: pltpu.with_memory_space_constraint(array, pltpu.HBM)
    return pl.pallas_call(
        pack_kernel,
        in_specs=[kept] * 4,
        out_specs=kept,
        out_shape=pltpu.HBM((rows, width), BF),
        scratch_shapes=[
            pltpu.VMEM((3, 1, count), jnp.int32),
            pltpu.VMEM((2 * count, samples // 2), BF),
            pltpu.VMEM((rows, width), BF),
            pltpu.SemaphoreType.DMA((3,)),
            pltpu.SemaphoreType.DMA((strips, 2)),
            pltpu.SemaphoreType.DMA((strips + 1,)),
        ],
        compiler_params=pltpu.CompilerParams(vmem_limit_bytes=40 << 20),
        name="pack",
    )(pin(dest), pin(bins), pin(classes), pin(traces))


def stack_kernel(arrived_ref, band_ref, out_ref, averaged, weights, sem):
    width = arrived_ref.shape[1]
    half = width - 128
    parts, _, each, _, band = weights.shape
    loads = []
    for part in range(parts):
        loads.append(
            pltpu.make_async_copy(
                band_ref.at[:, pl.ds(part * each, each)], weights.at[part], sem.at[part]
            )
        )
        loads[-1].start()
    stacked = tn(arrived_ref[:, half:], arrived_ref[...])
    fold = jnp.maximum(stacked[:CELLS, width - 1 : width], 1.0)
    averaged[:, :half] = (stacked[:CELLS, :half] / fold).astype(BF)
    averaged[:, half : 2 * half] = (stacked[CELLS : 2 * CELLS, :half] / fold).astype(BF)
    averaged[:, 2 * half :] = jnp.zeros((CELLS, band), BF)
    kind = iota((CELLS, band), 0) % CLASSES
    for block in range(parts * each):
        if block % each == 0:
            loads[block // each].wait()
        start = block * band
        pair = averaged[:, start : start + 2 * band]
        wide = jnp.concatenate(
            [weights[block // each, number, block % each] for number in range(CLASSES)], axis=1
        )
        moved = nn(pair, wide)
        total = moved[:, :band]
        for number in range(1, CLASSES):
            total = jnp.where(kind == number, moved[:, number * band : (number + 1) * band], total)
        out_ref[:, start : start + band] = total.astype(BF)


def stack(arrived, band_weights):
    rows, width = arrived.shape
    samples = 2 * (width - 128)
    classes, blocks, steps, band, _ = band_weights.shape
    weights = band_weights.reshape(classes, blocks, steps * band, band)
    parts = 8
    whole = pl.BlockSpec(memory_space=pltpu.VMEM)
    return pl.pallas_call(
        stack_kernel,
        in_specs=[whole, pl.BlockSpec(memory_space=pltpu.HBM)],
        out_specs=whole,
        out_shape=jax.ShapeDtypeStruct((CELLS, samples), BF),
        scratch_shapes=[
            pltpu.VMEM((CELLS, samples + band), BF),
            pltpu.VMEM((parts, classes, blocks // parts, steps * band, band), BF),
            pltpu.SemaphoreType.DMA((parts,)),
        ],
        compiler_params=pltpu.CompilerParams(vmem_limit_bytes=24 << 20),
        name="stack",
    )(arrived, pltpu.with_memory_space_constraint(weights, pltpu.HBM))


def later(value):
    rolled = pltpu.roll(value, 1, 1)
    return jnp.where(iota(value.shape, 1) == 0, 0.0, rolled)


def sooner(value):
    samples = value.shape[1]
    rolled = pltpu.roll(value, samples - 1, 1)
    return jnp.where(iota(value.shape, 1) == samples - 1, 0.0, rolled)


def conv_kernel(place_ref, mid_ref, low_ref, high_ref, first_ref, second_ref, out_ref, taps, hidden):
    samples = mid_ref.shape[1]
    tall = BX * CLASSES
    group = 9 * tall
    for which, ref in enumerate((low_ref, mid_ref, high_ref)):
        value = ref[...].astype(F32)
        for tap, shifted in enumerate((later(value), value, sooner(value))):
            shifted = shifted.astype(BF)
            for line in range(BI + 4):
                at = line * group + (tap * 3 + which) * tall
                taps[at : at + tall, :] = shifted[line * tall : (line + 1) * tall]
    wide = (BX + 2) * CH
    bin_x = iota((wide, 1), 0) // CH + place_ref[1] * BX - 1
    inside_x = (bin_x >= 0) & (bin_x < place_ref[3])
    first = first_ref[...]
    tile = 512
    for line in range(BI + 2):
        bin_i = line + place_ref[0] * BI - 1
        inside = inside_x & (bin_i >= 0) & (bin_i < place_ref[2])
        for start in range(0, samples, tile):
            window = taps[line * group : (line + 3) * group, start : start + tile]
            value = jax.nn.gelu(nn(first, window))
            value = jnp.where(inside, value, 0.0)
            hidden[line * wide : (line + 1) * wide, start : start + tile] = value.astype(BF)
    second = second_ref[...]
    value = nn(second, hidden[...])
    rows = CH * BI * BX
    total = value[rows : 2 * rows] + later(value[:rows]) + sooner(value[2 * rows :])
    out_ref[...] = total.astype(BF).reshape(out_ref.shape)


def convolutions(place, mid, low, high, first, second):
    samples = mid.shape[1]
    whole = pl.BlockSpec(memory_space=pltpu.VMEM)
    return pl.pallas_call(
        conv_kernel,
        in_specs=[pl.BlockSpec(memory_space=pltpu.SMEM)] + [whole] * 5,
        out_specs=whole,
        out_shape=jax.ShapeDtypeStruct((CH, BI, BX, samples), BF),
        scratch_shapes=[
            pltpu.VMEM(((BI + 4) * 9 * BX * CLASSES, samples), BF),
            pltpu.VMEM(((BI + 2) * (BX + 2) * CH, samples), BF),
        ],
        compiler_params=pltpu.CompilerParams(vmem_limit_bytes=48 << 20),
        name="convolutions",
    )(place, mid, low, high, first, second)


def first_matrix(kernel):
    spatial = kernel.transpose(2, 3, 4, 1, 0)
    placed = [
        jnp.pad(spatial, ((0, 0), (at, BX + 1 - at), (0, 0), (0, 0), (0, 0))) for at in range(BX + 2)
    ]
    matrix = jnp.stack(placed, axis=0)
    matrix = matrix.transpose(0, 5, 1, 3, 2, 4)
    return matrix.reshape((BX + 2) * CH, 9 * (BX + 4) * CLASSES)


def second_matrix(kernel):
    spatial = kernel.transpose(2, 3, 4, 0, 1)
    placed = [
        [
            jnp.pad(spatial, ((i, BI - 1 - i), (x, BX - 1 - x), (0, 0), (0, 0), (0, 0)))
            for x in range(BX)
        ]
        for i in range(BI)
    ]
    matrix = jnp.stack([jnp.stack(line, axis=0) for line in placed], axis=0)
    matrix = matrix.transpose(4, 5, 0, 1, 2, 3, 6)
    return matrix.reshape(3 * CH * BI * BX, (BI + 2) * (BX + 2) * CH)


def neighbours(block, axis):
    count = lax.axis_size(axis)
    forward = [(i, i + 1) for i in range(count - 1)]
    backward = [(target, source) for source, target in forward]
    return lax.ppermute(block, axis, forward), lax.ppermute(block, axis, backward)


def per_device(traces, trace_dest, trace_bin, trace_class, band_weights, conv_first, conv_second):
    inline_size = lax.axis_size("inline")
    xline_size = lax.axis_size("xline")
    devices = inline_size * xline_size
    at_i, at_x = lax.axis_index("inline"), lax.axis_index("xline")
    count, samples = traces.shape
    width = samples // 2 + 128
    outgoing = pack(
        traces,
        trace_dest.reshape(1, count),
        trace_bin.reshape(1, count),
        trace_class.reshape(1, count),
        devices,
    )
    arrived = lax.all_to_all(
        outgoing.reshape(devices, 2 * CAP, width), ALL, split_axis=0, concat_axis=0, tiled=True
    ).reshape(devices * 2 * CAP, width)
    first, second = first_matrix(conv_first), second_matrix(conv_second)
    arrived, first, second = lax.optimization_barrier((arrived, first, second))
    volume = stack(arrived, band_weights)
    before_i, after_i = neighbours(volume, "inline")
    column = jnp.concatenate([before_i, volume, after_i], axis=0)
    before_x, after_x = neighbours(column, "xline")
    place = jnp.stack(
        [at_i, at_x, jnp.int32(inline_size * BI), jnp.int32(xline_size * BX)]
    ).astype(jnp.int32)
    return convolutions(place, column, before_x, after_x, first, second)


def solution(mesh):
    return jax.shard_map(
        per_device,
        mesh=mesh,
        in_specs=(
            P(ALL, None),
            P(ALL, None),
            P(ALL),
            P(ALL),
            P(),
            P(),
            P(),
        ),
        out_specs=P(None, "inline", "xline", None),
        check_vma=False,
    )
```

time: 141 us -> 79.4 us (0.56)
  matrix products: 27.6 us -> 0 us
  starting transfers between devices: 45.9 us -> 23.9 us
  waiting for transfers between devices: 47.2 us -> 33 us
  Pallas kernels: 0 us -> 13.9 us
  local copies, waits for them, and re-layouts: 12.2 us -> 6.69 us
  other arithmetic: 5.77 us -> 0.92 us
    dot_general x57 -> x0, matrix products: 27.6 us -> none  [the longest x54 18.8 us: convolve(): jnp.einsum('oc,cijs->oijs', kernel[:, :, first, second, third], window, p...]
    ppermute x8 -> x4, starting transfers between devices: 27.9 us -> 13.1 us  [the longest x2 7.38 us: neighbours(): lax.ppermute(block, axis, backward)]
    pallas_call x0 -> x3, Pallas kernels: none -> 13.9 us  [the longest x1 5.44 us: pack(): pl.pallas_call(pack_kernel, in_specs=[kept] * 4, out_specs=kept, out_shap...]
    ppermute x8 -> x4, waiting for transfers between devices: 17 us -> 8.4 us  [the longest x2 5.91 us: neighbours(): lax.ppermute(block, axis, backward)]
    all_to_all x2 -> x1, starting transfers between devices: 18 us -> 10.8 us  [per_device(): lax.all_to_all(outgoing.reshape(devices, 2 * CAP, width), ALL, split_axis...]
    all_to_all x2 -> x1, waiting for transfers between devices: 30.2 us -> 24.6 us  [per_device(): lax.all_to_all(outgoing.reshape(devices, 2 * CAP, width), ALL, split_axis...]
    scatter x2 -> x0, local copies, waits for them, and re-layouts: 4.9 us -> none  [the longest x1 3.5 us: per_device(): jnp.zeros((devices_all * capacity, samples), jnp.bfloat16).at[position]]
    concatenate x4 -> x1, other arithmetic: 2.52 us -> 0.03 us  [per_device(): column = jnp.concatenate([before_i, volume, after_i], axis=0)]
  transfers between devices with their start and end apart: 10 -> 5, of which waited for: 8 -> 5; matrix products, arithmetic and copies ran while one was open for 5% -> 10% of each run, Pallas kernels for 0% -> 0%
where the time goes in v1:
time: 79.4 us; the launch traced here: 78.6 us
  waiting for transfers between devices  33 us (42%)
  starting transfers between devices  23.9 us (30%)
  Pallas kernels  13.9 us (18%)
  local copies, waits for them, and re-layouts  6.69 us (8%)
  other arithmetic  0.92 us (1%)
    all_to_all x1, waiting for transfers between devices, per_device(): lax.all_to_all(outgoing.reshape(devices, 2 * CAP, width), ALL, split_axis...  24.6 us
    all_to_all x1, starting transfers between devices, per_device(): lax.all_to_all(outgoing.reshape(devices, 2 * CAP, width), ALL, split_axis...  10.8 us
    ppermute x2, starting transfers between devices, neighbours(): lax.ppermute(block, axis, backward)  7.38 us
    ppermute x2, waiting for transfers between devices, neighbours(): lax.ppermute(block, axis, backward)  5.91 us
    ppermute x2, starting transfers between devices, neighbours(): lax.ppermute(block, axis, forward)  5.68 us
    pallas_call x1, Pallas kernels, pack(): pl.pallas_call(pack_kernel, in_specs=[kept] * 4, out_specs=kept, out_shap...  5.44 us
    pallas_call x1, Pallas kernels, convolutions(): pl.pallas_call(conv_kernel, in_specs=[pl.BlockSpec(memory_space=pltpu.SME...  4.35 us
    pallas_call x1, Pallas kernels, stack(): pl.pallas_call(stack_kernel, in_specs=[whole, pl.BlockSpec(memory_space=p...  4.14 us
  transfers between devices with their start and end apart: 5, of which 5 were waited for; matrix products, arithmetic and copies ran while one was open for 10% of the time, Pallas kernels for 0%

profile of v1, /device:TPU:3, one launch (start us, length us, event | category | flops | bytes accessed | tf_op | source)
XLA Modules:
  0.0 78.6 jit_solution(15144888425346283763)
XLA Ops:
  0.0 5.4 %pack.1 = bf16[1024,1152]{1,0:T(8,128)(2,1)} custom-call(s32[1,256]{1,0:T(1,128)} %bitcast.41, s32[1,256]{1,0:T(1,128)} %bitcast.42, s32[1,256]{1,0:T(1,128)} %bitcast.43, bf16[256,2048]{1,0:T(8,128)(2,1)} %traces_ref.1), custom_call_target="tpu_custom_call" | custom-call | tf_op jit(solution)/shard_map/pack/pallas_call | solution.py:104
  5.5 0.0 copy-start
  5.5 10.8 %all-to-all-start = ((bf16[128,8,1152]{2,1,0:T(8,128)(2,1)}), bf16[128,8,1152]{2,1,0:T(8,128)(2,1)S(1)}, u32[]{:S(2)}, u32[]{:S(2)}) async-start(bf16[128,8,1152]{2,1,0:T(8,128)(2,1)} %bitcast.37), calls=%async_computation | async-start | bytes 4718592 | tf_op jit(solution)/shard_map/all_to_all | solution.py:281
  16.3 0.0 copy-done
  16.3 0.2 pad_bitcast_fusion.3
  16.6 0.3 maximum_bitcast_fusion.1
  16.9 0.4 maximum_bitcast_fusion
  17.3 1.9 %copy.11 = bf16[3,32,2,2,4,4,32]{6,5,4,3,2,1,0:T(4,128)(2,1)} copy(bf16[3,32,2,2,4,4,32]{6,1,0,5,4,3,2:T(8,128)(2,1)S(1)} %maximum_bitcast_fusion) | data formatting | bytes 786432 | tf_op jit(solution)/shard_map/transpose | solution.py:256
  19.2 0.0 copy-start.1
  19.2 3.9 %reshape.30.second_ref = bf16[384,512]{1,0:T(8,128)(2,1)S(1)} reshape(bf16[3,32,2,2,4,4,32]{6,5,4,3,2,1,0:T(4,128)(2,1)} %copy.11) | data formatting | bytes 786432 | tf_op jit(solution)/shard_map/reshape | solution.py:257
  23.1 0.0 copy-done.1
  23.1 0.1 pad_bitcast_fusion.7
  23.2 0.1 maximum_bitcast_fusion.3
  23.3 0.2 copy.10
  23.5 0.2 reshape.29
  23.8 24.6 %all-to-all-done = bf16[128,8,1152]{2,1,0:T(8,128)(2,1)S(1)} async-done(((bf16[128,8,1152]{2,1,0:T(8,128)(2,1)}), bf16[128,8,1152]{2,1,0:T(8,128)(2,1)S(1)}, u32[]{:S(2)}, u32[]{:S(2)}) %all-to-all-start) | async-done | bytes 2359328 | tf_op jit(solution)/shard_map/all_to_all | solution.py:281
  48.4 4.1 %stack.69 = bf16[32,2048]{1,0:T(8,128)(2,1)S(1)} custom-call(bf16[1024,1152]{1,0:T(8,128)(2,1)S(1)} %bitcast.36, bf16[8,16,256,128]{3,2,1,0:T(8,128)(2,1)} %bitcast.38), custom_call_target="tpu_custom_call" | custom-call | tf_op jit(solution)/shard_map/stack/pallas_call | solution.py:162
  52.5 2.4 %collective-permute-start = (bf16[32,2048]{1,0:T(8,128)(2,1)S(1)}, bf16[32,2048]{1,0:T(8,128)(2,1)S(1)}, u32[]{:S(2)}, u32[]{:S(2)}) collective-permute-start(bf16[32,2048]{1,0:T(8,128)(2,1)S(1)} %stack.69), channel_id=1, source_target_pairs={{0,8},{8,16},{16,24},{24,32},{32,40},{40,48},{48,56},{56,64},{64,7... | collective-permute-start | bytes 393224 | tf_op jit(solution)/shard_map/ppermute | solution.py:264
  55.0 5.0 %collective-permute-start.1 = (bf16[32,2048]{1,0:T(8,128)(2,1)S(1)}, bf16[32,2048]{1,0:T(8,128)(2,1)S(1)}, u32[]{:S(2)}, u32[]{:S(2)}) collective-permute-start(bf16[32,2048]{1,0:T(8,128)(2,1)S(1)} %stack.69), channel_id=1, source_target_pairs={{8,0},{16,8},{24,16},{32,24},{40,32},{48,40},{56,48},{64,56},{72,6... | collective-permute-start | bytes 393224 | tf_op jit(solution)/shard_map/ppermute | solution.py:264
  59.9 0.4 collective-permute-done
  60.3 1.5 %collective-permute-done.1 = bf16[32,2048]{1,0:T(8,128)(2,1)S(1)} collective-permute-done((bf16[32,2048]{1,0:T(8,128)(2,1)S(1)}, bf16[32,2048]{1,0:T(8,128)(2,1)S(1)}, u32[]{:S(2)}, u32[]{:S(2)}) %collective-permute-start.1) | collective-permute-done | bytes 131104 | tf_op jit(solution)/shard_map/ppermute | solution.py:264
  61.9 3.3 %collective-permute-start.2 = (bf16[96,2048]{1,0:T(8,128)(2,1)S(1)}, bf16[96,2048]{1,0:T(8,128)(2,1)S(1)}, u32[]{:S(2)}, u32[]{:S(2)}) collective-permute-start(bf16[96,2048]{1,0:T(8,128)(2,1)S(1)} %pad_maximum_fusion.mid_ref), channel_id=1, source_target_pairs={{0,1},{1,2},{2,3},{3,4},{4,5},{5,6},{6,7},{8,9},{9,10},{10,11},{11... | collective-permute-start | bytes 1179656 | tf_op jit(solution)/shard_map/ppermute | solution.py:264
  65.2 2.4 %collective-permute-start.3 = (bf16[96,2048]{1,0:T(8,128)(2,1)S(1)}, bf16[96,2048]{1,0:T(8,128)(2,1)S(1)}, u32[]{:S(2)}, u32[]{:S(2)}) collective-permute-start(bf16[96,2048]{1,0:T(8,128)(2,1)S(1)} %pad_maximum_fusion.mid_ref), channel_id=1, source_target_pairs={{1,0},{2,1},{3,2},{4,3},{5,4},{6,5},{7,6},{9,8},{10,9},{11,10},{12... | collective-permute-start | bytes 1179656 | tf_op jit(solution)/shard_map/ppermute | solution.py:264
  67.6 0.1 pad_add_fusion.place_ref
  67.7 0.1 copy.12.first_ref
  67.8 2.1 %collective-permute-done.2.low_ref = bf16[96,2048]{1,0:T(8,128)(2,1)S(1)} collective-permute-done((bf16[96,2048]{1,0:T(8,128)(2,1)S(1)}, bf16[96,2048]{1,0:T(8,128)(2,1)S(1)}, u32[]{:S(2)}, u32[]{:S(2)}) %collective-permute-start.2) | collective-permute-done | bytes 393248 | tf_op jit(solution)/shard_map/ppermute | solution.py:264
  69.9 4.4 %collective-permute-done.3.high_ref = bf16[96,2048]{1,0:T(8,128)(2,1)S(1)} collective-permute-done((bf16[96,2048]{1,0:T(8,128)(2,1)S(1)}, bf16[96,2048]{1,0:T(8,128)(2,1)S(1)}, u32[]{:S(2)}, u32[]{:S(2)}) %collective-permute-start.3) | collective-permute-done | bytes 393248 | tf_op jit(solution)/shard_map/ppermute | solution.py:264
  74.3 4.4 %convolutions.1 = bf16[32,2,2,2048]{3,2,1,0:T(2,128)(2,1)} custom-call(s32[4]{0:T(128)S(1)} %pad_add_fusion.place_ref, bf16[96,2048]{1,0:T(8,128)(2,1)S(1)} %pad_maximum_fusion.mid_ref, bf16[96,2048]{1,0:T(8,128)(2,1)S(1)} %collective-permute-done.2.low_ref, bf16[96,2048]{1,0:T(8,128)(2,1)S(1)} %collective-permute-done.3.high_ref, ...), custom_call_target="tpu_custom_call" | custom-call | tf_op jit(solution)/shard_map/convolutions/pallas_call | solution.py:222
  (1 shorter events, 0.0 us)
Async XLA Ops:
  5.5 10.9 %copy-start = (bf16[32,32,3,3,3]{1,0,4,3,2:T(8,128)(2,1)S(1)}, bf16[32,32,3,3,3]{1,0,4,3,2:T(8,128)(2,1)}, u32[]{:S(2)}) copy-start(bf16[32,32,3,3,3]{1,0,4,3,2:T(8,128)(2,1)} %param.13) | copy-start | bytes 165892
  5.5 42.9 %all-to-all-start = ((bf16[128,8,1152]{2,1,0:T(8,128)(2,1)}), bf16[128,8,1152]{2,1,0:T(8,128)(2,1)S(1)}, u32[]{:S(2)}, u32[]{:S(2)}) async-start(bf16[128,8,1152]{2,1,0:T(8,128)(2,1)} %bitcast.37), calls=%async_computation | async-start | bytes 4718592 | tf_op jit(solution)/shard_map/all_to_all | solution.py:281
  19.2 3.9 %copy-start.1 = (bf16[32,8,3,3,3]{0,1,4,3,2:T(8,128)(2,1)S(1)}, bf16[32,8,3,3,3]{0,1,4,3,2:T(8,128)(2,1)}, u32[]{:S(2)}) copy-start(bf16[32,8,3,3,3]{0,1,4,3,2:T(8,128)(2,1)} %param.12) | copy-start | bytes 41476
  52.5 7.8 %collective-permute-start = (bf16[32,2048]{1,0:T(8,128)(2,1)S(1)}, bf16[32,2048]{1,0:T(8,128)(2,1)S(1)}, u32[]{:S(2)}, u32[]{:S(2)}) collective-permute-start(bf16[32,2048]{1,0:T(8,128)(2,1)S(1)} %stack.69), channel_id=1, source_target_pairs={{0,8},{8,16},{16,24},{24,32},{32,40},{40,48},{48,56},{56,64},{64,7... | collective-permute-start | bytes 393224 | tf_op jit(solution)/shard_map/ppermute | solution.py:264
  55.0 6.9 %collective-permute-start.1 = (bf16[32,2048]{1,0:T(8,128)(2,1)S(1)}, bf16[32,2048]{1,0:T(8,128)(2,1)S(1)}, u32[]{:S(2)}, u32[]{:S(2)}) collective-permute-start(bf16[32,2048]{1,0:T(8,128)(2,1)S(1)} %stack.69), channel_id=1, source_target_pairs={{8,0},{16,8},{24,16},{32,24},{40,32},{48,40},{56,48},{64,56},{72,6... | collective-permute-start | bytes 393224 | tf_op jit(solution)/shard_map/ppermute | solution.py:264
  61.9 8.0 %collective-permute-start.2 = (bf16[96,2048]{1,0:T(8,128)(2,1)S(1)}, bf16[96,2048]{1,0:T(8,128)(2,1)S(1)}, u32[]{:S(2)}, u32[]{:S(2)}) collective-permute-start(bf16[96,2048]{1,0:T(8,128)(2,1)S(1)} %pad_maximum_fusion.mid_ref), channel_id=1, source_target_pairs={{0,1},{1,2},{2,3},{3,4},{4,5},{5,6},{6,7},{8,9},{9,10},{10,11},{11... | collective-permute-start | bytes 1179656 | tf_op jit(solution)/shard_map/ppermute | solution.py:264
  65.2 9.1 %collective-permute-start.3 = (bf16[96,2048]{1,0:T(8,128)(2,1)S(1)}, bf16[96,2048]{1,0:T(8,128)(2,1)S(1)}, u32[]{:S(2)}, u32[]{:S(2)}) collective-permute-start(bf16[96,2048]{1,0:T(8,128)(2,1)S(1)} %pad_maximum_fusion.mid_ref), channel_id=1, source_target_pairs={{1,0},{2,1},{3,2},{4,3},{5,4},{6,5},{7,6},{9,8},{10,9},{11,10},{12... | collective-permute-start | bytes 1179656 | tf_op jit(solution)/shard_map/ppermute | solution.py:264

commit v2 on v1

--- a/solution.py
+++ b/solution.py
@@ -37,27 +37,28 @@
     return (iota((count, count), 0) < iota((count, count), 1)).astype(BF)
 
 
-def pack_kernel(dest_ref, bin_ref, class_ref, traces_ref, out_ref, tags, loaded, packed, tag_sem, load_sem, store_sem):
+def pack_kernel(
+    dest_ref, bin_ref, class_ref, traces_ref, out_ref, tags, loaded, packed, tag_sem, load_sem, store_sem
+):
     rows, width = packed.shape
     count, half = loaded.shape[0] // 2, loaded.shape[1]
     devices = rows // (2 * CAP)
-    strips = load_sem.shape[0]
-    tile = half // strips
+    parts = store_sem.shape[0]
+    each = rows // parts
     small = []
     for number, ref in enumerate((dest_ref, bin_ref, class_ref)):
         small.append(pltpu.make_async_copy(ref, tags.at[number], tag_sem.at[number]))
         small[-1].start()
     loads = []
-    for strip in range(strips):
-        for side in range(2):
-            loads.append(
-                pltpu.make_async_copy(
-                    traces_ref.at[:, pl.ds(side * half + strip * tile, tile)],
-                    loaded.at[pl.ds(side * count, count), pl.ds(strip * tile, tile)],
-                    load_sem.at[strip, side],
-                )
+    for side in range(2):
+        loads.append(
+            pltpu.make_async_copy(
+                traces_ref.at[:, pl.ds(side * half, half)],
+                loaded.at[pl.ds(side * count, count)],
+                load_sem.at[side],
             )
-            loads[-1].start()
+        )
+        loads[-1].start()
     for copy in small:
         copy.wait()
     dest = tags[0]
@@ -74,23 +75,16 @@
     tagged = jnp.concatenate(
         [((lane == cell) | (lane == 127)).astype(BF), (lane == cell + CELLS).astype(BF)], axis=1
     )
+    for load in loads:
+        load.wait()
     stores = []
-
-    def store(at, size, number):
-        copy = pltpu.make_async_copy(
-            packed.at[:, pl.ds(at, size)], out_ref.at[:, pl.ds(at, size)], store_sem.at[number]
-        )
-        copy.start()
-        stores.append(copy)
-
-    packed[:, half:] = nt(place, tagged).astype(BF)
-    store(half, 128, strips)
-    for strip in range(strips):
-        loads[2 * strip].wait()
-        loads[2 * strip + 1].wait()
-        at = strip * tile
-        packed[:, at : at + tile] = nn(place, loaded[:, at : at + tile]).astype(BF)
-        store(at, tile, strip)
+    for part in range(parts):
+        piece = slice(part * each, (part + 1) * each)
+        packed[piece, half:] = nt(place[piece], tagged).astype(BF)
+        packed[piece, :half] = nn(place[piece], loaded[...]).astype(BF)
+        chunk = pl.ds(part * each, each)
+        stores.append(pltpu.make_async_copy(packed.at[chunk], out_ref.at[chunk], store_sem.at[part]))
+        stores[-1].start()
     for copy in stores:
         copy.wait()
 
@@ -98,7 +92,6 @@
 def pack(traces, dest, bins, classes, devices):
     count, samples = traces.shape
     rows, width = devices * 2 * CAP, samples // 2 + 128
-    strips = 4
     kept = pl.BlockSpec(memory_space=pltpu.HBM)
     pin = lambda array: pltpu.with_memory_space_constraint(array, pltpu.HBM)
     return pl.pallas_call(
@@ -111,10 +104,10 @@
             pltpu.VMEM((2 * count, samples // 2), BF),
             pltpu.VMEM((rows, width), BF),
             pltpu.SemaphoreType.DMA((3,)),
-            pltpu.SemaphoreType.DMA((strips, 2)),
-            pltpu.SemaphoreType.DMA((strips + 1,)),
+            pltpu.SemaphoreType.DMA((2,)),
+            pltpu.SemaphoreType.DMA((4,)),
         ],
-        compiler_params=pltpu.CompilerParams(vmem_limit_bytes=40 << 20),
+        compiler_params=pltpu.CompilerParams(vmem_limit_bytes=24 << 20),
         name="pack",
     )(pin(dest), pin(bins), pin(classes), pin(traces))
 
@@ -185,65 +178,114 @@
     return jnp.where(iota(value.shape, 1) == samples - 1, 0.0, rolled)
 
 
-def conv_kernel(place_ref, mid_ref, low_ref, high_ref, first_ref, second_ref, out_ref, taps, hidden):
-    samples = mid_ref.shape[1]
+def fill(taps, refs):
     tall = BX * CLASSES
-    group = 9 * tall
-    for which, ref in enumerate((low_ref, mid_ref, high_ref)):
+    group = 3 * len(refs) * tall
+    for which, ref in enumerate(refs):
         value = ref[...].astype(F32)
         for tap, shifted in enumerate((later(value), value, sooner(value))):
             shifted = shifted.astype(BF)
             for line in range(BI + 4):
-                at = line * group + (tap * 3 + which) * tall
+                at = line * group + (tap * len(refs) + which) * tall
                 taps[at : at + tall, :] = shifted[line * tall : (line + 1) * tall]
-    wide = (BX + 2) * CH
-    bin_x = iota((wide, 1), 0) // CH + place_ref[1] * BX - 1
-    inside_x = (bin_x >= 0) & (bin_x < place_ref[3])
+    return group
+
+
+def inside(place_ref, start_x, line):
+    bin_x = iota((BX * CH, 1), 0) // CH + start_x + place_ref[1] * BX - 1
+    bin_i = line + place_ref[0] * BI - 1
+    return (bin_x >= 0) & (bin_x < place_ref[3]) & (bin_i >= 0) & (bin_i < place_ref[2])
+
+
+def joined(value):
+    rows = value.shape[0] // 3
+    return value[rows : 2 * rows] + later(value[:rows]) + sooner(value[2 * rows :])
+
+
+TILE = 512
+WIDE = BX * CH
+
+
+def near_kernel(place_ref, mid_ref, near_ref, first_ref, second_ref, partial_ref, sum_ref, taps, hidden):
+    samples = taps.shape[1]
+    group = fill(taps, (mid_ref, near_ref))
+    start_x = jnp.where(place_ref[1] % 2 == 0, BX, 0)
     first = first_ref[...]
-    tile = 512
     for line in range(BI + 2):
-        bin_i = line + place_ref[0] * BI - 1
-        inside = inside_x & (bin_i >= 0) & (bin_i < place_ref[2])
-        for start in range(0, samples, tile):
-            window = taps[line * group : (line + 3) * group, start : start + tile]
-            value = jax.nn.gelu(nn(first, window))
-            value = jnp.where(inside, value, 0.0)
-            hidden[line * wide : (line + 1) * wide, start : start + tile] = value.astype(BF)
-    second = second_ref[...]
-    value = nn(second, hidden[...])
-    rows = CH * BI * BX
-    total = value[rows : 2 * rows] + later(value[:rows]) + sooner(value[2 * rows :])
+        keep = inside(place_ref, start_x, line)
+        rows = slice(line * WIDE, (line + 1) * WIDE)
+        for start in range(0, samples, TILE):
+            lanes = slice(start, start + TILE)
+            both = nn(first, taps[line * group : (line + 3) * group, lanes])
+            hidden[rows, lanes] = jnp.where(keep, jax.nn.gelu(both[:WIDE]), 0.0).astype(BF)
+            partial_ref[rows, lanes] = both[WIDE:]
+    sum_ref[...] = joined(nn(second_ref[...], hidden[...]))
+
+
+def far_kernel(place_ref, far_ref, partial_ref, sum_ref, first_ref, second_ref, out_ref, taps, hidden):
+    samples = taps.shape[1]
+    group = fill(taps, (far_ref,))
+    start_x = jnp.where(place_ref[1] % 2 == 0, 0, BX)
+    first = first_ref[...]
+    for line in range(BI + 2):
+        keep = inside(place_ref, start_x, line)
+        rows = slice(line * WIDE, (line + 1) * WIDE)
+        for start in range(0, samples, TILE):
+            lanes = slice(start, start + TILE)
+            value = nn(first, taps[line * group : (line + 3) * group, lanes]) + partial_ref[rows, lanes]
+            hidden[rows, lanes] = jnp.where(keep, jax.nn.gelu(value), 0.0).astype(BF)
+    total = joined(nn(second_ref[...], hidden[...])) + sum_ref[...]
     out_ref[...] = total.astype(BF).reshape(out_ref.shape)
 
 
-def convolutions(place, mid, low, high, first, second):
+def convolutions(place, mid, near, far, matrices):
     samples = mid.shape[1]
+    first_near, first_far, second_near, second_far = matrices
     whole = pl.BlockSpec(memory_space=pltpu.VMEM)
+    scalars = pl.BlockSpec(memory_space=pltpu.SMEM)
+    tall = (BI + 4) * 3 * BX * CLASSES
+    bins = (BI + 2) * WIDE
+    partial, total = pl.pallas_call(
+        near_kernel,
+        in_specs=[scalars] + [whole] * 4,
+        out_specs=(whole, whole),
+        out_shape=(
+            jax.ShapeDtypeStruct((bins, samples), F32),
+            jax.ShapeDtypeStruct((CH * BI * BX, samples), F32),
+        ),
+        scratch_shapes=[pltpu.VMEM((2 * tall, samples), BF), pltpu.VMEM((bins, samples), BF)],
+        compiler_params=pltpu.CompilerParams(vmem_limit_bytes=24 << 20),
+        cost_estimate=pl.CostEstimate(flops=0, bytes_accessed=0, transcendentals=0),
+        name="near",
+    )(place, mid, near, first_near, second_near)
     return pl.pallas_call(
-        conv_kernel,
-        in_specs=[pl.BlockSpec(memory_space=pltpu.SMEM)] + [whole] * 5,
+        far_kernel,
+        in_specs=[scalars] + [whole] * 5,
         out_specs=whole,
         out_shape=jax.ShapeDtypeStruct((CH, BI, BX, samples), BF),
-        scratch_shapes=[
-            pltpu.VMEM(((BI + 4) * 9 * BX * CLASSES, samples), BF),
-            pltpu.VMEM(((BI + 2) * (BX + 2) * CH, samples), BF),
-        ],
-        compiler_params=pltpu.CompilerParams(vmem_limit_bytes=48 << 20),
-        name="convolutions",
-    )(place, mid, low, high, first, second)
-
-
-def first_matrix(kernel):
+        scratch_shapes=[pltpu.VMEM((tall, samples), BF), pltpu.VMEM((bins, samples), BF)],
+        compiler_params=pltpu.CompilerParams(vmem_limit_bytes=24 << 20),
+        name="far",
+    )(place, far, partial, total, first_far, second_far)
+
+
+def first_matrices(kernel, odd):
     spatial = kernel.transpose(2, 3, 4, 1, 0)
     placed = [
         jnp.pad(spatial, ((0, 0), (at, BX + 1 - at), (0, 0), (0, 0), (0, 0))) for at in range(BX + 2)
     ]
-    matrix = jnp.stack(placed, axis=0)
-    matrix = matrix.transpose(0, 5, 1, 3, 2, 4)
-    return matrix.reshape((BX + 2) * CH, 9 * (BX + 4) * CLASSES)
-
-
-def second_matrix(kernel):
+    matrix = jnp.stack(placed, axis=0).transpose(0, 5, 1, 3, 2, 4)
+    mirrored = jnp.concatenate([matrix[BX:], matrix[:BX]], axis=0)
+    mirrored = jnp.concatenate(
+        [mirrored[..., 2 * BX :, :], mirrored[..., BX : 2 * BX, :], mirrored[..., :BX, :]], axis=4
+    )
+    matrix = jnp.where(odd, mirrored, matrix)
+    near = jnp.concatenate([matrix[BX:, ..., BX:, :], matrix[:BX, ..., BX:, :]], axis=0)
+    far = matrix[:BX, ..., :BX, :]
+    return near.reshape(2 * WIDE, -1), far.reshape(WIDE, -1)
+
+
+def second_matrices(kernel, odd):
     spatial = kernel.transpose(2, 3, 4, 0, 1)
     placed = [
         [
@@ -254,14 +296,16 @@
     ]
     matrix = jnp.stack([jnp.stack(line, axis=0) for line in placed], axis=0)
     matrix = matrix.transpose(4, 5, 0, 1, 2, 3, 6)
-    return matrix.reshape(3 * CH * BI * BX, (BI + 2) * (BX + 2) * CH)
-
-
-def neighbours(block, axis):
+    low, high = matrix[..., :BX, :], matrix[..., BX:, :]
+    rows = 3 * CH * BI * BX
+    near, far = jnp.where(odd, low, high), jnp.where(odd, high, low)
+    return near.reshape(rows, -1), far.reshape(rows, -1)
+
+
+def swapped(block, axis, start):
     count = lax.axis_size(axis)
-    forward = [(i, i + 1) for i in range(count - 1)]
-    backward = [(target, source) for source, target in forward]
-    return lax.ppermute(block, axis, forward), lax.ppermute(block, axis, backward)
+    pairs = [(i, i + 1) for i in range(start, count - 1, 2)]
+    return lax.ppermute(block, axis, pairs + [(j, i) for i, j in pairs])
 
 
 def per_device(traces, trace_dest, trace_bin, trace_class, band_weights, conv_first, conv_second):
@@ -281,16 +325,19 @@
     arrived = lax.all_to_all(
         outgoing.reshape(devices, 2 * CAP, width), ALL, split_axis=0, concat_axis=0, tiled=True
     ).reshape(devices * 2 * CAP, width)
-    first, second = first_matrix(conv_first), second_matrix(conv_second)
-    arrived, first, second = lax.optimization_barrier((arrived, first, second))
+    odd_i, odd_x = at_i % 2 == 1, at_x % 2 == 1
+    matrices = first_matrices(conv_first, odd_x) + second_matrices(conv_second, odd_x)
+    arrived, matrices = lax.optimization_barrier((arrived, matrices))
     volume = stack(arrived, band_weights)
-    before_i, after_i = neighbours(volume, "inline")
-    column = jnp.concatenate([before_i, volume, after_i], axis=0)
-    before_x, after_x = neighbours(column, "xline")
+    one, other = swapped(volume, "inline", 0), swapped(volume, "inline", 1)
+    up, down = jnp.where(odd_i, one, other), jnp.where(odd_i, other, one)
+    column = jnp.concatenate([up, volume, down], axis=0)
+    far = swapped(column, "xline", 1)
+    near = swapped(column, "xline", 0)
     place = jnp.stack(
         [at_i, at_x, jnp.int32(inline_size * BI), jnp.int32(xline_size * BX)]
     ).astype(jnp.int32)
-    return convolutions(place, column, before_x, after_x, first, second)
+    return convolutions(place, column, near, far, matrices)
 
 
 def solution(mesh):

time: 79.4 us -> 73.7 us (0.928)
  starting transfers between devices: 23.9 us -> 18.8 us
  other arithmetic: 0.92 us -> 2.3 us
  local copies, waits for them, and re-layouts: 6.69 us -> 5.8 us
    ppermute x4, starting transfers between devices: 13.1 us -> 7.94 us  [swapped(): return lax.ppermute(block, axis, pairs + [(j, i) for i, j in pairs])]
    select_n x0 -> x2, local copies, waits for them, and re-layouts: none -> 2.35 us  [second_matrices(): near, far = (jnp.where(odd, low, high), jnp.where(odd, high, low))]
    transpose x2 -> x0, local copies, waits for them, and re-layouts: 2.13 us -> none  [the longest x1 1.95 us: second_matrix(): matrix = matrix.transpose(4, 5, 0, 1, 2, 3, 6)]
    pallas_call x1, Pallas kernels: 5.44 us -> 3.79 us  [pack(): pl.pallas_call(pack_kernel, in_specs=[kept] * 4, out_specs=kept, out_shap...]
    reshape x2 -> x4, local copies, waits for them, and re-layouts: 4.15 us -> 2.59 us  [the longest x2 1.55 us: first_matrices(): return (near.reshape(2 * WIDE, -1), far.reshape(WIDE, -1))]
    pallas_call x1 -> x2, Pallas kernels: 4.35 us -> 5.81 us  [the longest x1 3.24 us: convolutions(): pl.pallas_call(far_kernel, in_specs=[scalars] + [whole] * 5, out_specs=wh...]
    select_n x0 -> x3, other arithmetic: none -> 1.25 us  [the longest x1 0.99 us: second_matrices(): near, far = (jnp.where(odd, low, high), jnp.where(odd, high, low))]
  transfers between devices with their start and end apart: 5 -> 5, of which waited for: 5 -> 3; matrix products, arithmetic and copies ran while one was open for 10% -> 11% of each run, Pallas kernels for 0% -> 3%
where the time goes in v2:
time: 73.7 us; the launch traced here: 73.5 us
  waiting for transfers between devices  32.6 us (44%)
  starting transfers between devices  18.8 us (26%)
  Pallas kernels  13.7 us (19%)
  local copies, waits for them, and re-layouts  5.8 us (8%)
  other arithmetic  2.3 us (3%)
    all_to_all x1, waiting for transfers between devices, per_device(): lax.all_to_all(outgoing.reshape(devices, 2 * CAP, width), ALL, split_axis...  24.2 us
    all_to_all x1, starting transfers between devices, per_device(): lax.all_to_all(outgoing.reshape(devices, 2 * CAP, width), ALL, split_axis...  10.8 us
    ppermute x4, waiting for transfers between devices, swapped(): return lax.ppermute(block, axis, pairs + [(j, i) for i, j in pairs])  8.38 us
    ppermute x4, starting transfers between devices, swapped(): return lax.ppermute(block, axis, pairs + [(j, i) for i, j in pairs])  7.94 us
    pallas_call x1, Pallas kernels, stack(): pl.pallas_call(stack_kernel, in_specs=[whole, pl.BlockSpec(memory_space=p...  4.14 us
    pallas_call x1, Pallas kernels, pack(): pl.pallas_call(pack_kernel, in_specs=[kept] * 4, out_specs=kept, out_shap...  3.79 us
    pallas_call x1, Pallas kernels, convolutions(): pl.pallas_call(far_kernel, in_specs=[scalars] + [whole] * 5, out_specs=wh...  3.24 us
    pallas_call x1, Pallas kernels, convolutions(): pl.pallas_call(near_kernel, in_specs=[scalars] + [whole] * 4, out_specs=(...  2.57 us
  transfers between devices with their start and end apart: 5, of which 3 were waited for; matrix products, arithmetic and copies ran while one was open for 11% of the time, Pallas kernels for 3%

profile of v2, /device:TPU:3, one launch (start us, length us, event | category | flops | bytes accessed | tf_op | source)
XLA Modules:
  0.0 73.5 jit_solution(4388006191965181152)
XLA Ops:
  0.0 3.8 %pack.1 = bf16[1024,1152]{1,0:T(8,128)(2,1)} custom-call(s32[1,256]{1,0:T(1,128)} %bitcast.45, s32[1,256]{1,0:T(1,128)} %bitcast.46, s32[1,256]{1,0:T(1,128)} %bitcast.47, bf16[256,2048]{1,0:T(8,128)(2,1)} %traces_ref.1), custom_call_target="tpu_custom_call" | custom-call | tf_op jit(solution)/shard_map/pack/pallas_call | solution.py:97
  3.8 10.8 %all-to-all-start = ((bf16[128,8,1152]{2,1,0:T(8,128)(2,1)}), bf16[128,8,1152]{2,1,0:T(8,128)(2,1)S(1)}, u32[]{:S(2)}, u32[]{:S(2)}) async-start(bf16[128,8,1152]{2,1,0:T(8,128)(2,1)} %bitcast.41), calls=%async_computation | async-start | bytes 4718592 | tf_op jit(solution)/shard_map/all_to_all | solution.py:325
  14.7 0.1 pad_bitcast_fusion.7
  14.8 0.1 maximum_bitcast_fusion.3
  14.9 0.1 fusion.3
  15.0 0.2 fusion.1
  15.3 0.1 pad_maximum_fusion.2
  15.4 0.2 copy.12
  15.6 0.8 %reshape.35 = bf16[128,288]{0,1:T(8,128)(2,1)} reshape(bf16[4,32,3,3,4,8]{1,0,5,4,3,2:T(4,128)(2,1)S(1)} %copy.12) | data formatting | bytes 147456 | tf_op jit(solution)/shard_map/reshape | solution.py:285
  16.4 0.1 copy.13
  16.4 0.7 reshape.36
  17.2 0.3 pad_bitcast_fusion.3
  17.4 0.3 maximum_bitcast_fusion.1
  17.8 0.4 maximum_bitcast_fusion
  18.2 1.0 %broadcast_select_fusion = (bf16[3,32,2,2,4,2,32]{6,1,0,5,4,3,2:T(8,128)(2,1)S(1)}, bf16[3,32,2,2,4,2,32]{6,1,0,5,4,3,2:T(8,128)(2,1)}) fusion(pred[]{:T(512)S(6)} %eq.10, bf16[3,32,2,2,4,4,32]{6,1,0,5,4,3,2:T(8,128)(2,1)S(1)} %maximum_bitcast_fusion), kind=kLoop, calls=%fused_computation.3 | loop fusion | flops 196608 | bytes 786433 | tf_op jit(solution)/shard_map/jit(_where)/select_n | solution.py:301
  19.1 0.6 copy.15
  19.7 0.5 reshape.38.second_ref
  20.3 1.7 %copy.14 = bf16[3,32,2,2,4,2,32]{6,5,4,3,2,1,0:T(2,128)(2,1)S(1)} copy(bf16[3,32,2,2,4,2,32]{6,1,0,5,4,3,2:T(8,128)(2,1)} %get-tuple-element.20) | data formatting | bytes 393216 | tf_op jit(solution)/shard_map/jit(_where)/select_n | solution.py:301
  22.0 0.5 reshape.37.second_ref
  22.6 24.2 %all-to-all-done = bf16[128,8,1152]{2,1,0:T(8,128)(2,1)S(1)} async-done(((bf16[128,8,1152]{2,1,0:T(8,128)(2,1)}), bf16[128,8,1152]{2,1,0:T(8,128)(2,1)S(1)}, u32[]{:S(2)}, u32[]{:S(2)}) %all-to-all-start) | async-done | bytes 2359328 | tf_op jit(solution)/shard_map/all_to_all | solution.py:325
  46.7 4.1 %stack.69 = bf16[32,2048]{1,0:T(8,128)(2,1)S(1)} custom-call(bf16[1024,1152]{1,0:T(8,128)(2,1)S(1)} %bitcast.40, bf16[8,16,256,128]{3,2,1,0:T(8,128)(2,1)} %bitcast.42), custom_call_target="tpu_custom_call" | custom-call | tf_op jit(solution)/shard_map/stack/pallas_call | solution.py:155
  50.9 3.4 %collective-permute-start.1 = (bf16[32,2048]{1,0:T(8,128)(2,1)S(1)}, bf16[32,2048]{1,0:T(8,128)(2,1)S(1)}, u32[]{:S(2)}, u32[]{:S(2)}) collective-permute-start(bf16[32,2048]{1,0:T(8,128)(2,1)S(1)} %stack.69), channel_id=1, source_target_pairs={{8,16},{24,32},{40,48},{56,64},{72,80},{88,96},{104,112},{16,8},{3... | collective-permute-start | bytes 393224 | tf_op jit(solution)/shard_map/ppermute | solution.py:308
  54.3 0.1 collective-permute-start
  54.4 4.3 %collective-permute-done.1 = bf16[32,2048]{1,0:T(8,128)(2,1)S(1)} collective-permute-done((bf16[32,2048]{1,0:T(8,128)(2,1)S(1)}, bf16[32,2048]{1,0:T(8,128)(2,1)S(1)}, u32[]{:S(2)}, u32[]{:S(2)}) %collective-permute-start.1) | collective-permute-done | bytes 131104 | tf_op jit(solution)/shard_map/ppermute | solution.py:308
  58.8 2.4 %collective-permute-start.3 = (bf16[96,2048]{1,0:T(8,128)(2,1)S(1)}, bf16[96,2048]{1,0:T(8,128)(2,1)S(1)}, u32[]{:S(2)}, u32[]{:S(2)}) collective-permute-start(bf16[96,2048]{1,0:T(8,128)(2,1)S(1)} %pad_maximum_fusion.1.mid_ref), channel_id=1, source_target_pairs={{0,1},{2,3},{4,5},{6,7},{1,0},{3,2},{5,4},{7,6},{8,9},{10,11},{12,... | collective-permute-start | bytes 1179656 | tf_op jit(solution)/shard_map/ppermute | solution.py:308
  61.1 2.1 %collective-permute-start.2 = (bf16[96,2048]{1,0:T(8,128)(2,1)S(1)}, bf16[96,2048]{1,0:T(8,128)(2,1)S(1)}, u32[]{:S(2)}, u32[]{:S(2)}) collective-permute-start(bf16[96,2048]{1,0:T(8,128)(2,1)S(1)} %pad_maximum_fusion.1.mid_ref), channel_id=1, source_target_pairs={{1,2},{3,4},{5,6},{2,1},{4,3},{6,5},{9,10},{11,12},{13,14},{10,9},... | collective-permute-start | bytes 1179656 | tf_op jit(solution)/shard_map/ppermute | solution.py:308
  63.2 0.1 pad_add_fusion.place_ref
  63.3 0.1 copy.17.first_ref
  63.4 0.1 copy.16.first_ref
  63.6 2.6 %near.1 = (f32[256,2048]{1,0:T(8,128)S(1)}, f32[128,2048]{1,0:T(8,128)S(1)}) custom-call(s32[4]{0:T(128)S(1)} %pad_add_fusion.place_ref, bf16[96,2048]{1,0:T(8,128)(2,1)S(1)} %pad_maximum_fusion.1.mid_ref, bf16[96,2048]{1,0:T(8,128)(2,1)S(1)} %collective-permute-done.3.near_ref, bf16[128,288]{1,0:T(8,128)(2,1)S(1)} %copy.16.first_ref, ...), custom_call_target="tpu_custom_call" | custom-call | tf_op jit(solution)/shard_map/near/pallas_call | solution.py:248
  66.1 4.1 %collective-permute-done.2.far_ref = bf16[96,2048]{1,0:T(8,128)(2,1)S(1)} collective-permute-done((bf16[96,2048]{1,0:T(8,128)(2,1)S(1)}, bf16[96,2048]{1,0:T(8,128)(2,1)S(1)}, u32[]{:S(2)}, u32[]{:S(2)}) %collective-permute-start.2) | collective-permute-done | bytes 393248 | tf_op jit(solution)/shard_map/ppermute | solution.py:308
  70.2 3.2 %far.1 = bf16[32,2,2,2048]{3,2,1,0:T(2,128)(2,1)} custom-call(s32[4]{0:T(128)S(1)} %pad_add_fusion.place_ref, bf16[96,2048]{1,0:T(8,128)(2,1)S(1)} %collective-permute-done.2.far_ref, f32[256,2048]{1,0:T(8,128)S(1)} %get-tuple-element.15.partial_ref, f32[128,2048]{1,0:T(8,128)S(1)} %get-tuple-element.16.sum_ref, bf16[64,144]{1,0:T(8,128)(2,1)S(1)} %copy.17.first_ref, ...), custom_call_target="tpu_custom_call" | custom-call | tf_op jit(solution)/shard_map/far/pallas_call | solution.py:261
  (15 shorter events, 0.2 us)
Async XLA Ops:
  3.8 10.9 %copy-start.3 = (bf16[32,8,3,3,3]{0,1,4,3,2:T(8,128)(2,1)S(1)}, bf16[32,8,3,3,3]{0,1,4,3,2:T(8,128)(2,1)}, u32[]{:S(2)}) copy-start(bf16[32,8,3,3,3]{0,1,4,3,2:T(8,128)(2,1)} %param.12) | copy-start | bytes 41476
  3.8 42.9 %all-to-all-start = ((bf16[128,8,1152]{2,1,0:T(8,128)(2,1)}), bf16[128,8,1152]{2,1,0:T(8,128)(2,1)S(1)}, u32[]{:S(2)}, u32[]{:S(2)}) async-start(bf16[128,8,1152]{2,1,0:T(8,128)(2,1)} %bitcast.41), calls=%async_computation | async-start | bytes 4718592 | tf_op jit(solution)/shard_map/all_to_all | solution.py:325
  15.3 1.9 %copy-start.1 = (bf16[32,32,3,3,3]{1,0,4,3,2:T(8,128)(2,1)S(1)}, bf16[32,32,3,3,3]{1,0,4,3,2:T(8,128)(2,1)}, u32[]{:S(2)}) copy-start(bf16[32,32,3,3,3]{1,0,4,3,2:T(8,128)(2,1)} %param.13) | copy-start | bytes 165892
  46.7 16.6 %copy-start.2 = (bf16[64,144]{0,1:T(8,128)(2,1)S(1)}, bf16[64,144]{0,1:T(8,128)(2,1)}, u32[]{:S(2)}) copy-start(bf16[64,144]{0,1:T(8,128)(2,1)} %reshape.36) | copy-start | bytes 55300
  46.7 16.7 %copy-start = (bf16[128,288]{0,1:T(8,128)(2,1)S(1)}, bf16[128,288]{0,1:T(8,128)(2,1)}, u32[]{:S(2)}) copy-start(bf16[128,288]{0,1:T(8,128)(2,1)} %reshape.35) | copy-start | bytes 221188
  50.9 7.8 %collective-permute-start.1 = (bf16[32,2048]{1,0:T(8,128)(2,1)S(1)}, bf16[32,2048]{1,0:T(8,128)(2,1)S(1)}, u32[]{:S(2)}, u32[]{:S(2)}) collective-permute-start(bf16[32,2048]{1,0:T(8,128)(2,1)S(1)} %stack.69), channel_id=1, source_target_pairs={{8,16},{24,32},{40,48},{56,64},{72,80},{88,96},{104,112},{16,8},{3... | collective-permute-start | bytes 393224 | tf_op jit(solution)/shard_map/ppermute | solution.py:308
  54.3 4.4 %collective-permute-start = (bf16[32,2048]{1,0:T(8,128)(2,1)S(1)}, bf16[32,2048]{1,0:T(8,128)(2,1)S(1)}, u32[]{:S(2)}, u32[]{:S(2)}) collective-permute-start(bf16[32,2048]{1,0:T(8,128)(2,1)S(1)} %stack.69), channel_id=1, source_target_pairs={{0,8},{16,24},{32,40},{48,56},{64,72},{80,88},{96,104},{112,120},{... | collective-permute-start | bytes 393224 | tf_op jit(solution)/shard_map/ppermute | solution.py:308
  58.8 4.8 %collective-permute-start.3 = (bf16[96,2048]{1,0:T(8,128)(2,1)S(1)}, bf16[96,2048]{1,0:T(8,128)(2,1)S(1)}, u32[]{:S(2)}, u32[]{:S(2)}) collective-permute-start(bf16[96,2048]{1,0:T(8,128)(2,1)S(1)} %pad_maximum_fusion.1.mid_ref), channel_id=1, source_target_pairs={{0,1},{2,3},{4,5},{6,7},{1,0},{3,2},{5,4},{7,6},{8,9},{10,11},{12,... | collective-permute-start | bytes 1179656 | tf_op jit(solution)/shard_map/ppermute | solution.py:308
  61.1 9.1 %collective-permute-start.2 = (bf16[96,2048]{1,0:T(8,128)(2,1)S(1)}, bf16[96,2048]{1,0:T(8,128)(2,1)S(1)}, u32[]{:S(2)}, u32[]{:S(2)}) collective-permute-start(bf16[96,2048]{1,0:T(8,128)(2,1)S(1)} %pad_maximum_fusion.1.mid_ref), channel_id=1, source_target_pairs={{1,2},{3,4},{5,6},{2,1},{4,3},{6,5},{9,10},{11,12},{13,14},{10,9},... | collective-permute-start | bytes 1179656 | tf_op jit(solution)/shard_map/ppermute | solution.py:308

commit v3 on v2

--- a/solution.py
+++ b/solution.py
@@ -66,10 +66,6 @@
     rank = nn(named.astype(BF), before(count))
     slot = jnp.sum(jnp.where(named, rank, 0.0), axis=0, keepdims=True)
     position = dest * (2 * CAP) + slot.astype(jnp.int32)
-    row = iota((rows, count), 0)
-    place = jnp.concatenate(
-        [(row == position).astype(BF), (row == position + CAP).astype(BF)], axis=1
-    )
     cell = tags[1] * CLASSES + tags[2]
     lane = iota((128, count), 0)
     tagged = jnp.concatenate(
@@ -80,8 +76,12 @@
     stores = []
     for part in range(parts):
         piece = slice(part * each, (part + 1) * each)
-        packed[piece, half:] = nt(place[piece], tagged).astype(BF)
-        packed[piece, :half] = nn(place[piece], loaded[...]).astype(BF)
+        row = iota((each, count), 0) + part * each
+        place = jnp.concatenate(
+            [(row == position).astype(BF), (row == position + CAP).astype(BF)], axis=1
+        )
+        packed[piece, half:] = nt(place, tagged).astype(BF)
+        packed[piece, :half] = nn(place, loaded[...]).astype(BF)
         chunk = pl.ds(part * each, each)
         stores.append(pltpu.make_async_copy(packed.at[chunk], out_ref.at[chunk], store_sem.at[part]))
         stores[-1].start()
@@ -112,82 +112,116 @@
     )(pin(dest), pin(bins), pin(classes), pin(traces))
 
 
-def stack_kernel(arrived_ref, band_ref, out_ref, averaged, weights, sem):
+def stack_kernel(arrived_ref, out_ref):
     width = arrived_ref.shape[1]
     half = width - 128
-    parts, _, each, _, band = weights.shape
-    loads = []
-    for part in range(parts):
-        loads.append(
-            pltpu.make_async_copy(
-                band_ref.at[:, pl.ds(part * each, each)], weights.at[part], sem.at[part]
-            )
-        )
-        loads[-1].start()
     stacked = tn(arrived_ref[:, half:], arrived_ref[...])
     fold = jnp.maximum(stacked[:CELLS, width - 1 : width], 1.0)
-    averaged[:, :half] = (stacked[:CELLS, :half] / fold).astype(BF)
-    averaged[:, half : 2 * half] = (stacked[CELLS : 2 * CELLS, :half] / fold).astype(BF)
-    averaged[:, 2 * half :] = jnp.zeros((CELLS, band), BF)
-    kind = iota((CELLS, band), 0) % CLASSES
-    for block in range(parts * each):
-        if block % each == 0:
-            loads[block // each].wait()
-        start = block * band
-        pair = averaged[:, start : start + 2 * band]
-        wide = jnp.concatenate(
-            [weights[block // each, number, block % each] for number in range(CLASSES)], axis=1
-        )
-        moved = nn(pair, wide)
-        total = moved[:, :band]
-        for number in range(1, CLASSES):
-            total = jnp.where(kind == number, moved[:, number * band : (number + 1) * band], total)
-        out_ref[:, start : start + band] = total.astype(BF)
-
-
-def stack(arrived, band_weights):
+    out_ref[:, :half] = (stacked[:CELLS, :half] / fold).astype(BF)
+    out_ref[:, half:] = (stacked[CELLS : 2 * CELLS, :half] / fold).astype(BF)
+
+
+def stack(arrived):
     rows, width = arrived.shape
-    samples = 2 * (width - 128)
-    classes, blocks, steps, band, _ = band_weights.shape
-    weights = band_weights.reshape(classes, blocks, steps * band, band)
-    parts = 8
     whole = pl.BlockSpec(memory_space=pltpu.VMEM)
     return pl.pallas_call(
         stack_kernel,
+        in_specs=[whole],
+        out_specs=whole,
+        out_shape=jax.ShapeDtypeStruct((CELLS, 2 * (width - 128)), BF),
+        compiler_params=pltpu.CompilerParams(vmem_limit_bytes=12 << 20),
+        name="stack",
+    )(arrived)
+
+
+BAND_PARTS = 8
+
+
+def band_loads(source_ref, weights, sem):
+    each = weights.shape[1] // BAND_PARTS
+    loads = []
+    for part in range(BAND_PARTS):
+        blocks = pl.ds(part * each, each)
+        loads.append(pltpu.make_async_copy(source_ref.at[:, blocks], weights.at[:, blocks], sem.at[part]))
+        loads[-1].start()
+    return loads
+
+
+def move_out(averaged, weights, out, loads=None):
+    rows = averaged.shape[0]
+    classes, blocks, _, band = weights.shape
+    kind = iota((rows, band), 0) % classes
+    for block in range(blocks):
+        if loads is not None and block % (blocks // BAND_PARTS) == 0:
+            loads[block // (blocks // BAND_PARTS)].wait()
+        start = block * band
+        wide = jnp.concatenate([weights[number, block] for number in range(classes)], axis=1)
+        moved = nn(averaged[:, start : start + 2 * band], wide)
+        total = moved[:, :band]
+        for number in range(1, classes):
+            total = jnp.where(kind == number, moved[:, number * band : (number + 1) * band], total)
+        out[:, start : start + band] = total.astype(BF)
+
+
+def band_kernel(averaged_ref, band_ref, out_ref, weights, padded, sem):
+    loads = band_loads(band_ref, weights, sem)
+    rows, samples = averaged_ref.shape
+    padded[:, :samples] = averaged_ref[...]
+    padded[:, samples:] = jnp.zeros((rows, padded.shape[1] - samples), BF)
+    move_out(padded, weights, out_ref, loads)
+
+
+def moved_out(averaged, weights):
+    rows, samples = averaged.shape
+    whole = pl.BlockSpec(memory_space=pltpu.VMEM)
+    return pl.pallas_call(
+        band_kernel,
         in_specs=[whole, pl.BlockSpec(memory_space=pltpu.HBM)],
         out_specs=whole,
-        out_shape=jax.ShapeDtypeStruct((CELLS, samples), BF),
+        out_shape=jax.ShapeDtypeStruct((rows, samples), BF),
         scratch_shapes=[
-            pltpu.VMEM((CELLS, samples + band), BF),
-            pltpu.VMEM((parts, classes, blocks // parts, steps * band, band), BF),
-            pltpu.SemaphoreType.DMA((parts,)),
+            pltpu.VMEM(weights.shape, BF),
+            pltpu.VMEM((rows, samples + weights.shape[3]), BF),
+            pltpu.SemaphoreType.DMA((BAND_PARTS,)),
         ],
-        compiler_params=pltpu.CompilerParams(vmem_limit_bytes=24 << 20),
-        name="stack",
-    )(arrived, pltpu.with_memory_space_constraint(weights, pltpu.HBM))
+        compiler_params=pltpu.CompilerParams(vmem_limit_bytes=16 << 20),
+        name="band",
+    )(averaged, pltpu.with_memory_space_constraint(weights, pltpu.HBM))
 
 
 def later(value):
     rolled = pltpu.roll(value, 1, 1)
-    return jnp.where(iota(value.shape, 1) == 0, 0.0, rolled)
+    return jnp.where(iota(value.shape, 1) == 0, jnp.zeros_like(rolled), rolled)
 
 
 def sooner(value):
     samples = value.shape[1]
     rolled = pltpu.roll(value, samples - 1, 1)
-    return jnp.where(iota(value.shape, 1) == samples - 1, 0.0, rolled)
-
-
-def fill(taps, refs):
+    return jnp.where(iota(value.shape, 1) == samples - 1, jnp.zeros_like(rolled), rolled)
+
+
+def fill(taps, columns, weights, padded, moved, loads=None):
     tall = BX * CLASSES
-    group = 3 * len(refs) * tall
-    for which, ref in enumerate(refs):
-        value = ref[...].astype(F32)
+    group = 3 * len(columns) * tall
+    samples = moved.shape[1]
+
+    def place(value, first_line, which):
         for tap, shifted in enumerate((later(value), value, sooner(value))):
-            shifted = shifted.astype(BF)
-            for line in range(BI + 4):
-                at = line * group + (tap * len(refs) + which) * tall
+            for line in range(BI):
+                at = (first_line + line) * group + (tap * len(columns) + which) * tall
                 taps[at : at + tall, :] = shifted[line * tall : (line + 1) * tall]
+
+    padded[:, samples:] = jnp.zeros((padded.shape[0], padded.shape[1] - samples), BF)
+    for which, column in enumerate(columns):
+        at = 2 * which * CELLS
+        padded[at : at + CELLS, :samples] = column[:CELLS, :]
+        padded[at + CELLS : at + 2 * CELLS, :samples] = column[2 * CELLS :, :]
+        place(column[CELLS : 2 * CELLS, :], BI, which)
+    move_out(padded, weights, moved, loads)
+    for which in range(len(columns)):
+        at = 2 * which * CELLS
+        place(moved[at : at + CELLS, :], 0, which)
+        place(moved[at + CELLS : at + 2 * CELLS, :], 2 * BI, which)
     return group
 
 
@@ -206,9 +240,13 @@
 WIDE = BX * CH
 
 
-def near_kernel(place_ref, mid_ref, near_ref, first_ref, second_ref, partial_ref, sum_ref, taps, hidden):
+def near_kernel(
+    place_ref, band_ref, mid_ref, near_ref, first_ref, second_ref,
+    partial_ref, sum_ref, weights, taps, hidden, padded, moved, sem,
+):
     samples = taps.shape[1]
-    group = fill(taps, (mid_ref, near_ref))
+    loads = band_loads(band_ref, weights, sem)
+    group = fill(taps, (mid_ref, near_ref), weights, padded, moved, loads)
     start_x = jnp.where(place_ref[1] % 2 == 0, BX, 0)
     first = first_ref[...]
     for line in range(BI + 2):
@@ -222,9 +260,11 @@
     sum_ref[...] = joined(nn(second_ref[...], hidden[...]))
 
 
-def far_kernel(place_ref, far_ref, partial_ref, sum_ref, first_ref, second_ref, out_ref, taps, hidden):
+def far_kernel(
+    place_ref, weights, far_ref, partial_ref, sum_ref, first_ref, second_ref, out_ref, taps, hidden, padded, moved
+):
     samples = taps.shape[1]
-    group = fill(taps, (far_ref,))
+    group = fill(taps, (far_ref,), weights, padded, moved)
     start_x = jnp.where(place_ref[1] % 2 == 0, 0, BX)
     first = first_ref[...]
     for line in range(BI + 2):
@@ -234,39 +274,52 @@
             lanes = slice(start, start + TILE)
             value = nn(first, taps[line * group : (line + 3) * group, lanes]) + partial_ref[rows, lanes]
             hidden[rows, lanes] = jnp.where(keep, jax.nn.gelu(value), 0.0).astype(BF)
-    total = joined(nn(second_ref[...], hidden[...])) + sum_ref[...]
+    held = hidden[...]
+    total = nn(second_ref[...], jnp.concatenate([later(held), held, sooner(held)], axis=0)) + sum_ref[...]
     out_ref[...] = total.astype(BF).reshape(out_ref.shape)
 
 
-def convolutions(place, mid, near, far, matrices):
+def convolutions(place, weights, mid, near, far, matrices):
     samples = mid.shape[1]
     first_near, first_far, second_near, second_far = matrices
     whole = pl.BlockSpec(memory_space=pltpu.VMEM)
     scalars = pl.BlockSpec(memory_space=pltpu.SMEM)
     tall = (BI + 4) * 3 * BX * CLASSES
     bins = (BI + 2) * WIDE
-    partial, total = pl.pallas_call(
+    longer = samples + weights.shape[3]
+    partial, total, held = pl.pallas_call(
         near_kernel,
-        in_specs=[scalars] + [whole] * 4,
-        out_specs=(whole, whole),
+        in_specs=[scalars, pl.BlockSpec(memory_space=pltpu.HBM)] + [whole] * 4,
+        out_specs=(whole, whole, whole),
         out_shape=(
             jax.ShapeDtypeStruct((bins, samples), F32),
             jax.ShapeDtypeStruct((CH * BI * BX, samples), F32),
+            jax.ShapeDtypeStruct(weights.shape, BF),
         ),
-        scratch_shapes=[pltpu.VMEM((2 * tall, samples), BF), pltpu.VMEM((bins, samples), BF)],
+        scratch_shapes=[
+            pltpu.VMEM((2 * tall, samples), BF),
+            pltpu.VMEM((bins, samples), BF),
+            pltpu.VMEM((4 * CELLS, longer), BF),
+            pltpu.VMEM((4 * CELLS, samples), BF),
+            pltpu.SemaphoreType.DMA((BAND_PARTS,)),
+        ],
         compiler_params=pltpu.CompilerParams(vmem_limit_bytes=24 << 20),
-        cost_estimate=pl.CostEstimate(flops=0, bytes_accessed=0, transcendentals=0),
         name="near",
-    )(place, mid, near, first_near, second_near)
+    )(place, pltpu.with_memory_space_constraint(weights, pltpu.HBM), mid, near, first_near, second_near)
     return pl.pallas_call(
         far_kernel,
-        in_specs=[scalars] + [whole] * 5,
+        in_specs=[scalars] + [whole] * 6,
         out_specs=whole,
         out_shape=jax.ShapeDtypeStruct((CH, BI, BX, samples), BF),
-        scratch_shapes=[pltpu.VMEM((tall, samples), BF), pltpu.VMEM((bins, samples), BF)],
+        scratch_shapes=[
+            pltpu.VMEM((tall, samples), BF),
+            pltpu.VMEM((bins, samples), BF),
+            pltpu.VMEM((2 * CELLS, longer), BF),
+            pltpu.VMEM((2 * CELLS, samples), BF),
+        ],
         compiler_params=pltpu.CompilerParams(vmem_limit_bytes=24 << 20),
         name="far",
-    )(place, far, partial, total, first_far, second_far)
+    )(place, held, far, partial, total, first_far, second_far)
 
 
 def first_matrices(kernel, odd):
@@ -299,7 +352,8 @@
     low, high = matrix[..., :BX, :], matrix[..., BX:, :]
     rows = 3 * CH * BI * BX
     near, far = jnp.where(odd, low, high), jnp.where(odd, high, low)
-    return near.reshape(rows, -1), far.reshape(rows, -1)
+    far = jnp.moveaxis(far, 0, 3)
+    return near.reshape(rows, -1), far.reshape(rows // 3, -1)
 
 
 def swapped(block, axis, start):
@@ -328,8 +382,11 @@
     odd_i, odd_x = at_i % 2 == 1, at_x % 2 == 1
     matrices = first_matrices(conv_first, odd_x) + second_matrices(conv_second, odd_x)
     arrived, matrices = lax.optimization_barrier((arrived, matrices))
-    volume = stack(arrived, band_weights)
-    one, other = swapped(volume, "inline", 0), swapped(volume, "inline", 1)
+    classes, blocks, steps, band, _ = band_weights.shape
+    weights = band_weights.reshape(classes, blocks, steps * band, band)
+    averaged = stack(arrived)
+    one, other = swapped(averaged, "inline", 0), swapped(averaged, "inline", 1)
+    volume = moved_out(averaged, weights)
     up, down = jnp.where(odd_i, one, other), jnp.where(odd_i, other, one)
     column = jnp.concatenate([up, volume, down], axis=0)
     far = swapped(column, "xline", 1)
@@ -337,7 +394,7 @@
     place = jnp.stack(
         [at_i, at_x, jnp.int32(inline_size * BI), jnp.int32(xline_size * BX)]
     ).astype(jnp.int32)
-    return convolutions(place, column, near, far, matrices)
+    return convolutions(place, weights, column, near, far, matrices)
 
 
 def solution(mesh):

time: 73.7 us -> 72.3 us (0.981)
  waiting for transfers between devices: 32.6 us -> 25.7 us
  Pallas kernels: 13.7 us -> 19 us
    ppermute x4, waiting for transfers between devices: 8.38 us -> 1.18 us  [swapped(): return lax.ppermute(block, axis, pairs + [(j, i) for i, j in pairs])]
    pallas_call x3 -> x4, Pallas kernels: 9.95 us -> 15.3 us  [the longest x1 6.44 us: convolutions(): pl.pallas_call(near_kernel, in_specs=[scalars, pl.BlockSpec(memory_space=...]
    select_n x2 -> x1, local copies, waits for them, and re-layouts: 2.35 us -> 0.61 us  [second_matrices(): near, far = (jnp.where(odd, low, high), jnp.where(odd, high, low))]
    transpose x0 -> x1, local copies, waits for them, and re-layouts: none -> 1.74 us  [second_matrices(): far = jnp.moveaxis(far, 0, 3)]
    reshape x2, local copies, waits for them, and re-layouts: 1.55 us -> 0.28 us  [first_matrices(): return (near.reshape(2 * WIDE, -1), far.reshape(WIDE, -1))]
    transpose x0 -> x1, other arithmetic: none -> 1 us  [second_matrices(): far = jnp.moveaxis(far, 0, 3)]
    select_n x1 -> x0, other arithmetic: 0.99 us -> none  [second_matrices(): near, far = (jnp.where(odd, low, high), jnp.where(odd, high, low))]
    another operation x1, local copies, waits for them, and re-layouts: 0.06 us -> 1.03 us  [first_matrices(): matrix = jnp.stack(placed, axis=0).transpose(0, 5, 1, 3, 2, 4)]
  transfers between devices with their start and end apart: 5 -> 5, of which waited for: 3 -> 3; matrix products, arithmetic and copies ran while one was open for 11% -> 11% of each run, Pallas kernels for 3% -> 14%
where the time goes in v3:
time: 72.3 us; the launch traced here: 72 us
  waiting for transfers between devices  25.7 us (36%)
  starting transfers between devices  19.3 us (27%)
  Pallas kernels  19 us (26%)
  local copies, waits for them, and re-layouts  5.45 us (8%)
  other arithmetic  2.31 us (3%)
    all_to_all x1, waiting for transfers between devices, per_device(): lax.all_to_all(outgoing.reshape(devices, 2 * CAP, width), ALL, split_axis...  24.5 us
    all_to_all x1, starting transfers between devices, per_device(): lax.all_to_all(outgoing.reshape(devices, 2 * CAP, width), ALL, split_axis...  10.8 us
    ppermute x4, starting transfers between devices, swapped(): return lax.ppermute(block, axis, pairs + [(j, i) for i, j in pairs])  8.41 us
    pallas_call x1, Pallas kernels, convolutions(): pl.pallas_call(near_kernel, in_specs=[scalars, pl.BlockSpec(memory_space=...  6.44 us
    pallas_call x1, Pallas kernels, convolutions(): pl.pallas_call(far_kernel, in_specs=[scalars] + [whole] * 6, out_specs=wh...  4.49 us
    pallas_call x1, Pallas kernels, moved_out(): pl.pallas_call(band_kernel, in_specs=[whole, pl.BlockSpec(memory_space=pl...  3.77 us
    pallas_call x1, Pallas kernels, pack(): pl.pallas_call(pack_kernel, in_specs=[kept] * 4, out_specs=kept, out_shap...  3.7 us
    transpose x1, local copies, waits for them, and re-layouts, second_matrices(): far = jnp.moveaxis(far, 0, 3)  1.74 us
  transfers between devices with their start and end apart: 5, of which 3 were waited for; matrix products, arithmetic and copies ran while one was open for 11% of the time, Pallas kernels for 14%

profile of v3, /device:TPU:3, one launch (start us, length us, event | category | flops | bytes accessed | tf_op | source)
XLA Modules:
  0.0 72.0 jit_solution(8702157210234481199)
XLA Ops:
  0.0 3.7 %pack.1 = bf16[1024,1152]{1,0:T(8,128)(2,1)} custom-call(s32[1,256]{1,0:T(1,128)} %bitcast.48, s32[1,256]{1,0:T(1,128)} %bitcast.49, s32[1,256]{1,0:T(1,128)} %bitcast.50, bf16[256,2048]{1,0:T(8,128)(2,1)} %traces_ref.1), custom_call_target="tpu_custom_call" | custom-call | tf_op jit(solution)/shard_map/pack/pallas_call | solution.py:97
  3.7 10.8 %all-to-all-start = ((bf16[128,8,1152]{2,1,0:T(8,128)(2,1)}), bf16[128,8,1152]{2,1,0:T(8,128)(2,1)S(1)}, u32[]{:S(2)}, u32[]{:S(2)}) async-start(bf16[128,8,1152]{2,1,0:T(8,128)(2,1)} %bitcast.45), calls=%async_computation | async-start | bytes 4718592 | tf_op jit(solution)/shard_map/all_to_all | solution.py:379
  14.6 0.3 pad_bitcast_fusion.3
  14.9 0.3 maximum_bitcast_fusion.1
  15.2 0.4 maximum_bitcast_fusion
  15.6 1.0 %select_bitcast_fusion = (bf16[32,2,2,3,4,2,32]{6,0,3,5,4,2,1:T(8,128)(2,1)}, bf16[3,32,2,2,4,2,32]{6,1,0,5,4,3,2:T(8,128)(2,1)S(1)}) fusion(pred[]{:T(512)S(6)} %eq.10, bf16[3,32,2,2,4,4,32]{6,1,0,5,4,3,2:T(8,128)(2,1)S(1)} %maximum_bitcast_fusion), kind=kLoop, calls=%fused_computation.3 | loop fusion | flops 196608 | bytes 786433 | tf_op jit(solution)/shard_map/transpose | solution.py:355
  16.6 0.6 copy.14
  17.2 0.5 reshape.38.second_ref
  17.7 1.7 %copy.15 = bf16[32,2,2,3,4,2,32]{6,5,4,3,2,1,0:T(2,128)(2,1)S(1)} copy(bf16[32,2,2,3,4,2,32]{6,0,3,5,4,2,1:T(8,128)(2,1)} %get-tuple-element.21) | data formatting | bytes 393216 | tf_op jit(solution)/shard_map/transpose | solution.py:355
  19.5 0.5 reshape.39.second_ref
  19.9 1.0 %pad_bitcast_fusion.7 = (bf16[1,3,6,3,8,32]{5,4,3,2,1,0:T(8,128)(2,1)S(1)}, bf16[1,3,6,3,8,32]{5,4,3,2,1,0:T(8,128)(2,1)S(1)}, bf16[1,3,6,3,8,32]{5,4,3,2,1,0:T(8,128)(2,1)S(1)}, bf16[1,3,6,3,8,32]{5,4,3,2,1,0:T(8,128)(2,1)S(1)}) fusion(bf16[3,3,3,8,32]{4,3,2,1,0:T(8,128)(2,1)} %bitcast.47), kind=kLoop, calls=%fused_computation.26 | loop fusion | bytes 124416 | tf_op jit(solution)/shard_map/stack | solution.py:330
  21.0 0.1 maximum_bitcast_fusion.3
  21.2 0.1 fusion.3
  21.2 0.2 fusion.1
  21.5 0.1 pad_maximum_fusion.2
  21.6 0.2 copy.12
  21.8 0.2 reshape.36
  22.0 0.1 reshape.37
  22.1 24.5 %all-to-all-done = bf16[128,8,1152]{2,1,0:T(8,128)(2,1)S(1)} async-done(((bf16[128,8,1152]{2,1,0:T(8,128)(2,1)}), bf16[128,8,1152]{2,1,0:T(8,128)(2,1)S(1)}, u32[]{:S(2)}, u32[]{:S(2)}) %all-to-all-start) | async-done | bytes 2359328 | tf_op jit(solution)/shard_map/all_to_all | solution.py:379
  46.6 0.6 stack.69.averaged_ref
  47.2 0.6 collective-permute-start
  47.8 3.0 %collective-permute-start.1 = (bf16[32,2048]{1,0:T(8,128)(2,1)S(1)}, bf16[32,2048]{1,0:T(8,128)(2,1)S(1)}, u32[]{:S(2)}, u32[]{:S(2)}) collective-permute-start(bf16[32,2048]{1,0:T(8,128)(2,1)S(1)} %stack.69.averaged_ref), channel_id=1, source_target_pairs={{8,16},{24,32},{40,48},{56,64},{72,80},{88,96},{104,112},{16,8},{3... | collective-permute-start | bytes 393224 | tf_op jit(solution)/shard_map/ppermute | solution.py:362
  50.9 3.8 %band.1 = bf16[32,2048]{1,0:T(8,128)(2,1)S(1)} custom-call(bf16[32,2048]{1,0:T(8,128)(2,1)S(1)} %stack.69.averaged_ref, bf16[8,16,256,128]{3,2,1,0:T(8,128)(2,1)} %bitcast.43), custom_call_target="tpu_custom_call" | custom-call | tf_op jit(solution)/shard_map/band/pallas_call | solution.py:177
  54.7 1.0 %collective-permute-done.1 = bf16[32,2048]{1,0:T(8,128)(2,1)S(1)} collective-permute-done((bf16[32,2048]{1,0:T(8,128)(2,1)S(1)}, bf16[32,2048]{1,0:T(8,128)(2,1)S(1)}, u32[]{:S(2)}, u32[]{:S(2)}) %collective-permute-start.1) | collective-permute-done | bytes 131104 | tf_op jit(solution)/shard_map/ppermute | solution.py:362
  55.7 2.7 %collective-permute-start.2 = (bf16[96,2048]{1,0:T(8,128)(2,1)S(1)}, bf16[96,2048]{1,0:T(8,128)(2,1)S(1)}, u32[]{:S(2)}, u32[]{:S(2)}) collective-permute-start(bf16[96,2048]{1,0:T(8,128)(2,1)S(1)} %pad_maximum_fusion.1.mid_ref), channel_id=1, source_target_pairs={{0,1},{2,3},{4,5},{6,7},{1,0},{3,2},{5,4},{7,6},{8,9},{10,11},{12,... | collective-permute-start | bytes 1179656 | tf_op jit(solution)/shard_map/ppermute | solution.py:362
  58.4 2.1 %collective-permute-start.3 = (bf16[96,2048]{1,0:T(8,128)(2,1)S(1)}, bf16[96,2048]{1,0:T(8,128)(2,1)S(1)}, u32[]{:S(2)}, u32[]{:S(2)}) collective-permute-start(bf16[96,2048]{1,0:T(8,128)(2,1)S(1)} %pad_maximum_fusion.1.mid_ref), channel_id=1, source_target_pairs={{1,2},{3,4},{5,6},{2,1},{4,3},{6,5},{9,10},{11,12},{13,14},{10,9},... | collective-permute-start | bytes 1179656 | tf_op jit(solution)/shard_map/ppermute | solution.py:362
  60.5 0.1 pad_add_fusion.place_ref
  60.6 0.1 copy.16.first_ref
  60.7 0.1 copy.17.first_ref
  60.8 6.4 %near.1 = (f32[256,2048]{1,0:T(8,128)S(1)}, f32[128,2048]{1,0:T(8,128)S(1)}, bf16[8,16,256,128]{3,2,1,0:T(8,128)(2,1)S(1)}) custom-call(s32[4]{0:T(128)S(1)} %pad_add_fusion.place_ref, bf16[8,16,256,128]{3,2,1,0:T(8,128)(2,1)} %bitcast.44, bf16[96,2048]{1,0:T(8,128)(2,1)S(1)} %pad_maximum_fusion.1.mid_ref, ...), custom_call_target="tpu_custom_call" | custom-call | tf_op jit(solution)/shard_map/near/pallas_call | solution.py:290
  67.3 0.2 collective-permute-done.3.far_ref
  67.5 4.5 %far.1 = bf16[32,2,2,2048]{3,2,1,0:T(2,128)(2,1)} custom-call(s32[4]{0:T(128)S(1)} %pad_add_fusion.place_ref, bf16[8,16,256,128]{3,2,1,0:T(8,128)(2,1)S(1)} %get-tuple-element.16.weights, bf16[96,2048]{1,0:T(8,128)(2,1)S(1)} %collective-permute-done.3.far_ref, f32[256,2048]{1,0:T(8,128)S(1)} %get-tuple-element.17.partial_ref, ...), custom_call_target="tpu_custom_call" | custom-call | tf_op jit(solution)/shard_map/far/pallas_call | solution.py:309
  (10 shorter events, 0.2 us)
Async XLA Ops:
  3.7 10.9 %copy-start = (bf16[32,32,3,3,3]{1,0,4,3,2:T(8,128)(2,1)S(1)}, bf16[32,32,3,3,3]{1,0,4,3,2:T(8,128)(2,1)}, u32[]{:S(2)}) copy-start(bf16[32,32,3,3,3]{1,0,4,3,2:T(8,128)(2,1)} %param.13) | copy-start | bytes 165892
  3.7 42.9 %all-to-all-start = ((bf16[128,8,1152]{2,1,0:T(8,128)(2,1)}), bf16[128,8,1152]{2,1,0:T(8,128)(2,1)S(1)}, u32[]{:S(2)}, u32[]{:S(2)}) async-start(bf16[128,8,1152]{2,1,0:T(8,128)(2,1)} %bitcast.45), calls=%async_computation | async-start | bytes 4718592 | tf_op jit(solution)/shard_map/all_to_all | solution.py:379
  47.2 7.4 %collective-permute-start = (bf16[32,2048]{1,0:T(8,128)(2,1)S(1)}, bf16[32,2048]{1,0:T(8,128)(2,1)S(1)}, u32[]{:S(2)}, u32[]{:S(2)}) collective-permute-start(bf16[32,2048]{1,0:T(8,128)(2,1)S(1)} %stack.69.averaged_ref), channel_id=1, source_target_pairs={{0,8},{16,24},{32,40},{48,56},{64,72},{80,88},{96,104},{112,120},{... | collective-permute-start | bytes 393224 | tf_op jit(solution)/shard_map/ppermute | solution.py:362
  47.8 7.8 %collective-permute-start.1 = (bf16[32,2048]{1,0:T(8,128)(2,1)S(1)}, bf16[32,2048]{1,0:T(8,128)(2,1)S(1)}, u32[]{:S(2)}, u32[]{:S(2)}) collective-permute-start(bf16[32,2048]{1,0:T(8,128)(2,1)S(1)} %stack.69.averaged_ref), channel_id=1, source_target_pairs={{8,16},{24,32},{40,48},{56,64},{72,80},{88,96},{104,112},{16,8},{3... | collective-permute-start | bytes 393224 | tf_op jit(solution)/shard_map/ppermute | solution.py:362
  55.7 5.1 %collective-permute-start.2 = (bf16[96,2048]{1,0:T(8,128)(2,1)S(1)}, bf16[96,2048]{1,0:T(8,128)(2,1)S(1)}, u32[]{:S(2)}, u32[]{:S(2)}) collective-permute-start(bf16[96,2048]{1,0:T(8,128)(2,1)S(1)} %pad_maximum_fusion.1.mid_ref), channel_id=1, source_target_pairs={{0,1},{2,3},{4,5},{6,7},{1,0},{3,2},{5,4},{7,6},{8,9},{10,11},{12,... | collective-permute-start | bytes 1179656 | tf_op jit(solution)/shard_map/ppermute | solution.py:362
  58.4 9.1 %collective-permute-start.3 = (bf16[96,2048]{1,0:T(8,128)(2,1)S(1)}, bf16[96,2048]{1,0:T(8,128)(2,1)S(1)}, u32[]{:S(2)}, u32[]{:S(2)}) collective-permute-start(bf16[96,2048]{1,0:T(8,128)(2,1)S(1)} %pad_maximum_fusion.1.mid_ref), channel_id=1, source_target_pairs={{1,2},{3,4},{5,6},{2,1},{4,3},{6,5},{9,10},{11,12},{13,14},{10,9},... | collective-permute-start | bytes 1179656 | tf_op jit(solution)/shard_map/ppermute | solution.py:362

commit v4 on v3

--- a/solution.py
+++ b/solution.py
@@ -134,41 +134,42 @@
     )(arrived)
 
 
-BAND_PARTS = 8
-
-
-def band_loads(source_ref, weights, sem):
-    each = weights.shape[1] // BAND_PARTS
-    loads = []
-    for part in range(BAND_PARTS):
-        blocks = pl.ds(part * each, each)
-        loads.append(pltpu.make_async_copy(source_ref.at[:, blocks], weights.at[:, blocks], sem.at[part]))
-        loads[-1].start()
+def band_loads(source_ref, weights, sem, sizes):
+    loads, first = {}, 0
+    for number, size in enumerate(sizes):
+        blocks = pl.ds(first, size)
+        loads[first] = pltpu.make_async_copy(source_ref.at[:, blocks], weights.at[:, blocks], sem.at[number])
+        loads[first].start()
+        first += size
     return loads
 
 
-def move_out(averaged, weights, out, loads=None):
-    rows = averaged.shape[0]
-    classes, blocks, _, band = weights.shape
-    kind = iota((rows, band), 0) % classes
-    for block in range(blocks):
-        if loads is not None and block % (blocks // BAND_PARTS) == 0:
-            loads[block // (blocks // BAND_PARTS)].wait()
-        start = block * band
-        wide = jnp.concatenate([weights[number, block] for number in range(classes)], axis=1)
-        moved = nn(averaged[:, start : start + 2 * band], wide)
-        total = moved[:, :band]
-        for number in range(1, classes):
-            total = jnp.where(kind == number, moved[:, number * band : (number + 1) * band], total)
-        out[:, start : start + band] = total.astype(BF)
+def moved_block(averaged, weights, block, loads):
+    if block in loads:
+        loads[block].wait()
+    classes, _, _, band = weights.shape
+    start = block * band
+    wide = jnp.concatenate([weights[number, block] for number in range(classes)], axis=1)
+    moved = nn(averaged[:, start : start + 2 * band], wide)
+    kind = iota((averaged.shape[0], band), 0) % classes
+    total = moved[:, :band]
+    for number in range(1, classes):
+        total = jnp.where(kind == number, moved[:, number * band : (number + 1) * band], total)
+    return total.astype(BF)
+
+
+BAND_SIZES = (2, 2, 2, 2, 2, 2, 2, 2)
+NEAR_SIZES = (2, 2, 2, 2, 2, 2, 2, 2)
 
 
 def band_kernel(averaged_ref, band_ref, out_ref, weights, padded, sem):
-    loads = band_loads(band_ref, weights, sem)
+    loads = band_loads(band_ref, weights, sem, BAND_SIZES)
     rows, samples = averaged_ref.shape
+    band = weights.shape[3]
     padded[:, :samples] = averaged_ref[...]
-    padded[:, samples:] = jnp.zeros((rows, padded.shape[1] - samples), BF)
-    move_out(padded, weights, out_ref, loads)
+    padded[:, samples:] = jnp.zeros((rows, band), BF)
+    for block in range(weights.shape[1]):
+        out_ref[:, block * band : (block + 1) * band] = moved_block(padded, weights, block, loads)
 
 
 def moved_out(averaged, weights):
@@ -182,101 +183,137 @@
         scratch_shapes=[
             pltpu.VMEM(weights.shape, BF),
             pltpu.VMEM((rows, samples + weights.shape[3]), BF),
-            pltpu.SemaphoreType.DMA((BAND_PARTS,)),
+            pltpu.SemaphoreType.DMA((len(BAND_SIZES),)),
         ],
         compiler_params=pltpu.CompilerParams(vmem_limit_bytes=16 << 20),
         name="band",
     )(averaged, pltpu.with_memory_space_constraint(weights, pltpu.HBM))
 
 
-def later(value):
-    rolled = pltpu.roll(value, 1, 1)
-    return jnp.where(iota(value.shape, 1) == 0, jnp.zeros_like(rolled), rolled)
-
-
-def sooner(value):
-    samples = value.shape[1]
-    rolled = pltpu.roll(value, samples - 1, 1)
-    return jnp.where(iota(value.shape, 1) == samples - 1, jnp.zeros_like(rolled), rolled)
-
-
-def fill(taps, columns, weights, padded, moved, loads=None):
-    tall = BX * CLASSES
-    group = 3 * len(columns) * tall
-    samples = moved.shape[1]
-
-    def place(value, first_line, which):
-        for tap, shifted in enumerate((later(value), value, sooner(value))):
-            for line in range(BI):
-                at = (first_line + line) * group + (tap * len(columns) + which) * tall
-                taps[at : at + tall, :] = shifted[line * tall : (line + 1) * tall]
-
-    padded[:, samples:] = jnp.zeros((padded.shape[0], padded.shape[1] - samples), BF)
+TILE = 2048
+WIDE = BX * CH
+EDGE = 128
+ALL_LINES = BI + 4
+TALL = BX * CLASSES
+
+
+def taps_of(padded, rows, start):
+    window = padded[rows, start : start + TILE + 2 * EDGE]
+    inner = slice(EDGE, EDGE + TILE)
+    width = window.shape[1]
+    return pltpu.roll(window, 1, 1)[:, inner], window[:, inner], pltpu.roll(window, width - 1, 1)[:, inner]
+
+
+def clear_edges(padded):
+    zeros = jnp.zeros((padded.shape[0], EDGE), BF)
+    padded[:, :EDGE] = zeros
+    padded[:, padded.shape[1] - EDGE :] = zeros
+
+
+def inside(place_ref, start_x, line):
+    bin_x = iota((WIDE, 1), 0) // CH + start_x + place_ref[1] * BX - 1
+    bin_i = line + place_ref[0] * BI - 1
+    return (bin_x >= 0) & (bin_x < place_ref[3]) & (bin_i >= 0) & (bin_i < place_ref[2])
+
+
+def run_tiles(
+    columns, weights, loads, first, second, keeps, split, store, averaged, volume, taps, hidden
+):
+    samples = volume.shape[1] - 2 * EDGE
+    _, blocks, _, band = weights.shape
+    count = len(columns)
+    group = 3 * count * TALL
+    clear_edges(volume)
+    clear_edges(hidden)
+    averaged[:, samples:] = jnp.zeros((averaged.shape[0], averaged.shape[1] - samples), BF)
     for which, column in enumerate(columns):
         at = 2 * which * CELLS
-        padded[at : at + CELLS, :samples] = column[:CELLS, :]
-        padded[at + CELLS : at + 2 * CELLS, :samples] = column[2 * CELLS :, :]
-        place(column[CELLS : 2 * CELLS, :], BI, which)
-    move_out(padded, weights, moved, loads)
-    for which in range(len(columns)):
-        at = 2 * which * CELLS
-        place(moved[at : at + CELLS, :], 0, which)
-        place(moved[at + CELLS : at + 2 * CELLS, :], 2 * BI, which)
-    return group
-
-
-def inside(place_ref, start_x, line):
-    bin_x = iota((BX * CH, 1), 0) // CH + start_x + place_ref[1] * BX - 1
-    bin_i = line + place_ref[0] * BI - 1
-    return (bin_x >= 0) & (bin_x < place_ref[3]) & (bin_i >= 0) & (bin_i < place_ref[2])
-
-
-def joined(value):
-    rows = value.shape[0] // 3
-    return value[rows : 2 * rows] + later(value[:rows]) + sooner(value[2 * rows :])
-
-
-TILE = 512
-WIDE = BX * CH
+        averaged[at : at + CELLS, :samples] = column[:CELLS, :]
+        averaged[at + CELLS : at + 2 * CELLS, :samples] = column[2 * CELLS : 3 * CELLS, :]
+        at = (3 * which + 1) * CELLS
+        volume[at : at + CELLS, EDGE : EDGE + samples] = column[CELLS : 2 * CELLS, :]
+
+    def move_out(block):
+        total = moved_block(averaged, weights, block, loads)
+        start = block * band
+        lanes = slice(EDGE + start, EDGE + start + band)
+        for which in range(count):
+            volume[3 * which * CELLS : (3 * which + 1) * CELLS, lanes] = total[
+                2 * which * CELLS : (2 * which + 1) * CELLS
+            ]
+            volume[(3 * which + 2) * CELLS : (3 * which + 3) * CELLS, lanes] = total[
+                (2 * which + 1) * CELLS : (2 * which + 2) * CELLS
+            ]
+
+    def first_convolution(start):
+        lanes = slice(start, start + TILE)
+        for which in range(count):
+            rows = slice(3 * which * CELLS, 3 * (which + 1) * CELLS)
+            for tap, value in enumerate(taps_of(volume, rows, start)):
+                for line in range(ALL_LINES):
+                    at = line * group + (tap * count + which) * TALL
+                    taps[at : at + TALL, lanes] = value[line * TALL : (line + 1) * TALL]
+        for line in range(BI + 2):
+            rows = slice(line * WIDE, (line + 1) * WIDE)
+            value = split(nn(first, taps[line * group : (line + 3) * group, lanes]), rows, lanes)
+            value = jnp.where(keeps[line], jax.nn.gelu(value), 0.0).astype(BF)
+            hidden[rows, EDGE + start : EDGE + start + TILE] = value
+
+    def second_convolution(start):
+        held = jnp.concatenate(taps_of(hidden, slice(None), start), axis=0)
+        store(nn(second, held), slice(start, start + TILE))
+
+    done = 0
+    for start in range(0, samples, TILE):
+        ready = min((start + TILE) // band + 1, blocks)
+        for block in range(done, ready):
+            move_out(block)
+        done = ready
+        first_convolution(start)
+        if start:
+            second_convolution(start - TILE)
+    second_convolution(samples - TILE)
 
 
 def near_kernel(
     place_ref, band_ref, mid_ref, near_ref, first_ref, second_ref,
-    partial_ref, sum_ref, weights, taps, hidden, padded, moved, sem,
+    partial_ref, sum_ref, weights, averaged, volume, taps, hidden, sem,
 ):
-    samples = taps.shape[1]
-    loads = band_loads(band_ref, weights, sem)
-    group = fill(taps, (mid_ref, near_ref), weights, padded, moved, loads)
+    loads = band_loads(band_ref, weights, sem, NEAR_SIZES)
     start_x = jnp.where(place_ref[1] % 2 == 0, BX, 0)
-    first = first_ref[...]
-    for line in range(BI + 2):
-        keep = inside(place_ref, start_x, line)
-        rows = slice(line * WIDE, (line + 1) * WIDE)
-        for start in range(0, samples, TILE):
-            lanes = slice(start, start + TILE)
-            both = nn(first, taps[line * group : (line + 3) * group, lanes])
-            hidden[rows, lanes] = jnp.where(keep, jax.nn.gelu(both[:WIDE]), 0.0).astype(BF)
-            partial_ref[rows, lanes] = both[WIDE:]
-    sum_ref[...] = joined(nn(second_ref[...], hidden[...]))
+    keeps = [inside(place_ref, start_x, line) for line in range(BI + 2)]
+
+    def split(both, rows, lanes):
+        partial_ref[rows, lanes] = both[WIDE:]
+        return both[:WIDE]
+
+    def store(value, lanes):
+        sum_ref[:, lanes] = value
+
+    run_tiles(
+        (mid_ref, near_ref), weights, loads, first_ref[...], second_ref[...], keeps, split, store,
+        averaged, volume, taps, hidden,
+    )
 
 
 def far_kernel(
-    place_ref, weights, far_ref, partial_ref, sum_ref, first_ref, second_ref, out_ref, taps, hidden, padded, moved
+    place_ref, weights, far_ref, partial_ref, sum_ref, first_ref, second_ref, out_ref,
+    averaged, volume, taps, hidden,
 ):
-    samples = taps.shape[1]
-    group = fill(taps, (far_ref,), weights, padded, moved)
     start_x = jnp.where(place_ref[1] % 2 == 0, 0, BX)
-    first = first_ref[...]
-    for line in range(BI + 2):
-        keep = inside(place_ref, start_x, line)
-        rows = slice(line * WIDE, (line + 1) * WIDE)
-        for start in range(0, samples, TILE):
-            lanes = slice(start, start + TILE)
-            value = nn(first, taps[line * group : (line + 3) * group, lanes]) + partial_ref[rows, lanes]
-            hidden[rows, lanes] = jnp.where(keep, jax.nn.gelu(value), 0.0).astype(BF)
-    held = hidden[...]
-    total = nn(second_ref[...], jnp.concatenate([later(held), held, sooner(held)], axis=0)) + sum_ref[...]
-    out_ref[...] = total.astype(BF).reshape(out_ref.shape)
+    keeps = [inside(place_ref, start_x, line) for line in range(BI + 2)]
+
+    def split(value, rows, lanes):
+        return value + partial_ref[rows, lanes]
+
+    def store(value, lanes):
+        total = (value + sum_ref[:, lanes]).astype(BF)
+        out_ref[:, :, :, lanes] = total.reshape(out_ref.shape[:3] + (TILE,))
+
+    run_tiles(
+        (far_ref,), weights, {}, first_ref[...], second_ref[...], keeps, split, store,
+        averaged, volume, taps, hidden,
+    )
 
 
 def convolutions(place, weights, mid, near, far, matrices):
@@ -284,9 +321,16 @@
     first_near, first_far, second_near, second_far = matrices
     whole = pl.BlockSpec(memory_space=pltpu.VMEM)
     scalars = pl.BlockSpec(memory_space=pltpu.SMEM)
-    tall = (BI + 4) * 3 * BX * CLASSES
     bins = (BI + 2) * WIDE
-    longer = samples + weights.shape[3]
+
+    def buffers(count):
+        return [
+            pltpu.VMEM((2 * count * CELLS, samples + weights.shape[3]), BF),
+            pltpu.VMEM((3 * count * CELLS, samples + 2 * EDGE), BF),
+            pltpu.VMEM((3 * count * ALL_LINES * TALL, samples), BF),
+            pltpu.VMEM((bins, samples + 2 * EDGE), BF),
+        ]
+
     partial, total, held = pl.pallas_call(
         near_kernel,
         in_specs=[scalars, pl.BlockSpec(memory_space=pltpu.HBM)] + [whole] * 4,
@@ -296,14 +340,9 @@
             jax.ShapeDtypeStruct((CH * BI * BX, samples), F32),
             jax.ShapeDtypeStruct(weights.shape, BF),
         ),
-        scratch_shapes=[
-            pltpu.VMEM((2 * tall, samples), BF),
-            pltpu.VMEM((bins, samples), BF),
-            pltpu.VMEM((4 * CELLS, longer), BF),
-            pltpu.VMEM((4 * CELLS, samples), BF),
-            pltpu.SemaphoreType.DMA((BAND_PARTS,)),
-        ],
+        scratch_shapes=buffers(2) + [pltpu.SemaphoreType.DMA((len(NEAR_SIZES),))],
         compiler_params=pltpu.CompilerParams(vmem_limit_bytes=24 << 20),
+        cost_estimate=pl.CostEstimate(flops=0, bytes_accessed=0, transcendentals=0),
         name="near",
     )(place, pltpu.with_memory_space_constraint(weights, pltpu.HBM), mid, near, first_near, second_near)
     return pl.pallas_call(
@@ -311,12 +350,7 @@
         in_specs=[scalars] + [whole] * 6,
         out_specs=whole,
         out_shape=jax.ShapeDtypeStruct((CH, BI, BX, samples), BF),
-        scratch_shapes=[
-            pltpu.VMEM((tall, samples), BF),
-            pltpu.VMEM((bins, samples), BF),
-            pltpu.VMEM((2 * CELLS, longer), BF),
-            pltpu.VMEM((2 * CELLS, samples), BF),
-        ],
+        scratch_shapes=buffers(1),
         compiler_params=pltpu.CompilerParams(vmem_limit_bytes=24 << 20),
         name="far",
     )(place, held, far, partial, total, first_far, second_far)
@@ -350,10 +384,9 @@
     matrix = jnp.stack([jnp.stack(line, axis=0) for line in placed], axis=0)
     matrix = matrix.transpose(4, 5, 0, 1, 2, 3, 6)
     low, high = matrix[..., :BX, :], matrix[..., BX:, :]
-    rows = 3 * CH * BI * BX
+    rows = CH * BI * BX
     near, far = jnp.where(odd, low, high), jnp.where(odd, high, low)
-    far = jnp.moveaxis(far, 0, 3)
-    return near.reshape(rows, -1), far.reshape(rows // 3, -1)
+    return tuple(jnp.moveaxis(side, 0, 3).reshape(rows, -1) for side in (near, far))
 
 
 def swapped(block, axis, start):
@@ -389,7 +422,8 @@
     volume = moved_out(averaged, weights)
     up, down = jnp.where(odd_i, one, other), jnp.where(odd_i, other, one)
     column = jnp.concatenate([up, volume, down], axis=0)
-    far = swapped(column, "xline", 1)
+    sent = jnp.concatenate([up, volume, down, up[:16]], axis=0)
+    far = swapped(sent, "xline", 1)
     near = swapped(column, "xline", 0)
     place = jnp.stack(
         [at_i, at_x, jnp.int32(inline_size * BI), jnp.int32(xline_size * BX)]

time: 72.3 us -> 71.5 us (0.989)
  starting transfers between devices: 19.3 us -> 18 us
    reshape x2, local copies, waits for them, and re-layouts: 0.28 us -> 1.55 us  [first_matrices(): return (near.reshape(2 * WIDE, -1), far.reshape(WIDE, -1))]
    ppermute x4, starting transfers between devices: 8.41 us -> 7.2 us  [swapped(): return lax.ppermute(block, axis, pairs + [(j, i) for i, j in pairs])]
    another operation x1, local copies, waits for them, and re-layouts: 1.03 us -> 0.06 us  [first_matrices(): matrix = jnp.stack(placed, axis=0).transpose(0, 5, 1, 3, 2, 4)]
    ppermute x4, waiting for transfers between devices: 1.18 us -> 1.97 us  [swapped(): return lax.ppermute(block, axis, pairs + [(j, i) for i, j in pairs])]
    transpose x1 -> x2, local copies, waits for them, and re-layouts: 1.74 us -> 2.35 us  [second_matrices(): jnp.moveaxis(side, 0, 3).reshape(rows, -1)]
where the time goes in v4:
time: 71.5 us; the launch traced here: 71.1 us
  waiting for transfers between devices  26.2 us (37%)
  Pallas kernels  18.5 us (26%)
  starting transfers between devices  18 us (25%)
  local copies, waits for them, and re-layouts  5.72 us (8%)
  other arithmetic  2.33 us (3%)
    all_to_all x1, waiting for transfers between devices, per_device(): lax.all_to_all(outgoing.reshape(devices, 2 * CAP, width), ALL, split_axis...  24.3 us
    all_to_all x1, starting transfers between devices, per_device(): lax.all_to_all(outgoing.reshape(devices, 2 * CAP, width), ALL, split_axis...  10.8 us
    ppermute x4, starting transfers between devices, swapped(): return lax.ppermute(block, axis, pairs + [(j, i) for i, j in pairs])  7.2 us
    pallas_call x1, Pallas kernels, convolutions(): pl.pallas_call(near_kernel, in_specs=[scalars, pl.BlockSpec(memory_space=...  6.04 us
    pallas_call x1, Pallas kernels, convolutions(): pl.pallas_call(far_kernel, in_specs=[scalars] + [whole] * 6, out_specs=wh...  4.42 us
    pallas_call x1, Pallas kernels, moved_out(): pl.pallas_call(band_kernel, in_specs=[whole, pl.BlockSpec(memory_space=pl...  3.77 us
    pallas_call x1, Pallas kernels, pack(): pl.pallas_call(pack_kernel, in_specs=[kept] * 4, out_specs=kept, out_shap...  3.69 us
    transpose x2, local copies, waits for them, and re-layouts, second_matrices(): jnp.moveaxis(side, 0, 3).reshape(rows, -1)  2.35 us
  transfers between devices with their start and end apart: 5, of which 3 were waited for; matrix products, arithmetic and copies ran while one was open for 11% of the time, Pallas kernels for 14%

profile of v4, /device:TPU:3, one launch (start us, length us, event | category | flops | bytes accessed | tf_op | source)
XLA Modules:
  0.0 71.1 jit_solution(12314848484238815167)
XLA Ops:
  0.0 3.7 %pack.1 = bf16[1024,1152]{1,0:T(8,128)(2,1)} custom-call(s32[1,256]{1,0:T(1,128)} %bitcast.50, s32[1,256]{1,0:T(1,128)} %bitcast.51, s32[1,256]{1,0:T(1,128)} %bitcast.52, bf16[256,2048]{1,0:T(8,128)(2,1)} %traces_ref.1), custom_call_target="tpu_custom_call" | custom-call | tf_op jit(solution)/shard_map/pack/pallas_call | solution.py:97
  3.7 10.8 %all-to-all-start = ((bf16[128,8,1152]{2,1,0:T(8,128)(2,1)}), bf16[128,8,1152]{2,1,0:T(8,128)(2,1)S(1)}, u32[]{:S(2)}, u32[]{:S(2)}) async-start(bf16[128,8,1152]{2,1,0:T(8,128)(2,1)} %bitcast.47), calls=%async_computation | async-start | bytes 4718592 | tf_op jit(solution)/shard_map/all_to_all | solution.py:412
  14.6 0.1 pad_bitcast_fusion.7
  14.7 0.1 maximum_bitcast_fusion.3
  14.8 0.1 fusion.3
  14.9 0.2 fusion.1
  15.2 0.1 pad_maximum_fusion.3
  15.3 0.2 copy.12
  15.5 0.8 %reshape.36 = bf16[128,288]{0,1:T(8,128)(2,1)} reshape(bf16[4,32,3,3,4,8]{1,0,5,4,3,2:T(4,128)(2,1)S(1)} %copy.12) | data formatting | bytes 147456 | tf_op jit(solution)/shard_map/reshape | solution.py:372
  16.3 0.7 %reshape.37 = bf16[64,144]{0,1:T(8,128)(2,1)} reshape(bf16[2,32,3,3,2,8]{1,0,5,4,3,2:T(2,128)(2,1)S(1)} %copy.13) | data formatting | bytes 36864 | tf_op jit(solution)/shard_map/reshape | solution.py:372
  17.1 0.3 pad_bitcast_fusion.3
  17.3 0.3 maximum_bitcast_fusion.1
  17.7 0.4 maximum_bitcast_fusion
  18.0 1.0 %select_bitcast_fusion = (bf16[32,2,2,3,4,2,32]{6,0,3,5,4,2,1:T(8,128)(2,1)}, bf16[32,2,2,3,4,2,32]{6,0,3,5,4,2,1:T(8,128)(2,1)S(1)}) fusion(pred[]{:T(512)S(6)} %eq.10, bf16[3,32,2,2,4,4,32]{6,1,0,5,4,3,2:T(8,128)(2,1)S(1)} %maximum_bitcast_fusion), kind=kLoop, calls=%fused_computation.3 | loop fusion | flops 196608 | bytes 786433 | tf_op jit(solution)/shard_map/transpose | solution.py:389
  19.0 0.6 copy.14
  19.6 0.5 reshape.38.second_ref
  20.1 1.7 %copy.15 = bf16[32,2,2,3,4,2,32]{6,5,4,3,2,1,0:T(2,128)(2,1)S(1)} copy(bf16[32,2,2,3,4,2,32]{6,0,3,5,4,2,1:T(8,128)(2,1)} %get-tuple-element.21) | data formatting | bytes 393216 | tf_op jit(solution)/shard_map/transpose | solution.py:389
  21.9 0.5 reshape.39.second_ref
  22.4 24.3 %all-to-all-done = bf16[128,8,1152]{2,1,0:T(8,128)(2,1)S(1)} async-done(((bf16[128,8,1152]{2,1,0:T(8,128)(2,1)}), bf16[128,8,1152]{2,1,0:T(8,128)(2,1)S(1)}, u32[]{:S(2)}, u32[]{:S(2)}) %all-to-all-start) | async-done | bytes 2359328 | tf_op jit(solution)/shard_map/all_to_all | solution.py:412
  46.6 0.6 stack.69.averaged_ref
  47.2 0.6 collective-permute-start
  47.8 3.0 %collective-permute-start.1 = (bf16[32,2048]{1,0:T(8,128)(2,1)S(1)}, bf16[32,2048]{1,0:T(8,128)(2,1)S(1)}, u32[]{:S(2)}, u32[]{:S(2)}) collective-permute-start(bf16[32,2048]{1,0:T(8,128)(2,1)S(1)} %stack.69.averaged_ref), channel_id=1, source_target_pairs={{8,16},{24,32},{40,48},{56,64},{72,80},{88,96},{104,112},{16,8},{3... | collective-permute-start | bytes 393224 | tf_op jit(solution)/shard_map/ppermute | solution.py:395
  50.9 3.8 %band.1 = bf16[32,2048]{1,0:T(8,128)(2,1)S(1)} custom-call(bf16[32,2048]{1,0:T(8,128)(2,1)S(1)} %stack.69.averaged_ref, bf16[8,16,256,128]{3,2,1,0:T(8,128)(2,1)} %bitcast.45), custom_call_target="tpu_custom_call" | custom-call | tf_op jit(solution)/shard_map/band/pallas_call | solution.py:178
  54.7 0.9 %collective-permute-done.1 = bf16[32,2048]{1,0:T(8,128)(2,1)S(1)} collective-permute-done((bf16[32,2048]{1,0:T(8,128)(2,1)S(1)}, bf16[32,2048]{1,0:T(8,128)(2,1)S(1)}, u32[]{:S(2)}, u32[]{:S(2)}) %collective-permute-start.1) | collective-permute-done | bytes 131104 | tf_op jit(solution)/shard_map/ppermute | solution.py:395
  55.7 2.8 %collective-permute-start.3 = (bf16[112,2048]{1,0:T(8,128)(2,1)S(1)}, bf16[112,2048]{1,0:T(8,128)(2,1)S(1)}, u32[]{:S(2)}, u32[]{:S(2)}) collective-permute-start(bf16[112,2048]{1,0:T(8,128)(2,1)S(1)} %pad_maximum_fusion), channel_id=1, source_target_pairs={{1,2},{3,4},{5,6},{2,1},{4,3},{6,5},{9,10},{11,12},{13,14},{10,9},... | collective-permute-start | bytes 1376264 | tf_op jit(solution)/shard_map/ppermute | solution.py:395
  58.5 0.8 %collective-permute-start.2 = (bf16[96,2048]{1,0:T(8,128)(2,1)S(1)}, bf16[96,2048]{1,0:T(8,128)(2,1)S(1)}, u32[]{:S(2)}, u32[]{:S(2)}) collective-permute-start(bf16[96,2048]{1,0:T(8,128)(2,1)S(1)} %pad_maximum_fusion.2.mid_ref), channel_id=1, source_target_pairs={{0,1},{2,3},{4,5},{6,7},{1,0},{3,2},{5,4},{7,6},{8,9},{10,11},{12,... | collective-permute-start | bytes 1179656 | tf_op jit(solution)/shard_map/ppermute | solution.py:395
  59.3 0.1 pad_add_fusion.place_ref
  59.4 0.1 copy.16.first_ref
  59.5 0.1 copy.17.first_ref
  59.6 1.0 %collective-permute-done.2.near_ref = bf16[96,2048]{1,0:T(8,128)(2,1)S(1)} collective-permute-done((bf16[96,2048]{1,0:T(8,128)(2,1)S(1)}, bf16[96,2048]{1,0:T(8,128)(2,1)S(1)}, u32[]{:S(2)}, u32[]{:S(2)}) %collective-permute-start.2) | collective-permute-done | bytes 393248 | tf_op jit(solution)/shard_map/ppermute | solution.py:395
  60.7 6.0 %near.1 = (f32[256,2048]{1,0:T(8,128)S(1)}, f32[128,2048]{1,0:T(8,128)S(1)}, bf16[8,16,256,128]{3,2,1,0:T(8,128)(2,1)S(1)}) custom-call(s32[4]{0:T(128)S(1)} %pad_add_fusion.place_ref, bf16[8,16,256,128]{3,2,1,0:T(8,128)(2,1)} %bitcast.46, bf16[96,2048]{1,0:T(8,128)(2,1)S(1)} %pad_maximum_fusion.2.mid_ref, ...), custom_call_target="tpu_custom_call" | custom-call | tf_op jit(solution)/shard_map/near/pallas_call | solution.py:334
  66.7 4.4 %far.1 = bf16[32,2,2,2048]{3,2,1,0:T(2,128)(2,1)} custom-call(s32[4]{0:T(128)S(1)} %pad_add_fusion.place_ref, bf16[8,16,256,128]{3,2,1,0:T(8,128)(2,1)S(1)} %get-tuple-element.16.weights, bf16[112,2048]{1,0:T(8,128)(2,1)S(1)} %collective-permute-done.3.far_ref, f32[256,2048]{1,0:T(8,128)S(1)} %get-tuple-element.17.partial_ref, ...), custom_call_target="tpu_custom_call" | custom-call | tf_op jit(solution)/shard_map/far/pallas_call | solution.py:348
  (18 shorter events, 0.3 us)
Async XLA Ops:
  3.7 10.9 %copy-start.3 = (bf16[32,8,3,3,3]{0,1,4,3,2:T(8,128)(2,1)S(1)}, bf16[32,8,3,3,3]{0,1,4,3,2:T(8,128)(2,1)}, u32[]{:S(2)}) copy-start(bf16[32,8,3,3,3]{0,1,4,3,2:T(8,128)(2,1)} %param.12) | copy-start | bytes 41476
  3.7 42.9 %all-to-all-start = ((bf16[128,8,1152]{2,1,0:T(8,128)(2,1)}), bf16[128,8,1152]{2,1,0:T(8,128)(2,1)S(1)}, u32[]{:S(2)}, u32[]{:S(2)}) async-start(bf16[128,8,1152]{2,1,0:T(8,128)(2,1)} %bitcast.47), calls=%async_computation | async-start | bytes 4718592 | tf_op jit(solution)/shard_map/all_to_all | solution.py:412
  14.9 2.2 %copy-start.1 = (bf16[32,32,3,3,3]{1,0,4,3,2:T(8,128)(2,1)S(1)}, bf16[32,32,3,3,3]{1,0,4,3,2:T(8,128)(2,1)}, u32[]{:S(2)}) copy-start(bf16[32,32,3,3,3]{1,0,4,3,2:T(8,128)(2,1)} %param.13) | copy-start | bytes 165892
  47.2 7.5 %collective-permute-start = (bf16[32,2048]{1,0:T(8,128)(2,1)S(1)}, bf16[32,2048]{1,0:T(8,128)(2,1)S(1)}, u32[]{:S(2)}, u32[]{:S(2)}) collective-permute-start(bf16[32,2048]{1,0:T(8,128)(2,1)S(1)} %stack.69.averaged_ref), channel_id=1, source_target_pairs={{0,8},{16,24},{32,40},{48,56},{64,72},{80,88},{96,104},{112,120},{... | collective-permute-start | bytes 393224 | tf_op jit(solution)/shard_map/ppermute | solution.py:395
  47.8 7.8 %collective-permute-start.1 = (bf16[32,2048]{1,0:T(8,128)(2,1)S(1)}, bf16[32,2048]{1,0:T(8,128)(2,1)S(1)}, u32[]{:S(2)}, u32[]{:S(2)}) collective-permute-start(bf16[32,2048]{1,0:T(8,128)(2,1)S(1)} %stack.69.averaged_ref), channel_id=1, source_target_pairs={{8,16},{24,32},{40,48},{56,64},{72,80},{88,96},{104,112},{16,8},{3... | collective-permute-start | bytes 393224 | tf_op jit(solution)/shard_map/ppermute | solution.py:395
  54.7 4.7 %copy-start = (bf16[128,288]{0,1:T(8,128)(2,1)S(1)}, bf16[128,288]{0,1:T(8,128)(2,1)}, u32[]{:S(2)}) copy-start(bf16[128,288]{0,1:T(8,128)(2,1)} %reshape.36) | copy-start | bytes 221188
  54.7 4.8 %copy-start.2 = (bf16[64,144]{0,1:T(8,128)(2,1)S(1)}, bf16[64,144]{0,1:T(8,128)(2,1)}, u32[]{:S(2)}) copy-start(bf16[64,144]{0,1:T(8,128)(2,1)} %reshape.37) | copy-start | bytes 55300
  55.7 11.0 %collective-permute-start.3 = (bf16[112,2048]{1,0:T(8,128)(2,1)S(1)}, bf16[112,2048]{1,0:T(8,128)(2,1)S(1)}, u32[]{:S(2)}, u32[]{:S(2)}) collective-permute-start(bf16[112,2048]{1,0:T(8,128)(2,1)S(1)} %pad_maximum_fusion), channel_id=1, source_target_pairs={{1,2},{3,4},{5,6},{2,1},{4,3},{6,5},{9,10},{11,12},{13,14},{10,9},... | collective-permute-start | bytes 1376264 | tf_op jit(solution)/shard_map/ppermute | solution.py:395
  58.5 2.1 %collective-permute-start.2 = (bf16[96,2048]{1,0:T(8,128)(2,1)S(1)}, bf16[96,2048]{1,0:T(8,128)(2,1)S(1)}, u32[]{:S(2)}, u32[]{:S(2)}) collective-permute-start(bf16[96,2048]{1,0:T(8,128)(2,1)S(1)} %pad_maximum_fusion.2.mid_ref), channel_id=1, source_target_pairs={{0,1},{2,3},{4,5},{6,7},{1,0},{3,2},{5,4},{7,6},{8,9},{10,11},{12,... | collective-permute-start | bytes 1179656 | tf_op jit(solution)/shard_map/ppermute | solution.py:395

commit v5 on v4

--- a/solution.py
+++ b/solution.py
@@ -159,7 +159,6 @@
 
 
 BAND_SIZES = (2, 2, 2, 2, 2, 2, 2, 2)
-NEAR_SIZES = (2, 2, 2, 2, 2, 2, 2, 2)
 
 
 def band_kernel(averaged_ref, band_ref, out_ref, weights, padded, sem):
@@ -178,10 +177,9 @@
     return pl.pallas_call(
         band_kernel,
         in_specs=[whole, pl.BlockSpec(memory_space=pltpu.HBM)],
-        out_specs=whole,
-        out_shape=jax.ShapeDtypeStruct((rows, samples), BF),
+        out_specs=(whole, whole),
+        out_shape=(jax.ShapeDtypeStruct((rows, samples), BF), jax.ShapeDtypeStruct(weights.shape, BF)),
         scratch_shapes=[
-            pltpu.VMEM(weights.shape, BF),
             pltpu.VMEM((rows, samples + weights.shape[3]), BF),
             pltpu.SemaphoreType.DMA((len(BAND_SIZES),)),
         ],
@@ -190,6 +188,43 @@
     )(averaged, pltpu.with_memory_space_constraint(weights, pltpu.HBM))
 
 
+def border_kernel(place_ref, one_ref, other_ref, own_ref, weights, column_ref, sent_ref, padded):
+    samples = own_ref.shape[1]
+    band = weights.shape[3]
+    odd = place_ref[0] % 2 == 1
+    one, other = one_ref[...], other_ref[...]
+    padded[:CELLS, :samples] = jnp.where(odd, one, other)
+    padded[CELLS:, :samples] = jnp.where(odd, other, one)
+    padded[:, samples:] = jnp.zeros((2 * CELLS, band), BF)
+    own = own_ref[...]
+    column_ref[CELLS : 2 * CELLS, :] = own
+    sent_ref[CELLS : 2 * CELLS, :] = own
+    sent_ref[3 * CELLS :, :] = own[: sent_ref.shape[0] - 3 * CELLS]
+    for block in range(weights.shape[1]):
+        lanes = slice(block * band, (block + 1) * band)
+        total = moved_block(padded, weights, block, {})
+        for ref in (column_ref, sent_ref):
+            ref[:CELLS, lanes] = total[:CELLS]
+            ref[2 * CELLS : 3 * CELLS, lanes] = total[CELLS:]
+
+
+def border(place, one, other, own, weights):
+    samples = own.shape[1]
+    whole = pl.BlockSpec(memory_space=pltpu.VMEM)
+    return pl.pallas_call(
+        border_kernel,
+        in_specs=[pl.BlockSpec(memory_space=pltpu.SMEM)] + [whole] * 4,
+        out_specs=(whole, whole),
+        out_shape=(
+            jax.ShapeDtypeStruct((3 * CELLS, samples), BF),
+            jax.ShapeDtypeStruct((3 * CELLS + 16, samples), BF),
+        ),
+        scratch_shapes=[pltpu.VMEM((2 * CELLS, samples + weights.shape[3]), BF)],
+        compiler_params=pltpu.CompilerParams(vmem_limit_bytes=16 << 20),
+        name="border",
+    )(place, one, other, own, weights)
+
+
 TILE = 2048
 WIDE = BX * CH
 EDGE = 128
@@ -216,34 +251,15 @@
     return (bin_x >= 0) & (bin_x < place_ref[3]) & (bin_i >= 0) & (bin_i < place_ref[2])
 
 
-def run_tiles(
-    columns, weights, loads, first, second, keeps, split, store, averaged, volume, taps, hidden
-):
+def run_tiles(columns, first, second, keeps, split, store, volume, taps, hidden):
     samples = volume.shape[1] - 2 * EDGE
-    _, blocks, _, band = weights.shape
     count = len(columns)
     group = 3 * count * TALL
     clear_edges(volume)
     clear_edges(hidden)
-    averaged[:, samples:] = jnp.zeros((averaged.shape[0], averaged.shape[1] - samples), BF)
     for which, column in enumerate(columns):
-        at = 2 * which * CELLS
-        averaged[at : at + CELLS, :samples] = column[:CELLS, :]
-        averaged[at + CELLS : at + 2 * CELLS, :samples] = column[2 * CELLS : 3 * CELLS, :]
-        at = (3 * which + 1) * CELLS
-        volume[at : at + CELLS, EDGE : EDGE + samples] = column[CELLS : 2 * CELLS, :]
-
-    def move_out(block):
-        total = moved_block(averaged, weights, block, loads)
-        start = block * band
-        lanes = slice(EDGE + start, EDGE + start + band)
-        for which in range(count):
-            volume[3 * which * CELLS : (3 * which + 1) * CELLS, lanes] = total[
-                2 * which * CELLS : (2 * which + 1) * CELLS
-            ]
-            volume[(3 * which + 2) * CELLS : (3 * which + 3) * CELLS, lanes] = total[
-                (2 * which + 1) * CELLS : (2 * which + 2) * CELLS
-            ]
+        at = 3 * which * CELLS
+        volume[at : at + 3 * CELLS, EDGE : EDGE + samples] = column[: 3 * CELLS, :]
 
     def first_convolution(start):
         lanes = slice(start, start + TILE)
@@ -263,12 +279,7 @@
         held = jnp.concatenate(taps_of(hidden, slice(None), start), axis=0)
         store(nn(second, held), slice(start, start + TILE))
 
-    done = 0
     for start in range(0, samples, TILE):
-        ready = min((start + TILE) // band + 1, blocks)
-        for block in range(done, ready):
-            move_out(block)
-        done = ready
         first_convolution(start)
         if start:
             second_convolution(start - TILE)
@@ -276,10 +287,8 @@
 
 
 def near_kernel(
-    place_ref, band_ref, mid_ref, near_ref, first_ref, second_ref,
-    partial_ref, sum_ref, weights, averaged, volume, taps, hidden, sem,
+    place_ref, mid_ref, near_ref, first_ref, second_ref, partial_ref, sum_ref, volume, taps, hidden,
 ):
-    loads = band_loads(band_ref, weights, sem, NEAR_SIZES)
     start_x = jnp.where(place_ref[1] % 2 == 0, BX, 0)
     keeps = [inside(place_ref, start_x, line) for line in range(BI + 2)]
 
@@ -291,14 +300,12 @@
         sum_ref[:, lanes] = value
 
     run_tiles(
-        (mid_ref, near_ref), weights, loads, first_ref[...], second_ref[...], keeps, split, store,
-        averaged, volume, taps, hidden,
+        (mid_ref, near_ref), first_ref[...], second_ref[...], keeps, split, store, volume, taps, hidden,
     )
 
 
 def far_kernel(
-    place_ref, weights, far_ref, partial_ref, sum_ref, first_ref, second_ref, out_ref,
-    averaged, volume, taps, hidden,
+    place_ref, far_ref, partial_ref, sum_ref, first_ref, second_ref, out_ref, volume, taps, hidden,
 ):
     start_x = jnp.where(place_ref[1] % 2 == 0, 0, BX)
     keeps = [inside(place_ref, start_x, line) for line in range(BI + 2)]
@@ -311,12 +318,11 @@
         out_ref[:, :, :, lanes] = total.reshape(out_ref.shape[:3] + (TILE,))
 
     run_tiles(
-        (far_ref,), weights, {}, first_ref[...], second_ref[...], keeps, split, store,
-        averaged, volume, taps, hidden,
-    )
-
-
-def convolutions(place, weights, mid, near, far, matrices):
+        (far_ref,), first_ref[...], second_ref[...], keeps, split, store, volume, taps, hidden,
+    )
+
+
+def convolutions(place, mid, near, far, matrices):
     samples = mid.shape[1]
     first_near, first_far, second_near, second_far = matrices
     whole = pl.BlockSpec(memory_space=pltpu.VMEM)
@@ -325,35 +331,33 @@
 
     def buffers(count):
         return [
-            pltpu.VMEM((2 * count * CELLS, samples + weights.shape[3]), BF),
             pltpu.VMEM((3 * count * CELLS, samples + 2 * EDGE), BF),
             pltpu.VMEM((3 * count * ALL_LINES * TALL, samples), BF),
             pltpu.VMEM((bins, samples + 2 * EDGE), BF),
         ]
 
-    partial, total, held = pl.pallas_call(
+    partial, total = pl.pallas_call(
         near_kernel,
-        in_specs=[scalars, pl.BlockSpec(memory_space=pltpu.HBM)] + [whole] * 4,
-        out_specs=(whole, whole, whole),
+        in_specs=[scalars] + [whole] * 4,
+        out_specs=(whole, whole),
         out_shape=(
             jax.ShapeDtypeStruct((bins, samples), F32),
             jax.ShapeDtypeStruct((CH * BI * BX, samples), F32),
-            jax.ShapeDtypeStruct(weights.shape, BF),
         ),
-        scratch_shapes=buffers(2) + [pltpu.SemaphoreType.DMA((len(NEAR_SIZES),))],
+        scratch_shapes=buffers(2),
         compiler_params=pltpu.CompilerParams(vmem_limit_bytes=24 << 20),
         cost_estimate=pl.CostEstimate(flops=0, bytes_accessed=0, transcendentals=0),
         name="near",
-    )(place, pltpu.with_memory_space_constraint(weights, pltpu.HBM), mid, near, first_near, second_near)
+    )(place, mid, near, first_near, second_near)
     return pl.pallas_call(
         far_kernel,
-        in_specs=[scalars] + [whole] * 6,
+        in_specs=[scalars] + [whole] * 5,
         out_specs=whole,
         out_shape=jax.ShapeDtypeStruct((CH, BI, BX, samples), BF),
         scratch_shapes=buffers(1),
         compiler_params=pltpu.CompilerParams(vmem_limit_bytes=24 << 20),
         name="far",
-    )(place, held, far, partial, total, first_far, second_far)
+    )(place, far, partial, total, first_far, second_far)
 
 
 def first_matrices(kernel, odd):
@@ -412,23 +416,21 @@
     arrived = lax.all_to_all(
         outgoing.reshape(devices, 2 * CAP, width), ALL, split_axis=0, concat_axis=0, tiled=True
     ).reshape(devices * 2 * CAP, width)
-    odd_i, odd_x = at_i % 2 == 1, at_x % 2 == 1
+    odd_x = at_x % 2 == 1
+    place = jnp.stack(
+        [at_i, at_x, jnp.int32(inline_size * BI), jnp.int32(xline_size * BX)]
+    ).astype(jnp.int32)
     matrices = first_matrices(conv_first, odd_x) + second_matrices(conv_second, odd_x)
-    arrived, matrices = lax.optimization_barrier((arrived, matrices))
+    arrived, matrices, place = lax.optimization_barrier((arrived, matrices, place))
     classes, blocks, steps, band, _ = band_weights.shape
     weights = band_weights.reshape(classes, blocks, steps * band, band)
     averaged = stack(arrived)
     one, other = swapped(averaged, "inline", 0), swapped(averaged, "inline", 1)
-    volume = moved_out(averaged, weights)
-    up, down = jnp.where(odd_i, one, other), jnp.where(odd_i, other, one)
-    column = jnp.concatenate([up, volume, down], axis=0)
-    sent = jnp.concatenate([up, volume, down, up[:16]], axis=0)
+    volume, weights = moved_out(averaged, weights)
+    column, sent = border(place, one, other, volume, weights)
     far = swapped(sent, "xline", 1)
     near = swapped(column, "xline", 0)
-    place = jnp.stack(
-        [at_i, at_x, jnp.int32(inline_size * BI), jnp.int32(xline_size * BX)]
-    ).astype(jnp.int32)
-    return convolutions(place, weights, column, near, far, matrices)
+    return convolutions(place, column, near, far, matrices)
 
 
 def solution(mesh):

time: 71.5 us -> 70.9 us (level)
  Pallas kernels: 18.5 us -> 15.6 us
  waiting for transfers between devices: 26.2 us -> 29 us
    pallas_call x2 -> x3, Pallas kernels: 10.5 us -> 7.56 us  [the longest x1 3.1 us: convolutions(): pl.pallas_call(far_kernel, in_specs=[scalars] + [whole] * 5, out_specs=wh...]
    ppermute x4, waiting for transfers between devices: 1.97 us -> 4.54 us  [swapped(): return lax.ppermute(block, axis, pairs + [(j, i) for i, j in pairs])]
    reshape x2, local copies, waits for them, and re-layouts: 1.55 us -> 0.28 us  [first_matrices(): return (near.reshape(2 * WIDE, -1), far.reshape(WIDE, -1))]
    another operation x1, local copies, waits for them, and re-layouts: 0.06 us -> 1.03 us  [first_matrices(): matrix = jnp.stack(placed, axis=0).transpose(0, 5, 1, 3, 2, 4)]
  transfers between devices with their start and end apart: 5 -> 5, of which waited for: 3 -> 4; matrix products, arithmetic and copies ran while one was open for 11% -> 11% of each run, Pallas kernels for 14% -> 9%
where the time goes in v5:
time: 70.9 us; the launch traced here: 70.6 us
  waiting for transfers between devices  29 us (41%)
  starting transfers between devices  18 us (25%)
  Pallas kernels  15.6 us (22%)
  local copies, waits for them, and re-layouts  5.41 us (8%)
  other arithmetic  2.25 us (3%)
    all_to_all x1, waiting for transfers between devices, per_device(): lax.all_to_all(outgoing.reshape(devices, 2 * CAP, width), ALL, split_axis...  24.5 us
    all_to_all x1, starting transfers between devices, per_device(): lax.all_to_all(outgoing.reshape(devices, 2 * CAP, width), ALL, split_axis...  10.8 us
    ppermute x4, starting transfers between devices, swapped(): return lax.ppermute(block, axis, pairs + [(j, i) for i, j in pairs])  7.19 us
    ppermute x4, waiting for transfers between devices, swapped(): return lax.ppermute(block, axis, pairs + [(j, i) for i, j in pairs])  4.54 us
    pallas_call x1, Pallas kernels, moved_out(): pl.pallas_call(band_kernel, in_specs=[whole, pl.BlockSpec(memory_space=pl...  3.77 us
    pallas_call x1, Pallas kernels, pack(): pl.pallas_call(pack_kernel, in_specs=[kept] * 4, out_specs=kept, out_shap...  3.7 us
    pallas_call x1, Pallas kernels, convolutions(): pl.pallas_call(far_kernel, in_specs=[scalars] + [whole] * 5, out_specs=wh...  3.1 us
    pallas_call x1, Pallas kernels, convolutions(): pl.pallas_call(near_kernel, in_specs=[scalars] + [whole] * 4, out_specs=(...  2.45 us
  transfers between devices with their start and end apart: 5, of which 4 were waited for; matrix products, arithmetic and copies ran while one was open for 11% of the time, Pallas kernels for 9%

profile of v5, /device:TPU:3, one launch (start us, length us, event | category | flops | bytes accessed | tf_op | source)
XLA Modules:
  0.0 70.6 jit_solution(7328930883019324707)
XLA Ops:
  0.0 3.7 %pack.1 = bf16[1024,1152]{1,0:T(8,128)(2,1)} custom-call(s32[1,256]{1,0:T(1,128)} %bitcast.49, s32[1,256]{1,0:T(1,128)} %bitcast.50, s32[1,256]{1,0:T(1,128)} %bitcast.51, bf16[256,2048]{1,0:T(8,128)(2,1)} %traces_ref.1), custom_call_target="tpu_custom_call" | custom-call | tf_op jit(solution)/shard_map/pack/pallas_call | solution.py:97
  3.7 10.8 %all-to-all-start = ((bf16[128,8,1152]{2,1,0:T(8,128)(2,1)}), bf16[128,8,1152]{2,1,0:T(8,128)(2,1)S(1)}, u32[]{:S(2)}, u32[]{:S(2)}) async-start(bf16[128,8,1152]{2,1,0:T(8,128)(2,1)} %bitcast.45), calls=%async_computation | async-start | bytes 4718592 | tf_op jit(solution)/shard_map/all_to_all | solution.py:416
  14.6 0.3 pad_bitcast_fusion.3
  14.9 0.3 maximum_bitcast_fusion.1
  15.2 0.4 maximum_bitcast_fusion
  15.6 1.0 %select_bitcast_fusion = (bf16[32,2,2,3,4,2,32]{6,0,3,5,4,2,1:T(8,128)(2,1)}, bf16[32,2,2,3,4,2,32]{6,0,3,5,4,2,1:T(8,128)(2,1)S(1)}) fusion(pred[]{:T(512)S(6)} %eq.5, bf16[3,32,2,2,4,4,32]{6,1,0,5,4,3,2:T(8,128)(2,1)S(1)} %maximum_bitcast_fusion), kind=kLoop, calls=%fused_computation.3 | loop fusion | flops 196608 | bytes 786433 | tf_op jit(solution)/shard_map/transpose | solution.py:393
  16.6 0.6 copy.14
  17.2 0.5 reshape.37.second_ref
  17.7 1.7 %copy.15 = bf16[32,2,2,3,4,2,32]{6,5,4,3,2,1,0:T(2,128)(2,1)S(1)} copy(bf16[32,2,2,3,4,2,32]{6,0,3,5,4,2,1:T(8,128)(2,1)} %get-tuple-element.29) | data formatting | bytes 393216 | tf_op jit(solution)/shard_map/transpose | solution.py:393
  19.4 0.5 reshape.38.second_ref
  19.9 1.0 %pad_bitcast_fusion.7 = (bf16[1,3,6,3,8,32]{5,4,3,2,1,0:T(8,128)(2,1)S(1)}, bf16[1,3,6,3,8,32]{5,4,3,2,1,0:T(8,128)(2,1)S(1)}, bf16[1,3,6,3,8,32]{5,4,3,2,1,0:T(8,128)(2,1)S(1)}, bf16[1,3,6,3,8,32]{5,4,3,2,1,0:T(8,128)(2,1)S(1)}) fusion(bf16[3,3,3,8,32]{4,3,2,1,0:T(8,128)(2,1)} %bitcast.48), kind=kLoop, calls=%fused_computation.23 | loop fusion | bytes 124416 | tf_op jit(solution)/shard_map/stack | solution.py:368
  20.9 0.1 maximum_bitcast_fusion.3
  21.2 0.2 fusion.1
  21.6 0.2 copy.12
  21.7 0.2 reshape.35
  22.0 0.1 reshape.36
  22.1 0.1 pad_add_fusion.place_ref
  22.2 24.5 %all-to-all-done = bf16[128,8,1152]{2,1,0:T(8,128)(2,1)S(1)} async-done(((bf16[128,8,1152]{2,1,0:T(8,128)(2,1)}), bf16[128,8,1152]{2,1,0:T(8,128)(2,1)S(1)}, u32[]{:S(2)}, u32[]{:S(2)}) %all-to-all-start) | async-done | bytes 2359328 | tf_op jit(solution)/shard_map/all_to_all | solution.py:416
  46.6 0.6 stack.69.averaged_ref
  47.2 0.6 collective-permute-start
  47.8 3.0 %collective-permute-start.1 = (bf16[32,2048]{1,0:T(8,128)(2,1)S(1)}, bf16[32,2048]{1,0:T(8,128)(2,1)S(1)}, u32[]{:S(2)}, u32[]{:S(2)}) collective-permute-start(bf16[32,2048]{1,0:T(8,128)(2,1)S(1)} %stack.69.averaged_ref), channel_id=1, source_target_pairs={{8,16},{24,32},{40,48},{56,64},{72,80},{88,96},{104,112},{16,8},{3... | collective-permute-start | bytes 393224 | tf_op jit(solution)/shard_map/ppermute | solution.py:399
  50.9 3.8 %band.1 = (bf16[32,2048]{1,0:T(8,128)(2,1)S(1)}, bf16[8,16,256,128]{3,2,1,0:T(8,128)(2,1)S(1)}) custom-call(bf16[32,2048]{1,0:T(8,128)(2,1)S(1)} %stack.69.averaged_ref, bf16[8,16,256,128]{3,2,1,0:T(8,128)(2,1)} %bitcast.46), custom_call_target="tpu_custom_call" | custom-call | tf_op jit(solution)/shard_map/band/pallas_call | solution.py:177
  54.7 1.0 %collective-permute-done.1.other_ref = bf16[32,2048]{1,0:T(8,128)(2,1)S(1)} collective-permute-done((bf16[32,2048]{1,0:T(8,128)(2,1)S(1)}, bf16[32,2048]{1,0:T(8,128)(2,1)S(1)}, u32[]{:S(2)}, u32[]{:S(2)}) %collective-permute-start.1) | collective-permute-done | bytes 131104 | tf_op jit(solution)/shard_map/ppermute | solution.py:399
  55.7 2.0 %border.1 = (bf16[96,2048]{1,0:T(8,128)(2,1)S(1)}, bf16[112,2048]{1,0:T(8,128)(2,1)S(1)}) custom-call(s32[4]{0:T(128)S(1)} %pad_add_fusion.place_ref, bf16[32,2048]{1,0:T(8,128)(2,1)S(1)} %collective-permute-done.one_ref, bf16[32,2048]{1,0:T(8,128)(2,1)S(1)} %collective-permute-done.1.other_ref, bf16[32,2048]{1,0:T(8,128)(2,1)S(1)} %get-tuple-element.19.own_ref, ...), custom_call_target="tpu_custom_call" | custom-call | tf_op jit(solution)/shard_map/border/pallas_call | solution.py:214
  57.7 2.8 %collective-permute-start.2 = (bf16[112,2048]{1,0:T(8,128)(2,1)S(1)}, bf16[112,2048]{1,0:T(8,128)(2,1)S(1)}, u32[]{:S(2)}, u32[]{:S(2)}) collective-permute-start(bf16[112,2048]{1,0:T(8,128)(2,1)S(1)} %get-tuple-element.21), channel_id=1, source_target_pairs={{1,2},{3,4},{5,6},{2,1},{4,3},{6,5},{9,10},{11,12},{13,14},{10,9},... | collective-permute-start | bytes 1376264 | tf_op jit(solution)/shard_map/ppermute | solution.py:399
  60.5 0.8 %collective-permute-start.3 = (bf16[96,2048]{1,0:T(8,128)(2,1)S(1)}, bf16[96,2048]{1,0:T(8,128)(2,1)S(1)}, u32[]{:S(2)}, u32[]{:S(2)}) collective-permute-start(bf16[96,2048]{1,0:T(8,128)(2,1)S(1)} %get-tuple-element.22.mid_ref), channel_id=1, source_target_pairs={{0,1},{2,3},{4,5},{6,7},{1,0},{3,2},{5,4},{7,6},{8,9},{10,11},{12,... | collective-permute-start | bytes 1179656 | tf_op jit(solution)/shard_map/ppermute | solution.py:399
  61.2 0.1 copy.16.first_ref
  61.3 0.1 copy.17.first_ref
  61.4 1.1 %collective-permute-done.3.near_ref = bf16[96,2048]{1,0:T(8,128)(2,1)S(1)} collective-permute-done((bf16[96,2048]{1,0:T(8,128)(2,1)S(1)}, bf16[96,2048]{1,0:T(8,128)(2,1)S(1)}, u32[]{:S(2)}, u32[]{:S(2)}) %collective-permute-start.3) | collective-permute-done | bytes 393248 | tf_op jit(solution)/shard_map/ppermute | solution.py:399
  62.6 2.4 %near.1 = (f32[256,2048]{1,0:T(8,128)S(1)}, f32[128,2048]{1,0:T(8,128)S(1)}) custom-call(s32[4]{0:T(128)S(1)} %pad_add_fusion.place_ref, bf16[96,2048]{1,0:T(8,128)(2,1)S(1)} %get-tuple-element.22.mid_ref, bf16[96,2048]{1,0:T(8,128)(2,1)S(1)} %collective-permute-done.3.near_ref, bf16[128,288]{1,0:T(8,128)(2,1)S(1)} %copy.16.first_ref, ...), custom_call_target="tpu_custom_call" | custom-call | tf_op jit(solution)/shard_map/near/pallas_call | solution.py:339
  65.0 2.4 %collective-permute-done.2.far_ref = bf16[112,2048]{1,0:T(8,128)(2,1)S(1)} collective-permute-done((bf16[112,2048]{1,0:T(8,128)(2,1)S(1)}, bf16[112,2048]{1,0:T(8,128)(2,1)S(1)}, u32[]{:S(2)}, u32[]{:S(2)}) %collective-permute-start.2) | collective-permute-done | bytes 458784 | tf_op jit(solution)/shard_map/ppermute | solution.py:399
  67.5 3.1 %far.1 = bf16[32,2,2,2048]{3,2,1,0:T(2,128)(2,1)} custom-call(s32[4]{0:T(128)S(1)} %pad_add_fusion.place_ref, bf16[112,2048]{1,0:T(8,128)(2,1)S(1)} %collective-permute-done.2.far_ref, f32[256,2048]{1,0:T(8,128)S(1)} %get-tuple-element.25.partial_ref, f32[128,2048]{1,0:T(8,128)S(1)} %get-tuple-element.26.sum_ref, bf16[64,144]{1,0:T(8,128)(2,1)S(1)} %copy.17.first_ref, ...), custom_call_target="tpu_custom_call" | custom-call | tf_op jit(solution)/shard_map/far/pallas_call | solution.py:352
  (9 shorter events, 0.3 us)
Async XLA Ops:
  3.7 10.9 %copy-start = (bf16[32,32,3,3,3]{1,0,4,3,2:T(8,128)(2,1)S(1)}, bf16[32,32,3,3,3]{1,0,4,3,2:T(8,128)(2,1)}, u32[]{:S(2)}) copy-start(bf16[32,32,3,3,3]{1,0,4,3,2:T(8,128)(2,1)} %param.13) | copy-start | bytes 165892
  3.7 42.9 %all-to-all-start = ((bf16[128,8,1152]{2,1,0:T(8,128)(2,1)}), bf16[128,8,1152]{2,1,0:T(8,128)(2,1)S(1)}, u32[]{:S(2)}, u32[]{:S(2)}) async-start(bf16[128,8,1152]{2,1,0:T(8,128)(2,1)} %bitcast.45), calls=%async_computation | async-start | bytes 4718592 | tf_op jit(solution)/shard_map/all_to_all | solution.py:416
  47.2 7.4 %collective-permute-start = (bf16[32,2048]{1,0:T(8,128)(2,1)S(1)}, bf16[32,2048]{1,0:T(8,128)(2,1)S(1)}, u32[]{:S(2)}, u32[]{:S(2)}) collective-permute-start(bf16[32,2048]{1,0:T(8,128)(2,1)S(1)} %stack.69.averaged_ref), channel_id=1, source_target_pairs={{0,8},{16,24},{32,40},{48,56},{64,72},{80,88},{96,104},{112,120},{... | collective-permute-start | bytes 393224 | tf_op jit(solution)/shard_map/ppermute | solution.py:399
  47.8 7.8 %collective-permute-start.1 = (bf16[32,2048]{1,0:T(8,128)(2,1)S(1)}, bf16[32,2048]{1,0:T(8,128)(2,1)S(1)}, u32[]{:S(2)}, u32[]{:S(2)}) collective-permute-start(bf16[32,2048]{1,0:T(8,128)(2,1)S(1)} %stack.69.averaged_ref), channel_id=1, source_target_pairs={{8,16},{24,32},{40,48},{56,64},{72,80},{88,96},{104,112},{16,8},{3... | collective-permute-start | bytes 393224 | tf_op jit(solution)/shard_map/ppermute | solution.py:399
  57.7 9.8 %collective-permute-start.2 = (bf16[112,2048]{1,0:T(8,128)(2,1)S(1)}, bf16[112,2048]{1,0:T(8,128)(2,1)S(1)}, u32[]{:S(2)}, u32[]{:S(2)}) collective-permute-start(bf16[112,2048]{1,0:T(8,128)(2,1)S(1)} %get-tuple-element.21), channel_id=1, source_target_pairs={{1,2},{3,4},{5,6},{2,1},{4,3},{6,5},{9,10},{11,12},{13,14},{10,9},... | collective-permute-start | bytes 1376264 | tf_op jit(solution)/shard_map/ppermute | solution.py:399
  60.5 2.1 %collective-permute-start.3 = (bf16[96,2048]{1,0:T(8,128)(2,1)S(1)}, bf16[96,2048]{1,0:T(8,128)(2,1)S(1)}, u32[]{:S(2)}, u32[]{:S(2)}) collective-permute-start(bf16[96,2048]{1,0:T(8,128)(2,1)S(1)} %get-tuple-element.22.mid_ref), channel_id=1, source_target_pairs={{0,1},{2,3},{4,5},{6,7},{1,0},{3,2},{5,4},{7,6},{8,9},{10,11},{12,... | collective-permute-start | bytes 1179656 | tf_op jit(solution)/shard_map/ppermute | solution.py:399

commit v6 on v5

--- a/solution.py
+++ b/solution.py
@@ -188,7 +188,9 @@
     )(averaged, pltpu.with_memory_space_constraint(weights, pltpu.HBM))
 
 
-def border_kernel(place_ref, one_ref, other_ref, own_ref, weights, column_ref, sent_ref, padded):
+def border_kernel(
+    place_ref, one_ref, other_ref, own_ref, weights, column_ref, top_ref, bottom_ref, padded
+):
     samples = own_ref.shape[1]
     band = weights.shape[3]
     odd = place_ref[0] % 2 == 1
@@ -198,14 +200,15 @@
     padded[:, samples:] = jnp.zeros((2 * CELLS, band), BF)
     own = own_ref[...]
     column_ref[CELLS : 2 * CELLS, :] = own
-    sent_ref[CELLS : 2 * CELLS, :] = own
-    sent_ref[3 * CELLS :, :] = own[: sent_ref.shape[0] - 3 * CELLS]
+    top_ref[CELLS:, :] = own[: CELLS // 2]
+    bottom_ref[: CELLS // 2, :] = own[CELLS // 2 :]
     for block in range(weights.shape[1]):
         lanes = slice(block * band, (block + 1) * band)
         total = moved_block(padded, weights, block, {})
-        for ref in (column_ref, sent_ref):
-            ref[:CELLS, lanes] = total[:CELLS]
-            ref[2 * CELLS : 3 * CELLS, lanes] = total[CELLS:]
+        column_ref[:CELLS, lanes] = total[:CELLS]
+        column_ref[2 * CELLS :, lanes] = total[CELLS:]
+        top_ref[:CELLS, lanes] = total[:CELLS]
+        bottom_ref[CELLS // 2 :, lanes] = total[CELLS:]
 
 
 def border(place, one, other, own, weights):
@@ -214,10 +217,11 @@
     return pl.pallas_call(
         border_kernel,
         in_specs=[pl.BlockSpec(memory_space=pltpu.SMEM)] + [whole] * 4,
-        out_specs=(whole, whole),
+        out_specs=(whole, whole, whole),
         out_shape=(
             jax.ShapeDtypeStruct((3 * CELLS, samples), BF),
-            jax.ShapeDtypeStruct((3 * CELLS + 16, samples), BF),
+            jax.ShapeDtypeStruct((3 * CELLS // 2, samples), BF),
+            jax.ShapeDtypeStruct((3 * CELLS // 2, samples), BF),
         ),
         scratch_shapes=[pltpu.VMEM((2 * CELLS, samples + weights.shape[3]), BF)],
         compiler_params=pltpu.CompilerParams(vmem_limit_bytes=16 << 20),
@@ -259,7 +263,9 @@
     clear_edges(hidden)
     for which, column in enumerate(columns):
         at = 3 * which * CELLS
-        volume[at : at + 3 * CELLS, EDGE : EDGE + samples] = column[: 3 * CELLS, :]
+        for piece in column:
+            volume[at : at + piece.shape[0], EDGE : EDGE + samples] = piece[...]
+            at += piece.shape[0]
 
     def first_convolution(start):
         lanes = slice(start, start + TILE)
@@ -287,7 +293,8 @@
 
 
 def near_kernel(
-    place_ref, mid_ref, near_ref, first_ref, second_ref, partial_ref, sum_ref, volume, taps, hidden,
+    place_ref, mid_ref, top_ref, bottom_ref, first_ref, second_ref,
+    partial_ref, sum_ref, volume, taps, hidden,
 ):
     start_x = jnp.where(place_ref[1] % 2 == 0, BX, 0)
     keeps = [inside(place_ref, start_x, line) for line in range(BI + 2)]
@@ -300,7 +307,8 @@
         sum_ref[:, lanes] = value
 
     run_tiles(
-        (mid_ref, near_ref), first_ref[...], second_ref[...], keeps, split, store, volume, taps, hidden,
+        ((mid_ref,), (top_ref, bottom_ref)), first_ref[...], second_ref[...], keeps, split, store,
+        volume, taps, hidden,
     )
 
 
@@ -318,11 +326,11 @@
         out_ref[:, :, :, lanes] = total.reshape(out_ref.shape[:3] + (TILE,))
 
     run_tiles(
-        (far_ref,), first_ref[...], second_ref[...], keeps, split, store, volume, taps, hidden,
-    )
-
-
-def convolutions(place, mid, near, far, matrices):
+        ((far_ref,),), first_ref[...], second_ref[...], keeps, split, store, volume, taps, hidden,
+    )
+
+
+def convolutions(place, mid, top, bottom, far, matrices):
     samples = mid.shape[1]
     first_near, first_far, second_near, second_far = matrices
     whole = pl.BlockSpec(memory_space=pltpu.VMEM)
@@ -338,7 +346,7 @@
 
     partial, total = pl.pallas_call(
         near_kernel,
-        in_specs=[scalars] + [whole] * 4,
+        in_specs=[scalars] + [whole] * 5,
         out_specs=(whole, whole),
         out_shape=(
             jax.ShapeDtypeStruct((bins, samples), F32),
@@ -348,7 +356,7 @@
         compiler_params=pltpu.CompilerParams(vmem_limit_bytes=24 << 20),
         cost_estimate=pl.CostEstimate(flops=0, bytes_accessed=0, transcendentals=0),
         name="near",
-    )(place, mid, near, first_near, second_near)
+    )(place, mid, top, bottom, first_near, second_near)
     return pl.pallas_call(
         far_kernel,
         in_specs=[scalars] + [whole] * 5,
@@ -427,10 +435,10 @@
     averaged = stack(arrived)
     one, other = swapped(averaged, "inline", 0), swapped(averaged, "inline", 1)
     volume, weights = moved_out(averaged, weights)
-    column, sent = border(place, one, other, volume, weights)
-    far = swapped(sent, "xline", 1)
-    near = swapped(column, "xline", 0)
-    return convolutions(place, column, near, far, matrices)
+    column, top, bottom = border(place, one, other, volume, weights)
+    far = swapped(column, "xline", 1)
+    top, bottom = swapped(top, "xline", 0), swapped(bottom, "xline", 0)
+    return convolutions(place, column, top, bottom, far, matrices)
 
 
 def solution(mesh):

time: 70.9 us -> 70.2 us (level)
  waiting for transfers between devices: 29 us -> 28.2 us
    ppermute x4 -> x5, waiting for transfers between devices: 4.54 us -> 3.76 us  [swapped(): return lax.ppermute(block, axis, pairs + [(j, i) for i, j in pairs])]
    ppermute x4 -> x5, starting transfers between devices: 7.19 us -> 7.27 us  [swapped(): return lax.ppermute(block, axis, pairs + [(j, i) for i, j in pairs])]
  transfers between devices with their start and end apart: 5 -> 6, of which waited for: 4 -> 5; matrix products, arithmetic and copies ran while one was open for 11% -> 11% of each run, Pallas kernels for 9% -> 9%
where the time goes in v6:
time: 70.2 us; the launch traced here: 69.9 us
  waiting for transfers between devices  28.2 us (40%)
  starting transfers between devices  18.1 us (26%)
  Pallas kernels  15.6 us (22%)
  local copies, waits for them, and re-layouts  5.41 us (8%)
  other arithmetic  2.25 us (3%)
    all_to_all x1, waiting for transfers between devices, per_device(): lax.all_to_all(outgoing.reshape(devices, 2 * CAP, width), ALL, split_axis...  24.5 us
    all_to_all x1, starting transfers between devices, per_device(): lax.all_to_all(outgoing.reshape(devices, 2 * CAP, width), ALL, split_axis...  10.8 us
    ppermute x5, starting transfers between devices, swapped(): return lax.ppermute(block, axis, pairs + [(j, i) for i, j in pairs])  7.27 us
    pallas_call x1, Pallas kernels, moved_out(): pl.pallas_call(band_kernel, in_specs=[whole, pl.BlockSpec(memory_space=pl...  3.77 us
    ppermute x5, waiting for transfers between devices, swapped(): return lax.ppermute(block, axis, pairs + [(j, i) for i, j in pairs])  3.76 us
    pallas_call x1, Pallas kernels, pack(): pl.pallas_call(pack_kernel, in_specs=[kept] * 4, out_specs=kept, out_shap...  3.69 us
    pallas_call x1, Pallas kernels, convolutions(): pl.pallas_call(far_kernel, in_specs=[scalars] + [whole] * 5, out_specs=wh...  3.1 us
    pallas_call x1, Pallas kernels, convolutions(): pl.pallas_call(near_kernel, in_specs=[scalars] + [whole] * 5, out_specs=(...  2.45 us
  transfers between devices with their start and end apart: 6, of which 5 were waited for; matrix products, arithmetic and copies ran while one was open for 11% of the time, Pallas kernels for 9%

profile of v6, /device:TPU:3, one launch (start us, length us, event | category | flops | bytes accessed | tf_op | source)
XLA Modules:
  0.0 69.9 jit_solution(18092198506436228127)
XLA Ops:
  0.0 3.7 %pack.1 = bf16[1024,1152]{1,0:T(8,128)(2,1)} custom-call(s32[1,256]{1,0:T(1,128)} %bitcast.49, s32[1,256]{1,0:T(1,128)} %bitcast.50, s32[1,256]{1,0:T(1,128)} %bitcast.51, bf16[256,2048]{1,0:T(8,128)(2,1)} %traces_ref.1), custom_call_target="tpu_custom_call" | custom-call | tf_op jit(solution)/shard_map/pack/pallas_call | solution.py:97
  3.7 10.8 %all-to-all-start = ((bf16[128,8,1152]{2,1,0:T(8,128)(2,1)}), bf16[128,8,1152]{2,1,0:T(8,128)(2,1)S(1)}, u32[]{:S(2)}, u32[]{:S(2)}) async-start(bf16[128,8,1152]{2,1,0:T(8,128)(2,1)} %bitcast.45), calls=%async_computation | async-start | bytes 4718592 | tf_op jit(solution)/shard_map/all_to_all | solution.py:424
  14.6 0.3 pad_bitcast_fusion.3
  14.9 0.3 maximum_bitcast_fusion.1
  15.2 0.4 maximum_bitcast_fusion
  15.6 1.0 %select_bitcast_fusion = (bf16[32,2,2,3,4,2,32]{6,0,3,5,4,2,1:T(8,128)(2,1)}, bf16[32,2,2,3,4,2,32]{6,0,3,5,4,2,1:T(8,128)(2,1)S(1)}) fusion(pred[]{:T(512)S(6)} %eq.5, bf16[3,32,2,2,4,4,32]{6,1,0,5,4,3,2:T(8,128)(2,1)S(1)} %maximum_bitcast_fusion), kind=kLoop, calls=%fused_computation.3 | loop fusion | flops 196608 | bytes 786433 | tf_op jit(solution)/shard_map/transpose | solution.py:401
  16.6 0.6 copy.14
  17.2 0.5 reshape.37.second_ref
  17.7 1.7 %copy.15 = bf16[32,2,2,3,4,2,32]{6,5,4,3,2,1,0:T(2,128)(2,1)S(1)} copy(bf16[32,2,2,3,4,2,32]{6,0,3,5,4,2,1:T(8,128)(2,1)} %get-tuple-element.31) | data formatting | bytes 393216 | tf_op jit(solution)/shard_map/transpose | solution.py:401
  19.4 0.5 reshape.38.second_ref
  19.9 1.0 %pad_bitcast_fusion.7 = (bf16[1,3,6,3,8,32]{5,4,3,2,1,0:T(8,128)(2,1)S(1)}, bf16[1,3,6,3,8,32]{5,4,3,2,1,0:T(8,128)(2,1)S(1)}, bf16[1,3,6,3,8,32]{5,4,3,2,1,0:T(8,128)(2,1)S(1)}, bf16[1,3,6,3,8,32]{5,4,3,2,1,0:T(8,128)(2,1)S(1)}) fusion(bf16[3,3,3,8,32]{4,3,2,1,0:T(8,128)(2,1)} %bitcast.48), kind=kLoop, calls=%fused_computation.23 | loop fusion | bytes 124416 | tf_op jit(solution)/shard_map/stack | solution.py:376
  20.9 0.1 maximum_bitcast_fusion.3
  21.2 0.2 fusion.1
  21.5 0.2 copy.12
  21.7 0.2 reshape.35
  22.0 0.1 reshape.36
  22.1 24.5 %all-to-all-done = bf16[128,8,1152]{2,1,0:T(8,128)(2,1)S(1)} async-done(((bf16[128,8,1152]{2,1,0:T(8,128)(2,1)}), bf16[128,8,1152]{2,1,0:T(8,128)(2,1)S(1)}, u32[]{:S(2)}, u32[]{:S(2)}) %all-to-all-start) | async-done | bytes 2359328 | tf_op jit(solution)/shard_map/all_to_all | solution.py:424
  46.6 0.6 stack.69.averaged_ref
  47.2 0.6 collective-permute-start
  47.8 3.0 %collective-permute-start.1 = (bf16[32,2048]{1,0:T(8,128)(2,1)S(1)}, bf16[32,2048]{1,0:T(8,128)(2,1)S(1)}, u32[]{:S(2)}, u32[]{:S(2)}) collective-permute-start(bf16[32,2048]{1,0:T(8,128)(2,1)S(1)} %stack.69.averaged_ref), channel_id=1, source_target_pairs={{8,16},{24,32},{40,48},{56,64},{72,80},{88,96},{104,112},{16,8},{3... | collective-permute-start | bytes 393224 | tf_op jit(solution)/shard_map/ppermute | solution.py:407
  50.9 3.8 %band.1 = (bf16[32,2048]{1,0:T(8,128)(2,1)S(1)}, bf16[8,16,256,128]{3,2,1,0:T(8,128)(2,1)S(1)}) custom-call(bf16[32,2048]{1,0:T(8,128)(2,1)S(1)} %stack.69.averaged_ref, bf16[8,16,256,128]{3,2,1,0:T(8,128)(2,1)} %bitcast.46), custom_call_target="tpu_custom_call" | custom-call | tf_op jit(solution)/shard_map/band/pallas_call | solution.py:177
  54.7 1.0 %collective-permute-done.1.other_ref = bf16[32,2048]{1,0:T(8,128)(2,1)S(1)} collective-permute-done((bf16[32,2048]{1,0:T(8,128)(2,1)S(1)}, bf16[32,2048]{1,0:T(8,128)(2,1)S(1)}, u32[]{:S(2)}, u32[]{:S(2)}) %collective-permute-start.1) | collective-permute-done | bytes 131104 | tf_op jit(solution)/shard_map/ppermute | solution.py:407
  55.6 2.0 %border.1 = (bf16[96,2048]{1,0:T(8,128)(2,1)S(1)}, bf16[48,2048]{1,0:T(8,128)(2,1)S(1)}, bf16[48,2048]{1,0:T(8,128)(2,1)S(1)}) custom-call(s32[4]{0:T(128)S(1)} %pad_add_fusion.place_ref, bf16[32,2048]{1,0:T(8,128)(2,1)S(1)} %collective-permute-done.one_ref, bf16[32,2048]{1,0:T(8,128)(2,1)S(1)} %collective-permute-done.1.other_ref, ...), custom_call_target="tpu_custom_call" | custom-call | tf_op jit(solution)/shard_map/border/pallas_call | solution.py:217
  57.7 2.8 %collective-permute-start.2 = (bf16[96,2048]{1,0:T(8,128)(2,1)S(1)}, bf16[96,2048]{1,0:T(8,128)(2,1)S(1)}, u32[]{:S(2)}, u32[]{:S(2)}) collective-permute-start(bf16[96,2048]{1,0:T(8,128)(2,1)S(1)} %get-tuple-element.22.mid_ref), channel_id=1, source_target_pairs={{1,2},{3,4},{5,6},{2,1},{4,3},{6,5},{9,10},{11,12},{13,14},{10,9},... | collective-permute-start | bytes 1179656 | tf_op jit(solution)/shard_map/ppermute | solution.py:407
  60.4 0.6 collective-permute-start.3
  61.0 0.3 collective-permute-start.4
  61.3 0.1 copy.16.first_ref
  61.5 0.6 collective-permute-done.3.top_ref
  62.1 0.4 collective-permute-done.4.bottom_ref
  62.5 2.4 %near.1 = (f32[256,2048]{1,0:T(8,128)S(1)}, f32[128,2048]{1,0:T(8,128)S(1)}) custom-call(s32[4]{0:T(128)S(1)} %pad_add_fusion.place_ref, bf16[96,2048]{1,0:T(8,128)(2,1)S(1)} %get-tuple-element.22.mid_ref, bf16[48,2048]{1,0:T(8,128)(2,1)S(1)} %collective-permute-done.3.top_ref, bf16[48,2048]{1,0:T(8,128)(2,1)S(1)} %collective-permute-done.4.bottom_ref, ...), custom_call_target="tpu_custom_call" | custom-call | tf_op jit(solution)/shard_map/near/pallas_call | solution.py:347
  64.9 1.8 %collective-permute-done.2.far_ref = bf16[96,2048]{1,0:T(8,128)(2,1)S(1)} collective-permute-done((bf16[96,2048]{1,0:T(8,128)(2,1)S(1)}, bf16[96,2048]{1,0:T(8,128)(2,1)S(1)}, u32[]{:S(2)}, u32[]{:S(2)}) %collective-permute-start.2) | collective-permute-done | bytes 393248 | tf_op jit(solution)/shard_map/ppermute | solution.py:407
  66.8 3.1 %far.1 = bf16[32,2,2,2048]{3,2,1,0:T(2,128)(2,1)} custom-call(s32[4]{0:T(128)S(1)} %pad_add_fusion.place_ref, bf16[96,2048]{1,0:T(8,128)(2,1)S(1)} %collective-permute-done.2.far_ref, f32[256,2048]{1,0:T(8,128)S(1)} %get-tuple-element.27.partial_ref, f32[128,2048]{1,0:T(8,128)S(1)} %get-tuple-element.28.sum_ref, bf16[64,144]{1,0:T(8,128)(2,1)S(1)} %copy.17.first_ref, ...), custom_call_target="tpu_custom_call" | custom-call | tf_op jit(solution)/shard_map/far/pallas_call | solution.py:360
  (11 shorter events, 0.4 us)
Async XLA Ops:
  3.7 10.9 %copy-start = (bf16[32,32,3,3,3]{1,0,4,3,2:T(8,128)(2,1)S(1)}, bf16[32,32,3,3,3]{1,0,4,3,2:T(8,128)(2,1)}, u32[]{:S(2)}) copy-start(bf16[32,32,3,3,3]{1,0,4,3,2:T(8,128)(2,1)} %param.13) | copy-start | bytes 165892
  3.7 42.9 %all-to-all-start = ((bf16[128,8,1152]{2,1,0:T(8,128)(2,1)}), bf16[128,8,1152]{2,1,0:T(8,128)(2,1)S(1)}, u32[]{:S(2)}, u32[]{:S(2)}) async-start(bf16[128,8,1152]{2,1,0:T(8,128)(2,1)} %bitcast.45), calls=%async_computation | async-start | bytes 4718592 | tf_op jit(solution)/shard_map/all_to_all | solution.py:424
  47.2 7.4 %collective-permute-start = (bf16[32,2048]{1,0:T(8,128)(2,1)S(1)}, bf16[32,2048]{1,0:T(8,128)(2,1)S(1)}, u32[]{:S(2)}, u32[]{:S(2)}) collective-permute-start(bf16[32,2048]{1,0:T(8,128)(2,1)S(1)} %stack.69.averaged_ref), channel_id=1, source_target_pairs={{0,8},{16,24},{32,40},{48,56},{64,72},{80,88},{96,104},{112,120},{... | collective-permute-start | bytes 393224 | tf_op jit(solution)/shard_map/ppermute | solution.py:407
  47.8 7.8 %collective-permute-start.1 = (bf16[32,2048]{1,0:T(8,128)(2,1)S(1)}, bf16[32,2048]{1,0:T(8,128)(2,1)S(1)}, u32[]{:S(2)}, u32[]{:S(2)}) collective-permute-start(bf16[32,2048]{1,0:T(8,128)(2,1)S(1)} %stack.69.averaged_ref), channel_id=1, source_target_pairs={{8,16},{24,32},{40,48},{56,64},{72,80},{88,96},{104,112},{16,8},{3... | collective-permute-start | bytes 393224 | tf_op jit(solution)/shard_map/ppermute | solution.py:407
  57.7 9.1 %collective-permute-start.2 = (bf16[96,2048]{1,0:T(8,128)(2,1)S(1)}, bf16[96,2048]{1,0:T(8,128)(2,1)S(1)}, u32[]{:S(2)}, u32[]{:S(2)}) collective-permute-start(bf16[96,2048]{1,0:T(8,128)(2,1)S(1)} %get-tuple-element.22.mid_ref), channel_id=1, source_target_pairs={{1,2},{3,4},{5,6},{2,1},{4,3},{6,5},{9,10},{11,12},{13,14},{10,9},... | collective-permute-start | bytes 1179656 | tf_op jit(solution)/shard_map/ppermute | solution.py:407
  60.4 1.6 %collective-permute-start.3 = (bf16[48,2048]{1,0:T(8,128)(2,1)S(1)}, bf16[48,2048]{1,0:T(8,128)(2,1)S(1)}, u32[]{:S(2)}, u32[]{:S(2)}) collective-permute-start(bf16[48,2048]{1,0:T(8,128)(2,1)S(1)} %get-tuple-element.23), channel_id=1, source_target_pairs={{0,1},{2,3},{4,5},{6,7},{1,0},{3,2},{5,4},{7,6},{8,9},{10,11},{12,... | collective-permute-start | bytes 589832 | tf_op jit(solution)/shard_map/ppermute | solution.py:407
  61.0 1.4 %collective-permute-start.4 = (bf16[48,2048]{1,0:T(8,128)(2,1)S(1)}, bf16[48,2048]{1,0:T(8,128)(2,1)S(1)}, u32[]{:S(2)}, u32[]{:S(2)}) collective-permute-start(bf16[48,2048]{1,0:T(8,128)(2,1)S(1)} %get-tuple-element.24), channel_id=1, source_target_pairs={{0,1},{2,3},{4,5},{6,7},{1,0},{3,2},{5,4},{7,6},{8,9},{10,11},{12,... | collective-permute-start | bytes 589832 | tf_op jit(solution)/shard_map/ppermute | solution.py:407

commit v7 on v6

--- a/solution.py
+++ b/solution.py
@@ -230,15 +230,16 @@
 
 
 TILE = 2048
+PART = 1024
 WIDE = BX * CH
 EDGE = 128
 ALL_LINES = BI + 4
 TALL = BX * CLASSES
 
 
-def taps_of(padded, rows, start):
-    window = padded[rows, start : start + TILE + 2 * EDGE]
-    inner = slice(EDGE, EDGE + TILE)
+def taps_of(padded, rows, start, size):
+    window = padded[rows, start : start + size + 2 * EDGE]
+    inner = slice(EDGE, EDGE + size)
     width = window.shape[1]
     return pltpu.roll(window, 1, 1)[:, inner], window[:, inner], pltpu.roll(window, width - 1, 1)[:, inner]
 
@@ -271,7 +272,7 @@
         lanes = slice(start, start + TILE)
         for which in range(count):
             rows = slice(3 * which * CELLS, 3 * (which + 1) * CELLS)
-            for tap, value in enumerate(taps_of(volume, rows, start)):
+            for tap, value in enumerate(taps_of(volume, rows, start, TILE)):
                 for line in range(ALL_LINES):
                     at = line * group + (tap * count + which) * TALL
                     taps[at : at + TALL, lanes] = value[line * TALL : (line + 1) * TALL]
@@ -282,8 +283,9 @@
             hidden[rows, EDGE + start : EDGE + start + TILE] = value
 
     def second_convolution(start):
-        held = jnp.concatenate(taps_of(hidden, slice(None), start), axis=0)
-        store(nn(second, held), slice(start, start + TILE))
+        for at in range(start, start + TILE, PART):
+            held = jnp.concatenate(taps_of(hidden, slice(None), at, PART), axis=0)
+            store(nn(second, held), slice(at, at + PART))
 
     for start in range(0, samples, TILE):
         first_convolution(start)
@@ -313,8 +315,9 @@
 
 
 def far_kernel(
-    place_ref, far_ref, partial_ref, sum_ref, first_ref, second_ref, out_ref, volume, taps, hidden,
+    place_ref, far_ref, partial_ref, sum_ref, first_ref, second_ref, out_ref, volume, taps, hidden, made, sem,
 ):
+    copies = []
     start_x = jnp.where(place_ref[1] % 2 == 0, 0, BX)
     keeps = [inside(place_ref, start_x, line) for line in range(BI + 2)]
 
@@ -323,11 +326,18 @@
 
     def store(value, lanes):
         total = (value + sum_ref[:, lanes]).astype(BF)
-        out_ref[:, :, :, lanes] = total.reshape(out_ref.shape[:3] + (TILE,))
+        number = lanes.start // PART
+        made[number] = total.reshape(made.shape[1:])
+        copies.append(
+            pltpu.make_async_copy(made.at[number], out_ref.at[:, :, :, pl.ds(lanes.start, PART)], sem.at[number])
+        )
+        copies[-1].start()
 
     run_tiles(
         ((far_ref,),), first_ref[...], second_ref[...], keeps, split, store, volume, taps, hidden,
     )
+    for copy in copies:
+        copy.wait()
 
 
 def convolutions(place, mid, top, bottom, far, matrices):
@@ -360,9 +370,13 @@
     return pl.pallas_call(
         far_kernel,
         in_specs=[scalars] + [whole] * 5,
-        out_specs=whole,
-        out_shape=jax.ShapeDtypeStruct((CH, BI, BX, samples), BF),
-        scratch_shapes=buffers(1),
+        out_specs=pl.BlockSpec(memory_space=pltpu.HBM),
+        out_shape=pltpu.HBM((CH, BI, BX, samples), BF),
+        scratch_shapes=buffers(1)
+        + [
+            pltpu.VMEM((samples // PART, CH, BI, BX, PART), BF),
+            pltpu.SemaphoreType.DMA((samples // PART,)),
+        ],
         compiler_params=pltpu.CompilerParams(vmem_limit_bytes=24 << 20),
         name="far",
     )(place, far, partial, total, first_far, second_far)

time: 70.2 us -> 70.3 us (level)
  no operation moved by 1% of the time
where the time goes in v7:
time: 70.3 us; the launch traced here: 70 us
  waiting for transfers between devices  28.2 us (40%)
  starting transfers between devices  18.1 us (26%)
  Pallas kernels  15.6 us (22%)
  local copies, waits for them, and re-layouts  5.41 us (8%)
  other arithmetic  2.25 us (3%)
    all_to_all x1, waiting for transfers between devices, per_device(): lax.all_to_all(outgoing.reshape(devices, 2 * CAP, width), ALL, split_axis...  24.5 us
    all_to_all x1, starting transfers between devices, per_device(): lax.all_to_all(outgoing.reshape(devices, 2 * CAP, width), ALL, split_axis...  10.8 us
    ppermute x5, starting transfers between devices, swapped(): return lax.ppermute(block, axis, pairs + [(j, i) for i, j in pairs])  7.27 us
    pallas_call x1, Pallas kernels, moved_out(): pl.pallas_call(band_kernel, in_specs=[whole, pl.BlockSpec(memory_space=pl...  3.77 us
    ppermute x5, waiting for transfers between devices, swapped(): return lax.ppermute(block, axis, pairs + [(j, i) for i, j in pairs])  3.76 us
    pallas_call x1, Pallas kernels, pack(): pl.pallas_call(pack_kernel, in_specs=[kept] * 4, out_specs=kept, out_shap...  3.69 us
    pallas_call x1, Pallas kernels, convolutions(): pl.pallas_call(far_kernel, in_specs=[scalars] + [whole] * 5, out_specs=pl...  3.04 us
    pallas_call x1, Pallas kernels, convolutions(): pl.pallas_call(near_kernel, in_specs=[scalars] + [whole] * 5, out_specs=(...  2.45 us
  transfers between devices with their start and end apart: 6, of which 5 were waited for; matrix products, arithmetic and copies ran while one was open for 11% of the time, Pallas kernels for 9%

profile of v7, /device:TPU:3, one launch (start us, length us, event | category | flops | bytes accessed | tf_op | source)
XLA Modules:
  0.0 70.0 jit_solution(17314986891394178914)
XLA Ops:
  0.0 3.7 %pack.1 = bf16[1024,1152]{1,0:T(8,128)(2,1)} custom-call(s32[1,256]{1,0:T(1,128)} %bitcast.49, s32[1,256]{1,0:T(1,128)} %bitcast.50, s32[1,256]{1,0:T(1,128)} %bitcast.51, bf16[256,2048]{1,0:T(8,128)(2,1)} %traces_ref.1), custom_call_target="tpu_custom_call" | custom-call | tf_op jit(solution)/shard_map/pack/pallas_call | solution.py:97
  3.7 10.8 %all-to-all-start = ((bf16[128,8,1152]{2,1,0:T(8,128)(2,1)}), bf16[128,8,1152]{2,1,0:T(8,128)(2,1)S(1)}, u32[]{:S(2)}, u32[]{:S(2)}) async-start(bf16[128,8,1152]{2,1,0:T(8,128)(2,1)} %bitcast.45), calls=%async_computation | async-start | bytes 4718592 | tf_op jit(solution)/shard_map/all_to_all | solution.py:438
  14.6 0.3 pad_bitcast_fusion.3
  14.9 0.3 maximum_bitcast_fusion.1
  15.2 0.4 maximum_bitcast_fusion
  15.6 1.0 %select_bitcast_fusion = (bf16[32,2,2,3,4,2,32]{6,0,3,5,4,2,1:T(8,128)(2,1)}, bf16[32,2,2,3,4,2,32]{6,0,3,5,4,2,1:T(8,128)(2,1)S(1)}) fusion(pred[]{:T(512)S(6)} %eq.5, bf16[3,32,2,2,4,4,32]{6,1,0,5,4,3,2:T(8,128)(2,1)S(1)} %maximum_bitcast_fusion), kind=kLoop, calls=%fused_computation.3 | loop fusion | flops 196608 | bytes 786433 | tf_op jit(solution)/shard_map/transpose | solution.py:415
  16.6 0.6 copy.14
  17.2 0.5 reshape.37.second_ref
  17.7 1.7 %copy.15 = bf16[32,2,2,3,4,2,32]{6,5,4,3,2,1,0:T(2,128)(2,1)S(1)} copy(bf16[32,2,2,3,4,2,32]{6,0,3,5,4,2,1:T(8,128)(2,1)} %get-tuple-element.31) | data formatting | bytes 393216 | tf_op jit(solution)/shard_map/transpose | solution.py:415
  19.4 0.5 reshape.38.second_ref
  19.9 1.0 %pad_bitcast_fusion.7 = (bf16[1,3,6,3,8,32]{5,4,3,2,1,0:T(8,128)(2,1)S(1)}, bf16[1,3,6,3,8,32]{5,4,3,2,1,0:T(8,128)(2,1)S(1)}, bf16[1,3,6,3,8,32]{5,4,3,2,1,0:T(8,128)(2,1)S(1)}, bf16[1,3,6,3,8,32]{5,4,3,2,1,0:T(8,128)(2,1)S(1)}) fusion(bf16[3,3,3,8,32]{4,3,2,1,0:T(8,128)(2,1)} %bitcast.48), kind=kLoop, calls=%fused_computation.23 | loop fusion | bytes 124416 | tf_op jit(solution)/shard_map/stack | solution.py:390
  20.9 0.1 maximum_bitcast_fusion.3
  21.2 0.2 fusion.1
  21.5 0.2 copy.12
  21.7 0.2 reshape.35
  22.0 0.1 reshape.36
  22.1 24.5 %all-to-all-done = bf16[128,8,1152]{2,1,0:T(8,128)(2,1)S(1)} async-done(((bf16[128,8,1152]{2,1,0:T(8,128)(2,1)}), bf16[128,8,1152]{2,1,0:T(8,128)(2,1)S(1)}, u32[]{:S(2)}, u32[]{:S(2)}) %all-to-all-start) | async-done | bytes 2359328 | tf_op jit(solution)/shard_map/all_to_all | solution.py:438
  46.6 0.6 stack.69.averaged_ref
  47.2 0.6 collective-permute-start
  47.8 3.0 %collective-permute-start.1 = (bf16[32,2048]{1,0:T(8,128)(2,1)S(1)}, bf16[32,2048]{1,0:T(8,128)(2,1)S(1)}, u32[]{:S(2)}, u32[]{:S(2)}) collective-permute-start(bf16[32,2048]{1,0:T(8,128)(2,1)S(1)} %stack.69.averaged_ref), channel_id=1, source_target_pairs={{8,16},{24,32},{40,48},{56,64},{72,80},{88,96},{104,112},{16,8},{3... | collective-permute-start | bytes 393224 | tf_op jit(solution)/shard_map/ppermute | solution.py:421
  50.9 3.8 %band.1 = (bf16[32,2048]{1,0:T(8,128)(2,1)S(1)}, bf16[8,16,256,128]{3,2,1,0:T(8,128)(2,1)S(1)}) custom-call(bf16[32,2048]{1,0:T(8,128)(2,1)S(1)} %stack.69.averaged_ref, bf16[8,16,256,128]{3,2,1,0:T(8,128)(2,1)} %bitcast.46), custom_call_target="tpu_custom_call" | custom-call | tf_op jit(solution)/shard_map/band/pallas_call | solution.py:177
  54.7 1.0 %collective-permute-done.1.other_ref = bf16[32,2048]{1,0:T(8,128)(2,1)S(1)} collective-permute-done((bf16[32,2048]{1,0:T(8,128)(2,1)S(1)}, bf16[32,2048]{1,0:T(8,128)(2,1)S(1)}, u32[]{:S(2)}, u32[]{:S(2)}) %collective-permute-start.1) | collective-permute-done | bytes 131104 | tf_op jit(solution)/shard_map/ppermute | solution.py:421
  55.6 2.0 %border.1 = (bf16[96,2048]{1,0:T(8,128)(2,1)S(1)}, bf16[48,2048]{1,0:T(8,128)(2,1)S(1)}, bf16[48,2048]{1,0:T(8,128)(2,1)S(1)}) custom-call(s32[4]{0:T(128)S(1)} %pad_add_fusion.place_ref, bf16[32,2048]{1,0:T(8,128)(2,1)S(1)} %collective-permute-done.one_ref, bf16[32,2048]{1,0:T(8,128)(2,1)S(1)} %collective-permute-done.1.other_ref, ...), custom_call_target="tpu_custom_call" | custom-call | tf_op jit(solution)/shard_map/border/pallas_call | solution.py:217
  57.7 2.8 %collective-permute-start.2 = (bf16[96,2048]{1,0:T(8,128)(2,1)S(1)}, bf16[96,2048]{1,0:T(8,128)(2,1)S(1)}, u32[]{:S(2)}, u32[]{:S(2)}) collective-permute-start(bf16[96,2048]{1,0:T(8,128)(2,1)S(1)} %get-tuple-element.22.mid_ref), channel_id=1, source_target_pairs={{1,2},{3,4},{5,6},{2,1},{4,3},{6,5},{9,10},{11,12},{13,14},{10,9},... | collective-permute-start | bytes 1179656 | tf_op jit(solution)/shard_map/ppermute | solution.py:421
  60.4 0.6 collective-permute-start.3
  61.0 0.3 collective-permute-start.4
  61.3 0.1 copy.16.first_ref
  61.5 0.6 collective-permute-done.3.top_ref
  62.1 0.4 collective-permute-done.4.bottom_ref
  62.5 2.4 %near.1 = (f32[256,2048]{1,0:T(8,128)S(1)}, f32[128,2048]{1,0:T(8,128)S(1)}) custom-call(s32[4]{0:T(128)S(1)} %pad_add_fusion.place_ref, bf16[96,2048]{1,0:T(8,128)(2,1)S(1)} %get-tuple-element.22.mid_ref, bf16[48,2048]{1,0:T(8,128)(2,1)S(1)} %collective-permute-done.3.top_ref, bf16[48,2048]{1,0:T(8,128)(2,1)S(1)} %collective-permute-done.4.bottom_ref, ...), custom_call_target="tpu_custom_call" | custom-call | tf_op jit(solution)/shard_map/near/pallas_call | solution.py:357
  64.9 1.8 %collective-permute-done.2.far_ref = bf16[96,2048]{1,0:T(8,128)(2,1)S(1)} collective-permute-done((bf16[96,2048]{1,0:T(8,128)(2,1)S(1)}, bf16[96,2048]{1,0:T(8,128)(2,1)S(1)}, u32[]{:S(2)}, u32[]{:S(2)}) %collective-permute-start.2) | collective-permute-done | bytes 393248 | tf_op jit(solution)/shard_map/ppermute | solution.py:421
  66.8 3.0 %far.1 = bf16[32,2,2,2048]{3,2,1,0:T(2,128)(2,1)} custom-call(s32[4]{0:T(128)S(1)} %pad_add_fusion.place_ref, bf16[96,2048]{1,0:T(8,128)(2,1)S(1)} %collective-permute-done.2.far_ref, f32[256,2048]{1,0:T(8,128)S(1)} %get-tuple-element.27.partial_ref, f32[128,2048]{1,0:T(8,128)S(1)} %get-tuple-element.28.sum_ref, bf16[64,144]{1,0:T(8,128)(2,1)S(1)} %copy.17.first_ref, ...), custom_call_target="tpu_custom_call" | custom-call | tf_op jit(solution)/shard_map/far/pallas_call | solution.py:370
  (11 shorter events, 0.4 us)
Async XLA Ops:
  3.7 10.9 %copy-start = (bf16[32,32,3,3,3]{1,0,4,3,2:T(8,128)(2,1)S(1)}, bf16[32,32,3,3,3]{1,0,4,3,2:T(8,128)(2,1)}, u32[]{:S(2)}) copy-start(bf16[32,32,3,3,3]{1,0,4,3,2:T(8,128)(2,1)} %param.13) | copy-start | bytes 165892
  3.7 42.9 %all-to-all-start = ((bf16[128,8,1152]{2,1,0:T(8,128)(2,1)}), bf16[128,8,1152]{2,1,0:T(8,128)(2,1)S(1)}, u32[]{:S(2)}, u32[]{:S(2)}) async-start(bf16[128,8,1152]{2,1,0:T(8,128)(2,1)} %bitcast.45), calls=%async_computation | async-start | bytes 4718592 | tf_op jit(solution)/shard_map/all_to_all | solution.py:438
  47.2 7.4 %collective-permute-start = (bf16[32,2048]{1,0:T(8,128)(2,1)S(1)}, bf16[32,2048]{1,0:T(8,128)(2,1)S(1)}, u32[]{:S(2)}, u32[]{:S(2)}) collective-permute-start(bf16[32,2048]{1,0:T(8,128)(2,1)S(1)} %stack.69.averaged_ref), channel_id=1, source_target_pairs={{0,8},{16,24},{32,40},{48,56},{64,72},{80,88},{96,104},{112,120},{... | collective-permute-start | bytes 393224 | tf_op jit(solution)/shard_map/ppermute | solution.py:421
  47.8 7.8 %collective-permute-start.1 = (bf16[32,2048]{1,0:T(8,128)(2,1)S(1)}, bf16[32,2048]{1,0:T(8,128)(2,1)S(1)}, u32[]{:S(2)}, u32[]{:S(2)}) collective-permute-start(bf16[32,2048]{1,0:T(8,128)(2,1)S(1)} %stack.69.averaged_ref), channel_id=1, source_target_pairs={{8,16},{24,32},{40,48},{56,64},{72,80},{88,96},{104,112},{16,8},{3... | collective-permute-start | bytes 393224 | tf_op jit(solution)/shard_map/ppermute | solution.py:421
  57.7 9.1 %collective-permute-start.2 = (bf16[96,2048]{1,0:T(8,128)(2,1)S(1)}, bf16[96,2048]{1,0:T(8,128)(2,1)S(1)}, u32[]{:S(2)}, u32[]{:S(2)}) collective-permute-start(bf16[96,2048]{1,0:T(8,128)(2,1)S(1)} %get-tuple-element.22.mid_ref), channel_id=1, source_target_pairs={{1,2},{3,4},{5,6},{2,1},{4,3},{6,5},{9,10},{11,12},{13,14},{10,9},... | collective-permute-start | bytes 1179656 | tf_op jit(solution)/shard_map/ppermute | solution.py:421
  60.4 1.6 %collective-permute-start.3 = (bf16[48,2048]{1,0:T(8,128)(2,1)S(1)}, bf16[48,2048]{1,0:T(8,128)(2,1)S(1)}, u32[]{:S(2)}, u32[]{:S(2)}) collective-permute-start(bf16[48,2048]{1,0:T(8,128)(2,1)S(1)} %get-tuple-element.23), channel_id=1, source_target_pairs={{0,1},{2,3},{4,5},{6,7},{1,0},{3,2},{5,4},{7,6},{8,9},{10,11},{12,... | collective-permute-start | bytes 589832 | tf_op jit(solution)/shard_map/ppermute | solution.py:421
  61.0 1.4 %collective-permute-start.4 = (bf16[48,2048]{1,0:T(8,128)(2,1)S(1)}, bf16[48,2048]{1,0:T(8,128)(2,1)S(1)}, u32[]{:S(2)}, u32[]{:S(2)}) collective-permute-start(bf16[48,2048]{1,0:T(8,128)(2,1)S(1)} %get-tuple-element.24), channel_id=1, source_target_pairs={{0,1},{2,3},{4,5},{6,7},{1,0},{3,2},{5,4},{7,6},{8,9},{10,11},{12,... | collective-permute-start | bytes 589832 | tf_op jit(solution)/shard_map/ppermute | solution.py:421

commit v8 on v7

--- a/solution.py
+++ b/solution.py
@@ -105,7 +105,7 @@
             pltpu.VMEM((rows, width), BF),
             pltpu.SemaphoreType.DMA((3,)),
             pltpu.SemaphoreType.DMA((2,)),
-            pltpu.SemaphoreType.DMA((4,)),
+            pltpu.SemaphoreType.DMA((8,)),
         ],
         compiler_params=pltpu.CompilerParams(vmem_limit_bytes=24 << 20),
         name="pack",

time: 70.3 us -> 70.2 us (level)
  no operation moved by 1% of the time
where the time goes in v8:
time: 70.2 us; the launch traced here: 69.9 us
  waiting for transfers between devices  28.2 us (40%)
  starting transfers between devices  18.1 us (26%)
  Pallas kernels  15.5 us (22%)
  local copies, waits for them, and re-layouts  5.41 us (8%)
  other arithmetic  2.25 us (3%)
    all_to_all x1, waiting for transfers between devices, per_device(): lax.all_to_all(outgoing.reshape(devices, 2 * CAP, width), ALL, split_axis...  24.5 us
    all_to_all x1, starting transfers between devices, per_device(): lax.all_to_all(outgoing.reshape(devices, 2 * CAP, width), ALL, split_axis...  10.9 us
    ppermute x5, starting transfers between devices, swapped(): return lax.ppermute(block, axis, pairs + [(j, i) for i, j in pairs])  7.28 us
    pallas_call x1, Pallas kernels, moved_out(): pl.pallas_call(band_kernel, in_specs=[whole, pl.BlockSpec(memory_space=pl...  3.77 us
    ppermute x5, waiting for transfers between devices, swapped(): return lax.ppermute(block, axis, pairs + [(j, i) for i, j in pairs])  3.75 us
    pallas_call x1, Pallas kernels, pack(): pl.pallas_call(pack_kernel, in_specs=[kept] * 4, out_specs=kept, out_shap...  3.64 us
    pallas_call x1, Pallas kernels, convolutions(): pl.pallas_call(far_kernel, in_specs=[scalars] + [whole] * 5, out_specs=pl...  3.04 us
    pallas_call x1, Pallas kernels, convolutions(): pl.pallas_call(near_kernel, in_specs=[scalars] + [whole] * 5, out_specs=(...  2.45 us
  transfers between devices with their start and end apart: 6, of which 5 were waited for; matrix products, arithmetic and copies ran while one was open for 11% of the time, Pallas kernels for 9%

profile of v8, /device:TPU:3, one launch (start us, length us, event | category | flops | bytes accessed | tf_op | source)
XLA Modules:
  0.0 69.9 jit_solution(1342475987192478810)
XLA Ops:
  0.0 3.6 %pack.1 = bf16[1024,1152]{1,0:T(8,128)(2,1)} custom-call(s32[1,256]{1,0:T(1,128)} %bitcast.49, s32[1,256]{1,0:T(1,128)} %bitcast.50, s32[1,256]{1,0:T(1,128)} %bitcast.51, bf16[256,2048]{1,0:T(8,128)(2,1)} %traces_ref.1), custom_call_target="tpu_custom_call" | custom-call | tf_op jit(solution)/shard_map/pack/pallas_call | solution.py:97
  3.7 10.9 %all-to-all-start = ((bf16[128,8,1152]{2,1,0:T(8,128)(2,1)}), bf16[128,8,1152]{2,1,0:T(8,128)(2,1)S(1)}, u32[]{:S(2)}, u32[]{:S(2)}) async-start(bf16[128,8,1152]{2,1,0:T(8,128)(2,1)} %bitcast.45), calls=%async_computation | async-start | bytes 4718592 | tf_op jit(solution)/shard_map/all_to_all | solution.py:438
  14.5 0.3 pad_bitcast_fusion.3
  14.8 0.3 maximum_bitcast_fusion.1
  15.2 0.4 maximum_bitcast_fusion
  15.5 1.0 %select_bitcast_fusion = (bf16[32,2,2,3,4,2,32]{6,0,3,5,4,2,1:T(8,128)(2,1)}, bf16[32,2,2,3,4,2,32]{6,0,3,5,4,2,1:T(8,128)(2,1)S(1)}) fusion(pred[]{:T(512)S(6)} %eq.5, bf16[3,32,2,2,4,4,32]{6,1,0,5,4,3,2:T(8,128)(2,1)S(1)} %maximum_bitcast_fusion), kind=kLoop, calls=%fused_computation.3 | loop fusion | flops 196608 | bytes 786433 | tf_op jit(solution)/shard_map/transpose | solution.py:415
  16.5 0.6 copy.14
  17.1 0.5 reshape.37.second_ref
  17.6 1.7 %copy.15 = bf16[32,2,2,3,4,2,32]{6,5,4,3,2,1,0:T(2,128)(2,1)S(1)} copy(bf16[32,2,2,3,4,2,32]{6,0,3,5,4,2,1:T(8,128)(2,1)} %get-tuple-element.31) | data formatting | bytes 393216 | tf_op jit(solution)/shard_map/transpose | solution.py:415
  19.4 0.5 reshape.38.second_ref
  19.8 1.0 %pad_bitcast_fusion.7 = (bf16[1,3,6,3,8,32]{5,4,3,2,1,0:T(8,128)(2,1)S(1)}, bf16[1,3,6,3,8,32]{5,4,3,2,1,0:T(8,128)(2,1)S(1)}, bf16[1,3,6,3,8,32]{5,4,3,2,1,0:T(8,128)(2,1)S(1)}, bf16[1,3,6,3,8,32]{5,4,3,2,1,0:T(8,128)(2,1)S(1)}) fusion(bf16[3,3,3,8,32]{4,3,2,1,0:T(8,128)(2,1)} %bitcast.48), kind=kLoop, calls=%fused_computation.23 | loop fusion | bytes 124416 | tf_op jit(solution)/shard_map/stack | solution.py:390
  20.9 0.1 maximum_bitcast_fusion.3
  21.1 0.2 fusion.1
  21.5 0.2 copy.12
  21.7 0.2 reshape.35
  21.9 0.1 reshape.36
  22.1 24.5 %all-to-all-done = bf16[128,8,1152]{2,1,0:T(8,128)(2,1)S(1)} async-done(((bf16[128,8,1152]{2,1,0:T(8,128)(2,1)}), bf16[128,8,1152]{2,1,0:T(8,128)(2,1)S(1)}, u32[]{:S(2)}, u32[]{:S(2)}) %all-to-all-start) | async-done | bytes 2359328 | tf_op jit(solution)/shard_map/all_to_all | solution.py:438
  46.6 0.6 stack.69.averaged_ref
  47.2 0.6 collective-permute-start
  47.8 3.0 %collective-permute-start.1 = (bf16[32,2048]{1,0:T(8,128)(2,1)S(1)}, bf16[32,2048]{1,0:T(8,128)(2,1)S(1)}, u32[]{:S(2)}, u32[]{:S(2)}) collective-permute-start(bf16[32,2048]{1,0:T(8,128)(2,1)S(1)} %stack.69.averaged_ref), channel_id=1, source_target_pairs={{8,16},{24,32},{40,48},{56,64},{72,80},{88,96},{104,112},{16,8},{3... | collective-permute-start | bytes 393224 | tf_op jit(solution)/shard_map/ppermute | solution.py:421
  50.8 3.8 %band.1 = (bf16[32,2048]{1,0:T(8,128)(2,1)S(1)}, bf16[8,16,256,128]{3,2,1,0:T(8,128)(2,1)S(1)}) custom-call(bf16[32,2048]{1,0:T(8,128)(2,1)S(1)} %stack.69.averaged_ref, bf16[8,16,256,128]{3,2,1,0:T(8,128)(2,1)} %bitcast.46), custom_call_target="tpu_custom_call" | custom-call | tf_op jit(solution)/shard_map/band/pallas_call | solution.py:177
  54.6 1.0 %collective-permute-done.1.other_ref = bf16[32,2048]{1,0:T(8,128)(2,1)S(1)} collective-permute-done((bf16[32,2048]{1,0:T(8,128)(2,1)S(1)}, bf16[32,2048]{1,0:T(8,128)(2,1)S(1)}, u32[]{:S(2)}, u32[]{:S(2)}) %collective-permute-start.1) | collective-permute-done | bytes 131104 | tf_op jit(solution)/shard_map/ppermute | solution.py:421
  55.6 2.0 %border.1 = (bf16[96,2048]{1,0:T(8,128)(2,1)S(1)}, bf16[48,2048]{1,0:T(8,128)(2,1)S(1)}, bf16[48,2048]{1,0:T(8,128)(2,1)S(1)}) custom-call(s32[4]{0:T(128)S(1)} %pad_add_fusion.place_ref, bf16[32,2048]{1,0:T(8,128)(2,1)S(1)} %collective-permute-done.one_ref, bf16[32,2048]{1,0:T(8,128)(2,1)S(1)} %collective-permute-done.1.other_ref, ...), custom_call_target="tpu_custom_call" | custom-call | tf_op jit(solution)/shard_map/border/pallas_call | solution.py:217
  57.6 2.8 %collective-permute-start.2 = (bf16[96,2048]{1,0:T(8,128)(2,1)S(1)}, bf16[96,2048]{1,0:T(8,128)(2,1)S(1)}, u32[]{:S(2)}, u32[]{:S(2)}) collective-permute-start(bf16[96,2048]{1,0:T(8,128)(2,1)S(1)} %get-tuple-element.22.mid_ref), channel_id=1, source_target_pairs={{1,2},{3,4},{5,6},{2,1},{4,3},{6,5},{9,10},{11,12},{13,14},{10,9},... | collective-permute-start | bytes 1179656 | tf_op jit(solution)/shard_map/ppermute | solution.py:421
  60.4 0.6 collective-permute-start.3
  61.0 0.3 collective-permute-start.4
  61.3 0.1 copy.16.first_ref
  61.5 0.6 collective-permute-done.3.top_ref
  62.1 0.4 collective-permute-done.4.bottom_ref
  62.4 2.4 %near.1 = (f32[256,2048]{1,0:T(8,128)S(1)}, f32[128,2048]{1,0:T(8,128)S(1)}) custom-call(s32[4]{0:T(128)S(1)} %pad_add_fusion.place_ref, bf16[96,2048]{1,0:T(8,128)(2,1)S(1)} %get-tuple-element.22.mid_ref, bf16[48,2048]{1,0:T(8,128)(2,1)S(1)} %collective-permute-done.3.top_ref, bf16[48,2048]{1,0:T(8,128)(2,1)S(1)} %collective-permute-done.4.bottom_ref, ...), custom_call_target="tpu_custom_call" | custom-call | tf_op jit(solution)/shard_map/near/pallas_call | solution.py:357
  64.9 1.8 %collective-permute-done.2.far_ref = bf16[96,2048]{1,0:T(8,128)(2,1)S(1)} collective-permute-done((bf16[96,2048]{1,0:T(8,128)(2,1)S(1)}, bf16[96,2048]{1,0:T(8,128)(2,1)S(1)}, u32[]{:S(2)}, u32[]{:S(2)}) %collective-permute-start.2) | collective-permute-done | bytes 393248 | tf_op jit(solution)/shard_map/ppermute | solution.py:421
  66.7 3.0 %far.1 = bf16[32,2,2,2048]{3,2,1,0:T(2,128)(2,1)} custom-call(s32[4]{0:T(128)S(1)} %pad_add_fusion.place_ref, bf16[96,2048]{1,0:T(8,128)(2,1)S(1)} %collective-permute-done.2.far_ref, f32[256,2048]{1,0:T(8,128)S(1)} %get-tuple-element.27.partial_ref, f32[128,2048]{1,0:T(8,128)S(1)} %get-tuple-element.28.sum_ref, bf16[64,144]{1,0:T(8,128)(2,1)S(1)} %copy.17.first_ref, ...), custom_call_target="tpu_custom_call" | custom-call | tf_op jit(solution)/shard_map/far/pallas_call | solution.py:370
  (11 shorter events, 0.4 us)
Async XLA Ops:
  3.6 10.9 %copy-start = (bf16[32,32,3,3,3]{1,0,4,3,2:T(8,128)(2,1)S(1)}, bf16[32,32,3,3,3]{1,0,4,3,2:T(8,128)(2,1)}, u32[]{:S(2)}) copy-start(bf16[32,32,3,3,3]{1,0,4,3,2:T(8,128)(2,1)} %param.13) | copy-start | bytes 165892
  3.7 42.9 %all-to-all-start = ((bf16[128,8,1152]{2,1,0:T(8,128)(2,1)}), bf16[128,8,1152]{2,1,0:T(8,128)(2,1)S(1)}, u32[]{:S(2)}, u32[]{:S(2)}) async-start(bf16[128,8,1152]{2,1,0:T(8,128)(2,1)} %bitcast.45), calls=%async_computation | async-start | bytes 4718592 | tf_op jit(solution)/shard_map/all_to_all | solution.py:438
  47.2 7.4 %collective-permute-start = (bf16[32,2048]{1,0:T(8,128)(2,1)S(1)}, bf16[32,2048]{1,0:T(8,128)(2,1)S(1)}, u32[]{:S(2)}, u32[]{:S(2)}) collective-permute-start(bf16[32,2048]{1,0:T(8,128)(2,1)S(1)} %stack.69.averaged_ref), channel_id=1, source_target_pairs={{0,8},{16,24},{32,40},{48,56},{64,72},{80,88},{96,104},{112,120},{... | collective-permute-start | bytes 393224 | tf_op jit(solution)/shard_map/ppermute | solution.py:421
  47.8 7.8 %collective-permute-start.1 = (bf16[32,2048]{1,0:T(8,128)(2,1)S(1)}, bf16[32,2048]{1,0:T(8,128)(2,1)S(1)}, u32[]{:S(2)}, u32[]{:S(2)}) collective-permute-start(bf16[32,2048]{1,0:T(8,128)(2,1)S(1)} %stack.69.averaged_ref), channel_id=1, source_target_pairs={{8,16},{24,32},{40,48},{56,64},{72,80},{88,96},{104,112},{16,8},{3... | collective-permute-start | bytes 393224 | tf_op jit(solution)/shard_map/ppermute | solution.py:421
  57.6 9.1 %collective-permute-start.2 = (bf16[96,2048]{1,0:T(8,128)(2,1)S(1)}, bf16[96,2048]{1,0:T(8,128)(2,1)S(1)}, u32[]{:S(2)}, u32[]{:S(2)}) collective-permute-start(bf16[96,2048]{1,0:T(8,128)(2,1)S(1)} %get-tuple-element.22.mid_ref), channel_id=1, source_target_pairs={{1,2},{3,4},{5,6},{2,1},{4,3},{6,5},{9,10},{11,12},{13,14},{10,9},... | collective-permute-start | bytes 1179656 | tf_op jit(solution)/shard_map/ppermute | solution.py:421
  60.4 1.7 %collective-permute-start.3 = (bf16[48,2048]{1,0:T(8,128)(2,1)S(1)}, bf16[48,2048]{1,0:T(8,128)(2,1)S(1)}, u32[]{:S(2)}, u32[]{:S(2)}) collective-permute-start(bf16[48,2048]{1,0:T(8,128)(2,1)S(1)} %get-tuple-element.23), channel_id=1, source_target_pairs={{0,1},{2,3},{4,5},{6,7},{1,0},{3,2},{5,4},{7,6},{8,9},{10,11},{12,... | collective-permute-start | bytes 589832 | tf_op jit(solution)/shard_map/ppermute | solution.py:421
  61.0 1.4 %collective-permute-start.4 = (bf16[48,2048]{1,0:T(8,128)(2,1)S(1)}, bf16[48,2048]{1,0:T(8,128)(2,1)S(1)}, u32[]{:S(2)}, u32[]{:S(2)}) collective-permute-start(bf16[48,2048]{1,0:T(8,128)(2,1)S(1)} %get-tuple-element.24), channel_id=1, source_target_pairs={{0,1},{2,3},{4,5},{6,7},{1,0},{3,2},{5,4},{7,6},{8,9},{10,11},{12,... | collective-permute-start | bytes 589832 | tf_op jit(solution)/shard_map/ppermute | solution.py:421

commit v9 on v6

--- a/solution.py
+++ b/solution.py
@@ -158,7 +158,7 @@
     return total.astype(BF)
 
 
-BAND_SIZES = (2, 2, 2, 2, 2, 2, 2, 2)
+BAND_SIZES = (3, 3, 3, 3, 2, 1, 1)
 
 
 def band_kernel(averaged_ref, band_ref, out_ref, weights, padded, sem):

time: 70.2 us -> 70.2 us (level)
  no operation moved by 1% of the time
where the time goes in v9:
time: 70.2 us; the launch traced here: 69.9 us
  waiting for transfers between devices  28 us (40%)
  starting transfers between devices  18.1 us (26%)
  Pallas kernels  15.8 us (23%)
  local copies, waits for them, and re-layouts  5.41 us (8%)
  other arithmetic  2.25 us (3%)
    all_to_all x1, waiting for transfers between devices, per_device(): lax.all_to_all(outgoing.reshape(devices, 2 * CAP, width), ALL, split_axis...  24.5 us
    all_to_all x1, starting transfers between devices, per_device(): lax.all_to_all(outgoing.reshape(devices, 2 * CAP, width), ALL, split_axis...  10.8 us
    ppermute x5, starting transfers between devices, swapped(): return lax.ppermute(block, axis, pairs + [(j, i) for i, j in pairs])  7.27 us
    pallas_call x1, Pallas kernels, moved_out(): pl.pallas_call(band_kernel, in_specs=[whole, pl.BlockSpec(memory_space=pl...  3.97 us
    pallas_call x1, Pallas kernels, pack(): pl.pallas_call(pack_kernel, in_specs=[kept] * 4, out_specs=kept, out_shap...  3.69 us
    ppermute x5, waiting for transfers between devices, swapped(): return lax.ppermute(block, axis, pairs + [(j, i) for i, j in pairs])  3.56 us
    pallas_call x1, Pallas kernels, convolutions(): pl.pallas_call(far_kernel, in_specs=[scalars] + [whole] * 5, out_specs=wh...  3.1 us
    pallas_call x1, Pallas kernels, convolutions(): pl.pallas_call(near_kernel, in_specs=[scalars] + [whole] * 5, out_specs=(...  2.45 us
  transfers between devices with their start and end apart: 6, of which 5 were waited for; matrix products, arithmetic and copies ran while one was open for 11% of the time, Pallas kernels for 9%

profile of v9, /device:TPU:3, one launch (start us, length us, event | category | flops | bytes accessed | tf_op | source)
XLA Modules:
  0.0 69.9 jit_solution(5170290221352061365)
XLA Ops:
  0.0 3.7 %pack.1 = bf16[1024,1152]{1,0:T(8,128)(2,1)} custom-call(s32[1,256]{1,0:T(1,128)} %bitcast.49, s32[1,256]{1,0:T(1,128)} %bitcast.50, s32[1,256]{1,0:T(1,128)} %bitcast.51, bf16[256,2048]{1,0:T(8,128)(2,1)} %traces_ref.1), custom_call_target="tpu_custom_call" | custom-call | tf_op jit(solution)/shard_map/pack/pallas_call | solution.py:97
  3.7 10.8 %all-to-all-start = ((bf16[128,8,1152]{2,1,0:T(8,128)(2,1)}), bf16[128,8,1152]{2,1,0:T(8,128)(2,1)S(1)}, u32[]{:S(2)}, u32[]{:S(2)}) async-start(bf16[128,8,1152]{2,1,0:T(8,128)(2,1)} %bitcast.45), calls=%async_computation | async-start | bytes 4718592 | tf_op jit(solution)/shard_map/all_to_all | solution.py:424
  14.6 0.3 pad_bitcast_fusion.3
  14.9 0.3 maximum_bitcast_fusion.1
  15.2 0.4 maximum_bitcast_fusion
  15.6 1.0 %select_bitcast_fusion = (bf16[32,2,2,3,4,2,32]{6,0,3,5,4,2,1:T(8,128)(2,1)}, bf16[32,2,2,3,4,2,32]{6,0,3,5,4,2,1:T(8,128)(2,1)S(1)}) fusion(pred[]{:T(512)S(6)} %eq.5, bf16[3,32,2,2,4,4,32]{6,1,0,5,4,3,2:T(8,128)(2,1)S(1)} %maximum_bitcast_fusion), kind=kLoop, calls=%fused_computation.3 | loop fusion | flops 196608 | bytes 786433 | tf_op jit(solution)/shard_map/transpose | solution.py:401
  16.6 0.6 copy.14
  17.2 0.5 reshape.37.second_ref
  17.7 1.7 %copy.15 = bf16[32,2,2,3,4,2,32]{6,5,4,3,2,1,0:T(2,128)(2,1)S(1)} copy(bf16[32,2,2,3,4,2,32]{6,0,3,5,4,2,1:T(8,128)(2,1)} %get-tuple-element.31) | data formatting | bytes 393216 | tf_op jit(solution)/shard_map/transpose | solution.py:401
  19.4 0.5 reshape.38.second_ref
  19.9 1.0 %pad_bitcast_fusion.7 = (bf16[1,3,6,3,8,32]{5,4,3,2,1,0:T(8,128)(2,1)S(1)}, bf16[1,3,6,3,8,32]{5,4,3,2,1,0:T(8,128)(2,1)S(1)}, bf16[1,3,6,3,8,32]{5,4,3,2,1,0:T(8,128)(2,1)S(1)}, bf16[1,3,6,3,8,32]{5,4,3,2,1,0:T(8,128)(2,1)S(1)}) fusion(bf16[3,3,3,8,32]{4,3,2,1,0:T(8,128)(2,1)} %bitcast.48), kind=kLoop, calls=%fused_computation.23 | loop fusion | bytes 124416 | tf_op jit(solution)/shard_map/stack | solution.py:376
  20.9 0.1 maximum_bitcast_fusion.3
  21.2 0.2 fusion.1
  21.5 0.2 copy.12
  21.7 0.2 reshape.35
  22.0 0.1 reshape.36
  22.1 24.5 %all-to-all-done = bf16[128,8,1152]{2,1,0:T(8,128)(2,1)S(1)} async-done(((bf16[128,8,1152]{2,1,0:T(8,128)(2,1)}), bf16[128,8,1152]{2,1,0:T(8,128)(2,1)S(1)}, u32[]{:S(2)}, u32[]{:S(2)}) %all-to-all-start) | async-done | bytes 2359328 | tf_op jit(solution)/shard_map/all_to_all | solution.py:424
  46.6 0.6 stack.69.averaged_ref
  47.2 0.6 collective-permute-start
  47.8 3.0 %collective-permute-start.1 = (bf16[32,2048]{1,0:T(8,128)(2,1)S(1)}, bf16[32,2048]{1,0:T(8,128)(2,1)S(1)}, u32[]{:S(2)}, u32[]{:S(2)}) collective-permute-start(bf16[32,2048]{1,0:T(8,128)(2,1)S(1)} %stack.69.averaged_ref), channel_id=1, source_target_pairs={{8,16},{24,32},{40,48},{56,64},{72,80},{88,96},{104,112},{16,8},{3... | collective-permute-start | bytes 393224 | tf_op jit(solution)/shard_map/ppermute | solution.py:407
  50.9 4.0 %band.1 = (bf16[32,2048]{1,0:T(8,128)(2,1)S(1)}, bf16[8,16,256,128]{3,2,1,0:T(8,128)(2,1)S(1)}) custom-call(bf16[32,2048]{1,0:T(8,128)(2,1)S(1)} %stack.69.averaged_ref, bf16[8,16,256,128]{3,2,1,0:T(8,128)(2,1)} %bitcast.46), custom_call_target="tpu_custom_call" | custom-call | tf_op jit(solution)/shard_map/band/pallas_call | solution.py:177
  54.9 0.8 %collective-permute-done.1.other_ref = bf16[32,2048]{1,0:T(8,128)(2,1)S(1)} collective-permute-done((bf16[32,2048]{1,0:T(8,128)(2,1)S(1)}, bf16[32,2048]{1,0:T(8,128)(2,1)S(1)}, u32[]{:S(2)}, u32[]{:S(2)}) %collective-permute-start.1) | collective-permute-done | bytes 131104 | tf_op jit(solution)/shard_map/ppermute | solution.py:407
  55.6 2.0 %border.1 = (bf16[96,2048]{1,0:T(8,128)(2,1)S(1)}, bf16[48,2048]{1,0:T(8,128)(2,1)S(1)}, bf16[48,2048]{1,0:T(8,128)(2,1)S(1)}) custom-call(s32[4]{0:T(128)S(1)} %pad_add_fusion.place_ref, bf16[32,2048]{1,0:T(8,128)(2,1)S(1)} %collective-permute-done.one_ref, bf16[32,2048]{1,0:T(8,128)(2,1)S(1)} %collective-permute-done.1.other_ref, ...), custom_call_target="tpu_custom_call" | custom-call | tf_op jit(solution)/shard_map/border/pallas_call | solution.py:217
  57.7 2.8 %collective-permute-start.2 = (bf16[96,2048]{1,0:T(8,128)(2,1)S(1)}, bf16[96,2048]{1,0:T(8,128)(2,1)S(1)}, u32[]{:S(2)}, u32[]{:S(2)}) collective-permute-start(bf16[96,2048]{1,0:T(8,128)(2,1)S(1)} %get-tuple-element.22.mid_ref), channel_id=1, source_target_pairs={{1,2},{3,4},{5,6},{2,1},{4,3},{6,5},{9,10},{11,12},{13,14},{10,9},... | collective-permute-start | bytes 1179656 | tf_op jit(solution)/shard_map/ppermute | solution.py:407
  60.4 0.6 collective-permute-start.3
  61.0 0.3 collective-permute-start.4
  61.3 0.1 copy.16.first_ref
  61.5 0.6 collective-permute-done.3.top_ref
  62.1 0.4 collective-permute-done.4.bottom_ref
  62.5 2.4 %near.1 = (f32[256,2048]{1,0:T(8,128)S(1)}, f32[128,2048]{1,0:T(8,128)S(1)}) custom-call(s32[4]{0:T(128)S(1)} %pad_add_fusion.place_ref, bf16[96,2048]{1,0:T(8,128)(2,1)S(1)} %get-tuple-element.22.mid_ref, bf16[48,2048]{1,0:T(8,128)(2,1)S(1)} %collective-permute-done.3.top_ref, bf16[48,2048]{1,0:T(8,128)(2,1)S(1)} %collective-permute-done.4.bottom_ref, ...), custom_call_target="tpu_custom_call" | custom-call | tf_op jit(solution)/shard_map/near/pallas_call | solution.py:347
  64.9 1.8 %collective-permute-done.2.far_ref = bf16[96,2048]{1,0:T(8,128)(2,1)S(1)} collective-permute-done((bf16[96,2048]{1,0:T(8,128)(2,1)S(1)}, bf16[96,2048]{1,0:T(8,128)(2,1)S(1)}, u32[]{:S(2)}, u32[]{:S(2)}) %collective-permute-start.2) | collective-permute-done | bytes 393248 | tf_op jit(solution)/shard_map/ppermute | solution.py:407
  66.8 3.1 %far.1 = bf16[32,2,2,2048]{3,2,1,0:T(2,128)(2,1)} custom-call(s32[4]{0:T(128)S(1)} %pad_add_fusion.place_ref, bf16[96,2048]{1,0:T(8,128)(2,1)S(1)} %collective-permute-done.2.far_ref, f32[256,2048]{1,0:T(8,128)S(1)} %get-tuple-element.27.partial_ref, f32[128,2048]{1,0:T(8,128)S(1)} %get-tuple-element.28.sum_ref, bf16[64,144]{1,0:T(8,128)(2,1)S(1)} %copy.17.first_ref, ...), custom_call_target="tpu_custom_call" | custom-call | tf_op jit(solution)/shard_map/far/pallas_call | solution.py:360
  (11 shorter events, 0.4 us)
Async XLA Ops:
  3.7 10.9 %copy-start = (bf16[32,32,3,3,3]{1,0,4,3,2:T(8,128)(2,1)S(1)}, bf16[32,32,3,3,3]{1,0,4,3,2:T(8,128)(2,1)}, u32[]{:S(2)}) copy-start(bf16[32,32,3,3,3]{1,0,4,3,2:T(8,128)(2,1)} %param.13) | copy-start | bytes 165892
  3.7 42.9 %all-to-all-start = ((bf16[128,8,1152]{2,1,0:T(8,128)(2,1)}), bf16[128,8,1152]{2,1,0:T(8,128)(2,1)S(1)}, u32[]{:S(2)}, u32[]{:S(2)}) async-start(bf16[128,8,1152]{2,1,0:T(8,128)(2,1)} %bitcast.45), calls=%async_computation | async-start | bytes 4718592 | tf_op jit(solution)/shard_map/all_to_all | solution.py:424
  47.2 7.6 %collective-permute-start = (bf16[32,2048]{1,0:T(8,128)(2,1)S(1)}, bf16[32,2048]{1,0:T(8,128)(2,1)S(1)}, u32[]{:S(2)}, u32[]{:S(2)}) collective-permute-start(bf16[32,2048]{1,0:T(8,128)(2,1)S(1)} %stack.69.averaged_ref), channel_id=1, source_target_pairs={{0,8},{16,24},{32,40},{48,56},{64,72},{80,88},{96,104},{112,120},{... | collective-permute-start | bytes 393224 | tf_op jit(solution)/shard_map/ppermute | solution.py:407
  47.8 7.8 %collective-permute-start.1 = (bf16[32,2048]{1,0:T(8,128)(2,1)S(1)}, bf16[32,2048]{1,0:T(8,128)(2,1)S(1)}, u32[]{:S(2)}, u32[]{:S(2)}) collective-permute-start(bf16[32,2048]{1,0:T(8,128)(2,1)S(1)} %stack.69.averaged_ref), channel_id=1, source_target_pairs={{8,16},{24,32},{40,48},{56,64},{72,80},{88,96},{104,112},{16,8},{3... | collective-permute-start | bytes 393224 | tf_op jit(solution)/shard_map/ppermute | solution.py:407
  57.7 9.1 %collective-permute-start.2 = (bf16[96,2048]{1,0:T(8,128)(2,1)S(1)}, bf16[96,2048]{1,0:T(8,128)(2,1)S(1)}, u32[]{:S(2)}, u32[]{:S(2)}) collective-permute-start(bf16[96,2048]{1,0:T(8,128)(2,1)S(1)} %get-tuple-element.22.mid_ref), channel_id=1, source_target_pairs={{1,2},{3,4},{5,6},{2,1},{4,3},{6,5},{9,10},{11,12},{13,14},{10,9},... | collective-permute-start | bytes 1179656 | tf_op jit(solution)/shard_map/ppermute | solution.py:407
  60.4 1.6 %collective-permute-start.3 = (bf16[48,2048]{1,0:T(8,128)(2,1)S(1)}, bf16[48,2048]{1,0:T(8,128)(2,1)S(1)}, u32[]{:S(2)}, u32[]{:S(2)}) collective-permute-start(bf16[48,2048]{1,0:T(8,128)(2,1)S(1)} %get-tuple-element.23), channel_id=1, source_target_pairs={{0,1},{2,3},{4,5},{6,7},{1,0},{3,2},{5,4},{7,6},{8,9},{10,11},{12,... | collective-permute-start | bytes 589832 | tf_op jit(solution)/shard_map/ppermute | solution.py:407
  61.0 1.4 %collective-permute-start.4 = (bf16[48,2048]{1,0:T(8,128)(2,1)S(1)}, bf16[48,2048]{1,0:T(8,128)(2,1)S(1)}, u32[]{:S(2)}, u32[]{:S(2)}) collective-permute-start(bf16[48,2048]{1,0:T(8,128)(2,1)S(1)} %get-tuple-element.24), channel_id=1, source_target_pairs={{0,1},{2,3},{4,5},{6,7},{1,0},{3,2},{5,4},{7,6},{8,9},{10,11},{12,... | collective-permute-start | bytes 589832 | tf_op jit(solution)/shard_map/ppermute | solution.py:407
